TPU v7x, 32 devices: a whole 2x2x4 slice. The times are simulated.
32 devices in a mesh: dp: 8 (over y, x, core), group: 4 (over z).
Axes of the slice: x: 2, y: 2, z: 4, core: 2. Of those that a mesh axis runs over, the one named last changes fastest.
Arguments:
- tokens: bfloat16 [8, 2048, 1088], P('dp', 'group'), may hold values from -6 to 6
- segments: int32 [8, 2048], P('dp'), may hold values from 0 to 10, as said below
- out_grad: bfloat16 [8, 2048, 1088], P('dp', 'group'), as said below
- norm1_gain: bfloat16 [1088], P('group'), may hold values from 0.5 to 1.5
- norm1_bias: bfloat16 [1088], P('group'), may hold values from -1.75 to 1.75
- w_query: bfloat16 [1088, 1088], P('group'), may hold values from -0.1875 to 0.1875
- query_bias: bfloat16 [1088], P('group'), may hold values from -3 to 3
- w_key: bfloat16 [1088, 1088], P('group'), may hold values from -0.1875 to 0.1875
- w_value: bfloat16 [1088, 1088], P('group'), may hold values from -0.1875 to 0.1875
- value_bias: bfloat16 [1088], P('group'), may hold values from -3 to 3
- w_out: bfloat16 [1088, 1088], P('group'), may hold values from -0.75 to 0.75
- out_bias: bfloat16 [1088], P('group'), may hold values from -3 to 3
- norm2_gain: bfloat16 [1088], P('group'), may hold values from 0.5 to 1.5
- norm2_bias: bfloat16 [1088], P('group'), may hold values from -1.75 to 1.75
- w_fc: bfloat16 [1088, 4352], P('group'), may hold values from -0.1875 to 0.1875
- fc_bias: bfloat16 [4352], P('group'), may hold values from -3 to 3
- w_proj: bfloat16 [4352, 1088], P('group'), may hold values from -0.09375 to 0.09375
- proj_bias: bfloat16 [1088], P('group'), may hold values from -3 to 3
Outputs:
- activations: float32 [8, 2048, 1088], P('dp', 'group')
- tokens_grad: float32 [8, 2048, 1088], P('dp', 'group')
- norm1_gain_grad: float32 [1088], P('group')
- norm1_bias_grad: float32 [1088], P('group')
- w_query_grad: float32 [1088, 1088], P('group')
- query_bias_grad: float32 [1088], P('group')
- w_key_grad: float32 [1088, 1088], P('group')
- w_value_grad: float32 [1088, 1088], P('group')
- value_bias_grad: float32 [1088], P('group')
- w_out_grad: float32 [1088, 1088], P('group')
- out_bias_grad: float32 [1088], P('group')
- norm2_gain_grad: float32 [1088], P('group')
- norm2_bias_grad: float32 [1088], P('group')
- w_fc_grad: float32 [1088, 4352], P('group')
- fc_bias_grad: float32 [4352], P('group')
- w_proj_grad: float32 [4352, 1088], P('group')
- proj_bias_grad: float32 [1088], P('group')
Inputs may be any that keep to these rules, and one draw needn't show every extreme that they name: `segments`: segment numbers start at 0 in each sequence and rise by one at each document's start; every segment but the last holds 200 to 2000 tokens, the last is padding of 1 to 2000 tokens. `out_grad`: zero on every token of a sequence's last segment.
All inputs are finite; a program needn't handle non-finite values.
Results may differ from a plain program's by a relative error of at most 0.02.
Values may be sent and summed in bfloat16 or wider, within the bound.
No kernel may reach another device: no remote copies, remote signals or barrier semaphores. Data moves between devices by JAX's collectives and lax.ppermute only.
A program may use at most 256 MiB of HBM per device.

v0:
```python
from functools import partial

import jax
import jax.numpy as jnp
from jax import lax
from jax.sharding import PartitionSpec as P

HEAD = 64
KB = 512


EPSILON = 1e-05
NEG_FILL = -1e30


def layer_norm(values, gain, shift):
    center = values - jnp.mean(values, axis=-1, keepdims=True)
    spread = jnp.mean(center * center, axis=-1, keepdims=True)
    return center * lax.rsqrt(spread + EPSILON) * gain + shift


def score_block(query_heads, key_block, key_seg, key_base, query_pos, query_seg, head_scale):
    scores = (
        jnp.einsum("qhe,khe->hqk", query_heads, key_block, preferred_element_type=jnp.float32)
        * head_scale
    )
    key_pos = key_base + jnp.arange(key_block.shape[0], dtype=jnp.int32)
    keep_mask = (key_pos[None, :] <= query_pos[:, None]) & (key_seg[None, :] == query_seg[:, None])
    return jnp.where(keep_mask[None], scores, NEG_FILL)


def key_layout(keys_seq, values_seq, seg_seq, head_count):
    key_blocks = keys_seq.reshape(-1, KB, head_count, HEAD)
    value_blocks = values_seq.reshape(-1, KB, head_count, HEAD)
    seg_blocks = seg_seq.reshape(-1, KB)
    block_bases = jnp.arange(key_blocks.shape[0], dtype=jnp.int32) * KB
    return (key_blocks, value_blocks, seg_blocks, block_bases)


def attend_forward(query_seq, keys_seq, values_seq, seg_seq, row_start, head_scale):
    span_len = query_seq.shape[0]
    head_count = query_seq.shape[1] // HEAD
    query_heads = query_seq.reshape(span_len, head_count, HEAD)
    key_blocks, value_blocks, seg_blocks, block_bases = key_layout(
        keys_seq, values_seq, seg_seq, head_count
    )
    query_pos = row_start + jnp.arange(span_len, dtype=jnp.int32)
    query_seg = lax.dynamic_slice_in_dim(seg_seq, row_start, span_len)

    def max_pass(state_now, inputs):
        running_max, denom_sum = state_now
        key_block, key_seg, key_base = inputs
        scores = score_block(
            query_heads, key_block, key_seg, key_base, query_pos, query_seg, head_scale
        )
        new_max = jnp.maximum(running_max, jnp.max(scores, axis=-1))
        denom_sum = denom_sum * jnp.exp(running_max - new_max) + jnp.sum(
            jnp.exp(scores - new_max[..., None]), axis=-1
        )
        return ((new_max, denom_sum), None)

    start_max = jnp.full((head_count, span_len), NEG_FILL, jnp.float32)
    start_sum = jnp.zeros((head_count, span_len), jnp.float32)
    (running_max, denom_sum), _ = lax.scan(
        max_pass, (start_max, start_sum), (key_blocks, seg_blocks, block_bases)
    )
    log_total = running_max + jnp.log(denom_sum)

    def value_pass(accum, inputs):
        key_block, value_block, key_seg, key_base = inputs
        scores = score_block(
            query_heads, key_block, key_seg, key_base, query_pos, query_seg, head_scale
        )
        probs_low = jnp.exp(scores - log_total[..., None]).astype(jnp.bfloat16)
        return (
            accum
            + jnp.einsum(
                "hqk,khe->qhe", probs_low, value_block, preferred_element_type=jnp.float32
            ),
            None,
        )

    start_acc = jnp.zeros((span_len, head_count, HEAD), jnp.float32)
    accum, _ = lax.scan(value_pass, start_acc, (key_blocks, value_blocks, seg_blocks, block_bases))
    return (accum.reshape(span_len, -1), log_total)


def attend_backward(
    query_seq, keys_seq, values_seq, seg_seq, attn_grad, delta, log_total, row_start, head_scale
):
    span_len = query_seq.shape[0]
    feat_width = query_seq.shape[1]
    head_count = feat_width // HEAD
    query_heads = query_seq.reshape(span_len, head_count, HEAD)
    grad_heads = attn_grad.reshape(span_len, head_count, HEAD)
    key_blocks, value_blocks, seg_blocks, block_bases = key_layout(
        keys_seq, values_seq, seg_seq, head_count
    )
    query_pos = row_start + jnp.arange(span_len, dtype=jnp.int32)
    query_seg = lax.dynamic_slice_in_dim(seg_seq, row_start, span_len)

    def grad_pass(query_grad, inputs):
        key_block, value_block, key_seg, key_base = inputs
        scores = score_block(
            query_heads, key_block, key_seg, key_base, query_pos, query_seg, head_scale
        )
        probs = jnp.exp(scores - log_total[..., None])
        prob_grad = jnp.einsum(
            "qhe,khe->hqk", grad_heads, value_block, preferred_element_type=jnp.float32
        )
        score_grad = (probs * (prob_grad - delta[..., None])).astype(jnp.bfloat16)
        query_grad = (
            query_grad
            + jnp.einsum("hqk,khe->qhe", score_grad, key_block, preferred_element_type=jnp.float32)
            * head_scale
        )
        probs_low = probs.astype(jnp.bfloat16)
        value_grad = jnp.einsum(
            "hqk,qhe->khe", probs_low, grad_heads, preferred_element_type=jnp.float32
        )
        key_grad = (
            jnp.einsum("hqk,qhe->khe", score_grad, query_heads, preferred_element_type=jnp.float32)
            * head_scale
        )
        return (query_grad, (key_grad, value_grad))

    start_grad = jnp.zeros((span_len, head_count, HEAD), jnp.float32)
    query_grad, grad_pair = lax.scan(
        grad_pass, start_grad, (key_blocks, value_blocks, seg_blocks, block_bases)
    )
    return (
        query_grad.reshape(span_len, feat_width),
        grad_pair[0].reshape(-1, feat_width),
        grad_pair[1].reshape(-1, feat_width),
    )


def row_sum(values):
    return jnp.sum(values.astype(jnp.float32), axis=0)


def weight_grad(left, right):
    return jnp.einsum("ra,rb->ab", left, right, preferred_element_type=jnp.float32)


def back_through(grad_rows, weight):
    return jnp.einsum("rb,ab->ra", grad_rows, weight, preferred_element_type=jnp.float32)


def on_device(
    tokens,
    segments,
    out_grad,
    norm1_gain,
    norm1_bias,
    w_query,
    query_bias,
    w_key,
    w_value,
    value_bias,
    w_out,
    out_bias,
    norm2_gain,
    norm2_bias,
    w_fc,
    fc_bias,
    w_proj,
    proj_bias,
):
    shards = (
        norm1_gain,
        norm1_bias,
        w_query,
        query_bias,
        w_key,
        w_value,
        value_bias,
        w_out,
        out_bias,
        norm2_gain,
        norm2_bias,
        w_fc,
        fc_bias,
        w_proj,
        proj_bias,
    )
    whole = (
        lax.all_gather(shards[0], "group", axis=0, tiled=True),
        lax.all_gather(shards[1], "group", axis=0, tiled=True),
        lax.all_gather(shards[2], "group", axis=0, tiled=True),
        lax.all_gather(shards[3], "group", axis=0, tiled=True),
        lax.all_gather(shards[4], "group", axis=0, tiled=True),
        lax.all_gather(shards[5], "group", axis=0, tiled=True),
        lax.all_gather(shards[6], "group", axis=0, tiled=True),
        lax.all_gather(shards[7], "group", axis=0, tiled=True),
        lax.all_gather(shards[8], "group", axis=0, tiled=True),
        lax.all_gather(shards[9], "group", axis=0, tiled=True),
        lax.all_gather(shards[10], "group", axis=0, tiled=True),
        lax.all_gather(shards[11], "group", axis=0, tiled=True),
        lax.all_gather(shards[12], "group", axis=0, tiled=True),
        lax.all_gather(shards[13], "group", axis=0, tiled=True),
        lax.all_gather(shards[14], "group", axis=0, tiled=True),
    )
    seq_count, span_len, feat_width = tokens.shape
    head_count = feat_width // HEAD
    row_count = seq_count * span_len
    head_scale = HEAD ** (-0.5)
    row_start = lax.axis_index("group") * span_len
    inputs = tokens.astype(jnp.float32).reshape(row_count, feat_width)
    gain_one = whole[0].astype(jnp.float32)
    shift_one = whole[1].astype(jnp.float32)
    normed_one = layer_norm(inputs, gain_one, shift_one).astype(jnp.bfloat16)
    queries = (
        jnp.dot(normed_one, whole[2], preferred_element_type=jnp.float32)
        + whole[3].astype(jnp.float32)
    ).astype(jnp.bfloat16)
    keys_mine = jnp.dot(normed_one, whole[4], preferred_element_type=jnp.float32).astype(
        jnp.bfloat16
    )
    values_mine = (
        jnp.dot(normed_one, whole[5], preferred_element_type=jnp.float32)
        + whole[6].astype(jnp.float32)
    ).astype(jnp.bfloat16)
    keys_local = keys_mine.reshape(seq_count, span_len, feat_width)
    values_local = values_mine.reshape(seq_count, span_len, feat_width)
    keys_all, values_all = (
        lax.all_gather(keys_local, "group", axis=1, tiled=True),
        lax.all_gather(values_local, "group", axis=1, tiled=True),
    )
    queries_seq = queries.reshape(seq_count, span_len, feat_width)

    def forward_one(items):
        return attend_forward(items[0], items[1], items[2], items[3], row_start, head_scale)

    attended, log_total = lax.map(forward_one, (queries_seq, keys_all, values_all, segments))
    attended_low = attended.reshape(row_count, feat_width).astype(jnp.bfloat16)
    resid = (
        inputs
        + jnp.dot(attended_low, whole[7], preferred_element_type=jnp.float32)
        + whole[8].astype(jnp.float32)
    )
    gain_two = whole[9].astype(jnp.float32)
    shift_two = whole[10].astype(jnp.float32)
    normed_two = layer_norm(resid, gain_two, shift_two).astype(jnp.bfloat16)
    pre_act = jnp.dot(normed_two, whole[11], preferred_element_type=jnp.float32) + whole[12].astype(
        jnp.float32
    )
    gelu_tanh = partial(jax.nn.gelu, approximate=True)
    hidden = gelu_tanh(pre_act).astype(jnp.bfloat16)
    activations = (
        resid
        + jnp.dot(hidden, whole[13], preferred_element_type=jnp.float32)
        + whole[14].astype(jnp.float32)
    )
    weights_now = (
        lax.all_gather(shards[0], "group", axis=0, tiled=True),
        lax.all_gather(shards[1], "group", axis=0, tiled=True),
        lax.all_gather(shards[2], "group", axis=0, tiled=True),
        lax.all_gather(shards[3], "group", axis=0, tiled=True),
        lax.all_gather(shards[4], "group", axis=0, tiled=True),
        lax.all_gather(shards[5], "group", axis=0, tiled=True),
        lax.all_gather(shards[6], "group", axis=0, tiled=True),
        lax.all_gather(shards[7], "group", axis=0, tiled=True),
        lax.all_gather(shards[8], "group", axis=0, tiled=True),
        lax.all_gather(shards[9], "group", axis=0, tiled=True),
        lax.all_gather(shards[10], "group", axis=0, tiled=True),
        lax.all_gather(shards[11], "group", axis=0, tiled=True),
        lax.all_gather(shards[12], "group", axis=0, tiled=True),
        lax.all_gather(shards[13], "group", axis=0, tiled=True),
        lax.all_gather(shards[14], "group", axis=0, tiled=True),
    )
    keys_back, values_back = (
        lax.all_gather(keys_local, "group", axis=1, tiled=True),
        lax.all_gather(values_local, "group", axis=1, tiled=True),
    )
    cot_low = out_grad.reshape(row_count, feat_width)
    proj_bias_grad = row_sum(cot_low)
    w_proj_grad = weight_grad(hidden, cot_low)
    hidden_grad = back_through(cot_low, weights_now[13])
    _, gelu_back = jax.vjp(gelu_tanh, pre_act)
    pre_grad = gelu_back(hidden_grad)[0].astype(jnp.bfloat16)
    fc_bias_grad = row_sum(pre_grad)
    w_fc_grad = weight_grad(normed_two, pre_grad)
    normed_two_grad = back_through(pre_grad, weights_now[11])
    _, norm_two_back = jax.vjp(layer_norm, resid, gain_two, shift_two)
    resid_part, norm2_gain_grad, norm2_bias_grad = norm_two_back(normed_two_grad)
    resid_grad = cot_low.astype(jnp.float32) + resid_part
    resid_low = resid_grad.astype(jnp.bfloat16)
    out_bias_grad = row_sum(resid_low)
    w_out_grad = weight_grad(attended_low, resid_low)
    attended_grad = back_through(resid_low, weights_now[7]).astype(jnp.bfloat16)
    attended_grad_seq = attended_grad.reshape(seq_count, span_len, feat_width)
    delta = jnp.einsum(
        "sqhe,sqhe->shq",
        attended_grad_seq.reshape(seq_count, span_len, head_count, HEAD).astype(jnp.float32),
        attended.reshape(seq_count, span_len, head_count, HEAD),
    )

    def backward_one(items):
        return attend_backward(
            items[0],
            items[1],
            items[2],
            items[3],
            items[4],
            items[5],
            items[6],
            row_start,
            head_scale,
        )

    query_grad, key_terms, value_terms = lax.map(
        backward_one,
        (queries_seq, keys_back, values_back, segments, attended_grad_seq, delta, log_total),
    )
    key_grad, value_grad = (
        lax.psum_scatter(
            key_terms.astype(jnp.bfloat16), "group", scatter_dimension=1, tiled=True
        ).astype(jnp.float32),
        lax.psum_scatter(
            value_terms.astype(jnp.bfloat16), "group", scatter_dimension=1, tiled=True
        ).astype(jnp.float32),
    )
    query_low = query_grad.reshape(row_count, feat_width).astype(jnp.bfloat16)
    key_low = key_grad.reshape(row_count, feat_width).astype(jnp.bfloat16)
    value_low = value_grad.reshape(row_count, feat_width).astype(jnp.bfloat16)
    query_bias_grad = row_sum(query_low)
    value_bias_grad = row_sum(value_low)
    w_query_grad = weight_grad(normed_one, query_low)
    w_key_grad = weight_grad(normed_one, key_low)
    w_value_grad = weight_grad(normed_one, value_low)
    normed_one_grad = (
        back_through(query_low, weights_now[2])
        + back_through(key_low, weights_now[4])
        + back_through(value_low, weights_now[5])
    )
    _, norm_one_back = jax.vjp(layer_norm, inputs, gain_one, shift_one)
    input_part, norm1_gain_grad, norm1_bias_grad = norm_one_back(normed_one_grad)
    tokens_grad = resid_grad + input_part
    full_grads = (
        norm1_gain_grad,
        norm1_bias_grad,
        w_query_grad,
        query_bias_grad,
        w_key_grad,
        w_value_grad,
        value_bias_grad,
        w_out_grad,
        out_bias_grad,
        norm2_gain_grad,
        norm2_bias_grad,
        w_fc_grad,
        fc_bias_grad,
        w_proj_grad,
        proj_bias_grad,
    )
    owned = (
        lax.psum_scatter(
            full_grads[0].astype(jnp.bfloat16), "group", scatter_dimension=0, tiled=True
        ).astype(jnp.float32),
        lax.psum_scatter(
            full_grads[1].astype(jnp.bfloat16), "group", scatter_dimension=0, tiled=True
        ).astype(jnp.float32),
        lax.psum_scatter(
            full_grads[2].astype(jnp.bfloat16), "group", scatter_dimension=0, tiled=True
        ).astype(jnp.float32),
        lax.psum_scatter(
            full_grads[3].astype(jnp.bfloat16), "group", scatter_dimension=0, tiled=True
        ).astype(jnp.float32),
        lax.psum_scatter(
            full_grads[4].astype(jnp.bfloat16), "group", scatter_dimension=0, tiled=True
        ).astype(jnp.float32),
        lax.psum_scatter(
            full_grads[5].astype(jnp.bfloat16), "group", scatter_dimension=0, tiled=True
        ).astype(jnp.float32),
        lax.psum_scatter(
            full_grads[6].astype(jnp.bfloat16), "group", scatter_dimension=0, tiled=True
        ).astype(jnp.float32),
        lax.psum_scatter(
            full_grads[7].astype(jnp.bfloat16), "group", scatter_dimension=0, tiled=True
        ).astype(jnp.float32),
        lax.psum_scatter(
            full_grads[8].astype(jnp.bfloat16), "group", scatter_dimension=0, tiled=True
        ).astype(jnp.float32),
        lax.psum_scatter(
            full_grads[9].astype(jnp.bfloat16), "group", scatter_dimension=0, tiled=True
        ).astype(jnp.float32),
        lax.psum_scatter(
            full_grads[10].astype(jnp.bfloat16), "group", scatter_dimension=0, tiled=True
        ).astype(jnp.float32),
        lax.psum_scatter(
            full_grads[11].astype(jnp.bfloat16), "group", scatter_dimension=0, tiled=True
        ).astype(jnp.float32),
        lax.psum_scatter(
            full_grads[12].astype(jnp.bfloat16), "group", scatter_dimension=0, tiled=True
        ).astype(jnp.float32),
        lax.psum_scatter(
            full_grads[13].astype(jnp.bfloat16), "group", scatter_dimension=0, tiled=True
        ).astype(jnp.float32),
        lax.psum_scatter(
            full_grads[14].astype(jnp.bfloat16), "group", scatter_dimension=0, tiled=True
        ).astype(jnp.float32),
    )
    matrix_share = (
        lax.psum_scatter(
            owned[2].astype(jnp.bfloat16), "dp", scatter_dimension=1, tiled=True
        ).astype(jnp.float32),
        lax.psum_scatter(
            owned[4].astype(jnp.bfloat16), "dp", scatter_dimension=1, tiled=True
        ).astype(jnp.float32),
        lax.psum_scatter(
            owned[5].astype(jnp.bfloat16), "dp", scatter_dimension=1, tiled=True
        ).astype(jnp.float32),
        lax.psum_scatter(
            owned[7].astype(jnp.bfloat16), "dp", scatter_dimension=1, tiled=True
        ).astype(jnp.float32),
        lax.psum_scatter(
            owned[11].astype(jnp.bfloat16), "dp", scatter_dimension=1, tiled=True
        ).astype(jnp.float32),
        lax.psum_scatter(
            owned[13].astype(jnp.bfloat16), "dp", scatter_dimension=1, tiled=True
        ).astype(jnp.float32),
    )
    matrix_sums = (
        lax.all_gather(matrix_share[0].astype(jnp.bfloat16), "dp", axis=1, tiled=True).astype(
            jnp.float32
        ),
        lax.all_gather(matrix_share[1].astype(jnp.bfloat16), "dp", axis=1, tiled=True).astype(
            jnp.float32
        ),
        lax.all_gather(matrix_share[2].astype(jnp.bfloat16), "dp", axis=1, tiled=True).astype(
            jnp.float32
        ),
        lax.all_gather(matrix_share[3].astype(jnp.bfloat16), "dp", axis=1, tiled=True).astype(
            jnp.float32
        ),
        lax.all_gather(matrix_share[4].astype(jnp.bfloat16), "dp", axis=1, tiled=True).astype(
            jnp.float32
        ),
        lax.all_gather(matrix_share[5].astype(jnp.bfloat16), "dp", axis=1, tiled=True).astype(
            jnp.float32
        ),
    )
    vector_sums = lax.psum(
        (
            owned[0],
            owned[1],
            owned[3],
            owned[6],
            owned[8],
            owned[9],
            owned[10],
            owned[12],
            owned[14],
        ),
        "dp",
    )
    summed = (
        vector_sums[0],
        vector_sums[1],
        matrix_sums[0],
        vector_sums[2],
        matrix_sums[1],
        matrix_sums[2],
        vector_sums[3],
        matrix_sums[3],
        vector_sums[4],
        vector_sums[5],
        vector_sums[6],
        matrix_sums[4],
        vector_sums[7],
        matrix_sums[5],
        vector_sums[8],
    )
    return (
        activations.reshape(seq_count, span_len, feat_width),
        tokens_grad.reshape(seq_count, span_len, feat_width),
    ) + tuple(summed)


def solution(mesh):
    return jax.shard_map(
        on_device,
        mesh=mesh,
        in_specs=(
            P("dp", "group", None),
            P("dp", None),
            P("dp", "group", None),
            P("group"),
            P("group"),
            P("group", None),
            P("group"),
            P("group", None),
            P("group", None),
            P("group"),
            P("group", None),
            P("group"),
            P("group"),
            P("group"),
            P("group", None),
            P("group"),
            P("group", None),
            P("group"),
        ),
        out_specs=(
            P("dp", "group", None),
            P("dp", "group", None),
            P("group"),
            P("group"),
            P("group", None),
            P("group"),
            P("group", None),
            P("group", None),
            P("group"),
            P("group", None),
            P("group"),
            P("group"),
            P("group"),
            P("group", None),
            P("group"),
            P("group", None),
            P("group"),
        ),
        check_vma=False,
    )
```

profile of v0, /device:TPU:0, one launch (start us, length us, event | category | flops | bytes accessed | tf_op | source)
XLA Modules:
  0.0 1936.4 jit_solution(2903784194522113271)
XLA Ops:
  19.1 22.8 %all-reduce.26 = (bf16[1088]{0:T(1024)(128)(2,1)S(1)}, bf16[1088]{0:T(1024)(128)(2,1)S(1)}, bf16[1088]{0:T(1024)(128)(2,1)S(1)}, bf16[1088]{0:T(1024)(128)(2,1)S...) all-reduce(bf16[1088]{0:T(1024)(128)(2,1)S(1)} %dynamic-update-slic, ...), channel_id=1, replica_groups=mesh['dp'=8,'group'=4] {'group'}, use_global_device_ids=true, to_apply=%add.1 | all-reduce | flops 11968 | bytes 47872
  42.5 24.2 %all-gather.14.cloned.1.call-done = bf16[1088,1088]{1,0:T(8,128)(2,1)} async-done(((bf16[272,1088]{1,0:T(8,128)(2,1)}), bf16[1088,1088]{1,0:T(8,128)(2,1)}) %all-gather.14.cloned.1.call-update) | async-done | bytes 2367504 | tf_op jit(solution)/shard_map/all_gather | solution.py:193
  71.4 48.6 %all-gather.16.cloned.1.call-done = bf16[1088,1088]{1,0:T(8,128)(2,1)} async-done(((bf16[272,1088]{1,0:T(8,128)(2,1)}), bf16[1088,1088]{1,0:T(8,128)(2,1)}) %all-gather.16.cloned.1.call-update) | async-done | bytes 2367504 | tf_op jit(solution)/shard_map/all_gather | solution.py:192
  128.2 45.2 %all-gather.18.cloned.1.call-done = bf16[1088,1088]{1,0:T(8,128)(2,1)} async-done(((bf16[272,1088]{1,0:T(8,128)(2,1)}), bf16[1088,1088]{1,0:T(8,128)(2,1)}) %all-gather.18.cloned.1.call-update) | async-done | bytes 2367504 | tf_op jit(solution)/shard_map/all_gather | solution.py:190
  177.0 82.2 %all-gather.28.cloned.1.call-done = bf16[2048,1088]{0,1:T(8,128)(2,1)} async-done(((bf16[512,1088]{0,1:T(8,128)(2,1)}), bf16[2048,1088]{0,1:T(8,128)(2,1)}) %all-gather.28.cloned.1.call-update) | async-done | bytes 4456464 | tf_op jit(solution)/shard_map/all_gather | solution.py:228
  275.3 69.5 %all-gather.30.cloned.1.call-done = bf16[2048,1088]{0,1:T(8,128)(2,1)} async-done(((bf16[512,1088]{0,1:T(8,128)(2,1)}), bf16[2048,1088]{0,1:T(8,128)(2,1)}) %all-gather.30.cloned.1.call-update) | async-done | bytes 4456464 | tf_op jit(solution)/shard_map/all_gather | solution.py:227
  360.5 82.6 %while.62 = (s32[]{:T(128)}, f32[17,512]{1,0:T(8,128)S(1)}, f32[17,512]{1,0:T(8,128)S(1)}, s32[4]{0:T(128)S(1)}, s32[4,512]{1,0:T(4,128)S(1)}, /*index=5*/s32[51...) while((s32[]{:T(128)}, f32[17,512]{1,0:T(8,128)S(1)}, ...), condition=%wide.region_5.6_spmd.clone, body=%wide.region_2.5_spmd.clone.sunk | while | flops 602451456 | bytes 39135384 | solution.py:64
  443.2 43.6 %while.63 = (s32[]{:T(128)}, f32[512,17,64]{0,2,1:T(8,128)}, bf16[4,512,17,64]{1,3,2,0:T(8,128)(2,1)}, s32[4]{0:T(128)S(1)}, s32[4,512]{1,0:T(4,128)S(1)}, /*ind...) while((s32[]{:T(128)}, f32[512,17,64]{0,2,1:T(8,128)}, ...), condition=%wide.region_7.8_spmd.clone, body=%wide.region_6.7_spmd.clone.sunk | while | flops 1160578048 | bytes 8375966 | solution.py:84
  494.1 71.3 %all-gather.22.cloned.1.call-done = bf16[1088,4352]{1,0:T(8,128)(2,1)} async-done(((bf16[272,4352]{1,0:T(8,128)(2,1)}), bf16[1088,4352]{1,0:T(8,128)(2,1)}) %all-gather.22.cloned.1.call-update) | async-done | bytes 9469968 | tf_op jit(solution)/shard_map/all_gather | solution.py:199
  565.4 12.2 fusion.90
  577.6 164.0 %all-gather.24.cloned.1.call-done = bf16[4352,1088]{1,0:T(8,128)(2,1)} async-done(((bf16[1088,1088]{1,0:T(8,128)(2,1)}), bf16[4352,1088]{1,0:T(8,128)(2,1)}) %all-gather.24.cloned.1.call-update) | async-done | bytes 9469968 | tf_op jit(solution)/shard_map/all_gather | solution.py:201
  741.6 16.2 fusion.104
  773.7 162.7 %while.64 = (s32[]{:T(128)}, f32[512,17,64]{0,2,1:T(8,128)S(1)}, bf16[4,512,17,64]{1,3,2,0:T(8,128)(2,1)}, bf16[4,512,17,64]{1,3,2,0:T(8,128)(2,1)}, bf16[4,512,...) while((s32[]{:T(128)}, f32[512,17,64]{0,2,1:T(8,128)S(1)}, ...), condition=%wide.region_13.14_spmd.clone, body=%wide.region_12.13_spmd.clone.sunk | while | flops 2899706880 | bytes 97835208 | solution.py:128
  786.0 11.7 bitcast_dynamic-update-slice_fusion.5
  826.5 11.7 bitcast_dynamic-update-slice_fusion.5
  867.0 11.8 bitcast_dynamic-update-slice_fusion.5
  907.6 11.7 bitcast_dynamic-update-slice_fusion.5
  981.9 51.8 %reduce-scatter.19.cloned.1.call-done = bf16[1,512,1088]{1,2,0:T(8,128)(2,1)} async-done(((bf16[1,2048,1088]{1,2,0:T(8,128)(2,1)}), bf16[1,512,1088]{1,2,0:T(8,128)(2,1)}) %reduce-scatter.19.cloned.1.call-update) | async-done | bytes 1114128 | tf_op jit(solution)/shard_map/reduce_scatter | solution.py:320
  1038.2 79.2 %reduce-scatter.17.cloned.1.call-done = bf16[1,512,1088]{1,2,0:T(8,128)(2,1)} async-done(((bf16[1,2048,1088]{1,2,0:T(8,128)(2,1)}), bf16[1,512,1088]{1,2,0:T(8,128)(2,1)}) %reduce-scatter.17.cloned.1.call-update) | async-done | bytes 1114128 | tf_op jit(solution)/shard_map/reduce_scatter | solution.py:317
  1123.1 12.9 convolution_convert_fusion
  1147.9 23.5 %reduce-scatter.21.cloned.1.call-done = bf16[272,1088]{1,0:T(8,128)(2,1)} async-done(((bf16[1088,1088]{1,0:T(8,128)(2,1)}), bf16[272,1088]{1,0:T(8,128)(2,1)}) %reduce-scatter.21.cloned.1.call-update) | async-done | bytes 591888 | tf_op jit(solution)/shard_map/reduce_scatter | solution.py:364
  1171.4 52.4 %reduce-scatter.27.cloned.1.call-done = bf16[272,1088]{1,0:T(8,128)(2,1)} async-done(((bf16[1088,1088]{1,0:T(8,128)(2,1)}), bf16[272,1088]{1,0:T(8,128)(2,1)}) %reduce-scatter.27.cloned.1.call-update) | async-done | bytes 591888 | tf_op jit(solution)/shard_map/reduce_scatter | solution.py:379
  1223.8 52.4 %reduce-scatter.25.cloned.1.call-done = bf16[272,1088]{1,0:T(8,128)(2,1)} async-done(((bf16[1088,1088]{1,0:T(8,128)(2,1)}), bf16[272,1088]{1,0:T(8,128)(2,1)}) %reduce-scatter.25.cloned.1.call-update) | async-done | bytes 591888 | tf_op jit(solution)/shard_map/reduce_scatter | solution.py:373
  1276.2 52.4 %reduce-scatter.23.cloned.1.call-done = bf16[272,1088]{1,0:T(8,128)(2,1)} async-done(((bf16[1088,1088]{1,0:T(8,128)(2,1)}), bf16[272,1088]{1,0:T(8,128)(2,1)}) %reduce-scatter.23.cloned.1.call-update) | async-done | bytes 591888 | tf_op jit(solution)/shard_map/reduce_scatter | solution.py:370
  1328.6 172.5 %reduce-scatter.31.cloned.1.call-done = bf16[1088,1088]{1,0:T(8,128)(2,1)} async-done(((bf16[4352,1088]{1,0:T(8,128)(2,1)}), bf16[1088,1088]{1,0:T(8,128)(2,1)}) %reduce-scatter.31.cloned.1.call-update) | async-done | bytes 2367504 | tf_op jit(solution)/shard_map/reduce_scatter | solution.py:397
  1501.1 165.4 %reduce-scatter.29.cloned.1.call-done = bf16[272,4352]{1,0:T(8,128)(2,1)} async-done(((bf16[1088,4352]{1,0:T(8,128)(2,1)}), bf16[272,4352]{1,0:T(8,128)(2,1)}) %reduce-scatter.29.cloned.1.call-update) | async-done | bytes 2367504 | tf_op jit(solution)/shard_map/reduce_scatter | solution.py:391
  1672.9 89.5 %all-reduce.29.cloned.1.call-done = (bf16[272,1088]{1,0:T(8,128)(2,1)}, bf16[272,1088]{1,0:T(8,128)(2,1)}, bf16[272,1088]{1,0:T(8,128)(2,1)}, bf16[272,1088]{1,0:T(8,128)(2,1)}, bf16[1088,1088]{1,0:T(8,128)(2,1)}) async-done(((bf16[272,1088]{1,0:T(8,128)(2,1)}, bf16[272,1088]{1,0:T(8,128)(2,1)}, bf16[272,1088]{1,0:T(8,128)(2,1)}, bf16[272,1088]{1,0:T(8,128)(2,1)}, bf16[1088,1088]{1,0:T(8,128)(2,1)}), ...) | async-done | bytes 4734992
  1783.5 19.4 all-reduce.25
  1803.0 11.0 reduce-scatter.33.cloned.1.call-done
  1816.2 24.4 %all-reduce.23 = (f32[272]{0:T(512)}, f32[272]{0:T(512)}, f32[272]{0:T(512)}, f32[272]{0:T(512)}, f32[272]{0:T(512)}, /*index=5*/f32[272]{0:T(512)}, f32[272]{0:T(512)}, f32[1088]{0:T(1024)}, f32[272]{0:T(512)}) all-reduce(f32[272]{0:T(512)S(1)} %get-tuple-element.624, ...), channel_id=1, replica_groups=mesh['dp'=8,'group'=4] {'dp'}, use_global_device_ids=true, to_apply=%region_20.21 | all-reduce | flops 3264 | bytes 26112 | tf_op jit(solution)/shard_map/psum | solution.py:444
  1845.5 13.4 fusion.56
  1863.7 12.9 all_gather.97
  (342 shorter events, 480.1 us)
Async XLA Ops:
  7.2 59.5 %all-gather.14.cloned.1.call-start = ((), (), s32[]{:S(2)}) async-start(), calls=%async_computation.9 | async-start | bytes 3133440 | tf_op jit(solution)/shard_map/all_gather | solution.py:193
  7.9 112.1 %all-gather.16.cloned.1.call-start = ((), (), s32[]{:S(2)}) async-start(), calls=%async_computation.10 | async-start | bytes 3133440 | tf_op jit(solution)/shard_map/all_gather | solution.py:192
  8.7 164.7 %all-gather.18.cloned.1.call-start = ((), (), s32[]{:S(2)}) async-start(), calls=%async_computation.11 | async-start | bytes 3133440 | tf_op jit(solution)/shard_map/all_gather | solution.py:190
  9.4 249.9 %all-gather.28.cloned.1.call-start = ((), (), s32[]{:S(2)}) async-start(), calls=%async_computation.24 | async-start | bytes 5570560 | tf_op jit(solution)/shard_map/all_gather | solution.py:228
  41.9 131.5 %copy-start.42 = (f32[1088]{0:T(1024)}, f32[1088]{0:T(1024)S(1)}, u32[]{:S(2)}) copy-start(f32[1088]{0:T(1024)S(1)} %convert_element_type.242) | copy-start | bytes 13060
  41.9 131.5 %copy-start.25 = (f32[1088]{0:T(1024)}, f32[1088]{0:T(1024)S(1)}, u32[]{:S(2)}) copy-start(f32[1088]{0:T(1024)S(1)} %convert_element_type.241) | copy-start | bytes 13060
  42.2 131.2 %copy-start.29 = (f32[512]{0:T(512)}, f32[512]{0:T(512)S(1)}, u32[]{:S(2)}) copy-start(f32[512]{0:T(512)S(1)} %broadcast_multiply_fusion.1) | copy-start | bytes 6148
  42.5 130.8 %copy-start.33 = (f32[512]{0:T(512)}, f32[512]{0:T(512)S(1)}, u32[]{:S(2)}) copy-start(f32[512]{0:T(512)S(1)} %fusion.88) | copy-start | bytes 6148
  71.4 273.5 %all-gather.30.cloned.1.call-start = ((), (), s32[]{:S(2)}) async-start(), calls=%async_computation.25 | async-start | bytes 5570560 | tf_op jit(solution)/shard_map/all_gather | solution.py:227
  124.7 364.9 %all-gather.20.cloned.1.call-start = ((), (), s32[]{:S(2)}) async-start(), calls=%async_computation.12 | async-start | bytes 3133440 | tf_op jit(solution)/shard_map/all_gather | solution.py:195
  125.3 440.1 %all-gather.22.cloned.1.call-start = ((), (), s32[]{:S(2)}) async-start(), calls=%async_computation.13 | async-start | bytes 11837440 | tf_op jit(solution)/shard_map/all_gather | solution.py:199
  126.0 615.6 %all-gather.24.cloned.1.call-start = ((), (), s32[]{:S(2)}) async-start(), calls=%async_computation.14 | async-start | bytes 12533760 | tf_op jit(solution)/shard_map/all_gather | solution.py:201
  126.8 906.9 %reduce-scatter.19.cloned.1.call-start = ((), (), s32[]{:S(2)}) async-start(), calls=%async_computation.16 | async-start | bytes 5570560 | tf_op jit(solution)/shard_map/reduce_scatter | solution.py:320
  128.1 638.8 %copy-start.19 = (f32[1088]{0:T(1024)}, f32[1088]{0:T(1024)S(1)}, u32[]{:S(2)}) copy-start(f32[1088]{0:T(1024)S(1)} %convert_element_type.252) | copy-start | bytes 13060
  128.1 437.2 %copy-start.21 = (f32[1088]{0:T(1024)}, f32[1088]{0:T(1024)S(1)}, u32[]{:S(2)}) copy-start(f32[1088]{0:T(1024)S(1)} %convert_element_type.253) | copy-start | bytes 13060
  128.2 613.4 %copy-start.31 = (f32[4352]{0:T(1024)}, f32[4352]{0:T(1024)S(1)}, u32[]{:S(2)}) copy-start(f32[4352]{0:T(1024)S(1)} %convert_element_type.255) | copy-start | bytes 52228
  493.7 273.2 %copy-start.1 = (f32[512,1088]{0,1:T(8,128)}, f32[512,1088]{0,1:T(8,128)S(1)}, u32[]{:S(2)}) copy-start(f32[512,1088]{0,1:T(8,128)S(1)} %get-tuple-element.612) | copy-start | bytes 6684676
  493.7 273.2 %copy-start.23 = (f32[512]{0:T(512)}, f32[512]{0:T(512)S(1)}, u32[]{:S(2)}) copy-start(f32[512]{0:T(512)S(1)} %broadcast_multiply_fusion) | copy-start | bytes 6148
  494.1 272.9 %copy-start.27 = (f32[512]{0:T(512)}, f32[512]{0:T(512)S(1)}, u32[]{:S(2)}) copy-start(f32[512]{0:T(512)S(1)} %fusion.89) | copy-start | bytes 6148
  954.3 163.1 %reduce-scatter.17.cloned.1.call-start = ((), (), s32[]{:S(2)}) async-start(), calls=%async_computation.15 | async-start | bytes 5570560 | tf_op jit(solution)/shard_map/reduce_scatter | solution.py:317
  972.4 199.0 %reduce-scatter.21.cloned.1.call-start = ((), (), s32[]{:S(2)}) async-start(), calls=%async_computation.17 | async-start | bytes 3133440 | tf_op jit(solution)/shard_map/reduce_scatter | solution.py:364
  977.2 246.6 %reduce-scatter.27.cloned.1.call-start = ((), (), s32[]{:S(2)}) async-start(), calls=%async_computation.20 | async-start | bytes 3133440 | tf_op jit(solution)/shard_map/reduce_scatter | solution.py:379
  981.8 294.4 %reduce-scatter.25.cloned.1.call-start = ((), (), s32[]{:S(2)}) async-start(), calls=%async_computation.19 | async-start | bytes 3133440 | tf_op jit(solution)/shard_map/reduce_scatter | solution.py:373
  1038.2 290.4 %reduce-scatter.23.cloned.1.call-start = ((), (), s32[]{:S(2)}) async-start(), calls=%async_computation.18 | async-start | bytes 3133440 | tf_op jit(solution)/shard_map/reduce_scatter | solution.py:370
  1121.9 379.1 %reduce-scatter.31.cloned.1.call-start = ((), (), s32[]{:S(2)}) async-start(), calls=%async_computation.22 | async-start | bytes 12533760 | tf_op jit(solution)/shard_map/reduce_scatter | solution.py:397
  1136.1 530.4 %reduce-scatter.29.cloned.1.call-start = ((), (), s32[]{:S(2)}) async-start(), calls=%async_computation.21 | async-start | bytes 11837440 | tf_op jit(solution)/shard_map/reduce_scatter | solution.py:391
  1147.8 614.6 %all-reduce.29.cloned.1.call-start = ((), (), s32[]{:S(2)}) async-start(), calls=%async_computation.28 | async-start | bytes 10027008
  1501.1 312.9 %reduce-scatter.33.cloned.1.call-start = ((), (), s32[]{:S(2)}) async-start(), calls=%async_computation.27 | async-start | bytes 3760128
  1671.1 97.2 %copy-start.46 = (bf16[272]{0:T(512)(128)(2,1)S(1)}, bf16[272]{0:T(512)(128)(2,1)}, u32[]{:S(2)}) copy-start(bf16[272]{0:T(512)(128)(2,1)} %param.41) | copy-start | bytes 1636
  1671.1 241.1 %all-gather.26.cloned.1.call-start = ((), (), s32[]{:S(2)}) async-start(), calls=%async_computation.23 | async-start | bytes 2820096 | tf_op jit(solution)/shard_map/all_gather | solution.py:440
  1766.7 150.7 %all-gather.32.cloned.1.call-start = ((), (), s32[]{:S(2)}) async-start(), calls=%async_computation.26 | async-start | bytes 3133440 | tf_op jit(solution)/shard_map/all_gather | solution.py:437
  1782.4 58.2 %copy-start.36 = (f32[512]{0:T(512)S(1)}, f32[512]{0:T(512)}, u32[]{:S(2)}) copy-start(f32[512]{0:T(512)} %copy-done.35) | copy-start | bytes 6148
  (38 other events, 150.8 us)
Sparse Core Ops, SparseCore 0:
  9.6 57.0 all-gather.13
  68.3 51.7 all-gather.15
  121.6 51.6 all-gather.17
  175.4 83.8 all-gather.27
  261.3 83.5 all-gather.29
  346.3 51.3 all-gather.19
  399.2 166.0 all-gather.21
  566.9 174.6 all-gather.23
  954.5 79.1 reduce-scatter.18
  1035.8 81.5 reduce-scatter.16
  1120.3 51.0 reduce-scatter.20
  1173.7 50.0 reduce-scatter.26
  1226.1 50.0 reduce-scatter.24
  1278.5 50.0 reduce-scatter.22
  1330.8 170.2 reduce-scatter.30
  1503.3 163.1 reduce-scatter.28
  1670.3 92.0 all-reduce.28
  1766.7 47.2 reduce-scatter.32
  1816.4 29.6 all-gather.25
  1848.5 32.3 all-gather.31
where the time goes:
time: 1950 us; the launch traced here: 1940 us
  waiting for transfers between devices  1260 us (65%)
  matrix products  347 us (18%)
  local copies, waits for them, and re-layouts  132 us (7%)
  blocking collectives  110 us (6%)
  other arithmetic  66.7 us (3%)
    reduce_scatter x1, waiting for transfers between devices, on_device(): lax.psum_scatter(full_grads[13].astype(jnp.bfloat16), 'group', scatter_di...  172 us
    reduce_scatter x1, waiting for transfers between devices, on_device(): lax.psum_scatter(full_grads[11].astype(jnp.bfloat16), 'group', scatter_di...  165 us
    all_gather x1, waiting for transfers between devices, on_device(): lax.all_gather(shards[13], 'group', axis=0, tiled=True)  164 us
    unnamed x22, waiting for transfers between devices  105 us
    all_gather x1, waiting for transfers between devices, on_device(): lax.all_gather(values_local, 'group', axis=1, tiled=True)  82.2 us
    reduce_scatter x1, waiting for transfers between devices, on_device(): lax.psum_scatter(key_terms.astype(jnp.bfloat16), 'group', scatter_dimensi...  79.2 us
    dot_general x8, matrix products, score_block(): jnp.einsum('qhe,khe->hqk', query_heads, key_block, preferred_element_type...  76.9 us
    all_gather x1, waiting for transfers between devices, on_device(): lax.all_gather(shards[11], 'group', axis=0, tiled=True)  71.3 us
  transfers between devices with their start and end apart: 20, of which 17 were waited for; matrix products, arithmetic and copies ran while one was open for 16% of the time, Pallas kernels for 0%

commit v1 on v0

v1 whole, which is shorter than its diff:
```python
from functools import partial

import jax
import jax.numpy as jnp
from jax import lax
from jax.experimental import pallas as pl
from jax.experimental.pallas import tpu as pltpu
from jax.sharding import PartitionSpec as P

HEAD = 64
LANES = 128
EPSILON = 1e-05
NEG_FILL = -1e30
F32 = jnp.float32
BF16 = jnp.bfloat16
SCALE = HEAD ** (-0.5)


def lane_mask(shape, head):
    lane = lax.broadcasted_iota(jnp.int32, shape, 1)
    return (lane < HEAD) if head == 0 else (lane >= HEAD)


def keep_of(tile_base, tile_len, low_row, own_base):
    span_len = low_row.shape[1]
    key_pos = tile_base + lax.broadcasted_iota(jnp.int32, (tile_len, span_len), 0)
    query_pos = own_base + lax.broadcasted_iota(jnp.int32, (tile_len, span_len), 1)
    return (key_pos >= low_row) & (key_pos <= query_pos)


def tile_loops(bounds_ref, tile, own_tile, tile_count):
    low_tile = bounds_ref[0]
    mid_tile = bounds_ref[1]
    lax.fori_loop(low_tile, mid_tile, lambda t, c: tile(t, True), None)
    lax.fori_loop(mid_tile, own_tile, lambda t, c: tile(t, False), None)
    for t in range(own_tile, tile_count):
        tile(t, True)


def forward_kernel(
    tile_len, last_half, bounds_ref, q_ref, k_ref, v_ref, low_ref, o_ref, lse_ref, max_ref, sum_ref, acc_ref
):
    span_len = q_ref.shape[0]
    key_len = k_ref.shape[0]
    own_base = key_len - span_len
    pair = pl.program_id(0)
    last = pair == pl.num_programs(0) - 1
    valid = jnp.where(last, last_half, LANES)
    q_t = (q_ref[...].astype(F32) * SCALE).T
    row = lax.broadcasted_iota(jnp.int32, q_t.shape, 0)
    heads = (
        jnp.where(row < HEAD, q_t, 0.0).astype(BF16),
        jnp.where((row >= HEAD) & (row < valid), q_t, 0.0).astype(BF16),
    )
    max_ref[...] = jnp.full_like(max_ref, NEG_FILL)
    sum_ref[...] = jnp.zeros_like(sum_ref)
    acc_ref[...] = jnp.zeros_like(acc_ref)

    def tile(t, masked):
        base = t * tile_len
        rows = pl.ds(pl.multiple_of(base, tile_len), tile_len)
        lane = lax.broadcasted_iota(jnp.int32, (tile_len, LANES), 1)
        k_tile = jnp.where(lane < valid, k_ref[rows, :], jnp.zeros((), BF16))
        v_t = v_ref[rows, :].T
        if masked:
            keep = keep_of(base, tile_len, low_ref[...], own_base)

        def one(head):
            scores = jnp.dot(k_tile, heads[head], preferred_element_type=F32)
            if masked:
                scores = jnp.where(keep, scores, NEG_FILL)
            old_max = max_ref[head]
            new_max = jnp.maximum(old_max, jnp.max(scores, axis=0, keepdims=True))
            shrink = jnp.exp(old_max - new_max)
            probs = jnp.exp(scores - new_max)
            max_ref[head] = new_max
            sum_ref[head] = sum_ref[head] * shrink + jnp.sum(probs, axis=0, keepdims=True)
            acc_ref[head] = acc_ref[head] * shrink + jnp.dot(
                v_t[head * HEAD : (head + 1) * HEAD], probs.astype(BF16), preferred_element_type=F32
            )

        one(0)
        pl.when(valid > HEAD)(lambda: one(1))

    tile_loops(bounds_ref, tile, own_base // tile_len, key_len // tile_len)
    safe = jnp.where(sum_ref[...] > 0, sum_ref[...], 1.0)
    out = jnp.concatenate([acc_ref[0] / safe[0], acc_ref[1] / safe[1]], axis=0)
    o_ref[...] = out.T.astype(BF16)
    lse_ref[0] = jnp.concatenate([max_ref[0] + jnp.log(safe[0]), max_ref[1] + jnp.log(safe[1])], axis=0)


def backward_kernel(
    tile_len, last_half, bounds_ref, q_ref, k_ref, v_ref, g_ref, o_ref, lse_ref, low_ref, dq_ref, dk_ref, dv_ref, acc_ref
):
    span_len = q_ref.shape[0]
    key_len = k_ref.shape[0]
    own_base = key_len - span_len
    pair = pl.program_id(0)
    last = pair == pl.num_programs(0) - 1
    valid = jnp.where(last, last_half, LANES)
    lane = lax.broadcasted_iota(jnp.int32, (span_len, LANES), 1)
    q_now = jnp.where(lane < valid, q_ref[...].astype(F32) * SCALE, 0.0)
    g_now = jnp.where(lane < valid, g_ref[...].astype(F32), 0.0)
    o_now = jnp.where(lane < valid, o_ref[...].astype(F32), 0.0)
    q_t, g_t, o_t = q_now.T, g_now.T, o_now.T
    row = lax.broadcasted_iota(jnp.int32, q_t.shape, 0)
    prod = g_t * o_t
    part = []
    for head in range(2):
        row_ok = (row < HEAD) if head == 0 else (row >= HEAD)
        lane_ok = (lane < HEAD) if head == 0 else (lane >= HEAD)
        part.append(
            (
                jnp.where(row_ok, q_t, 0.0).astype(BF16),
                jnp.where(row_ok, g_t, 0.0).astype(BF16),
                jnp.where(lane_ok, q_now, 0.0).astype(BF16),
                jnp.where(lane_ok, g_now, 0.0).astype(BF16),
                jnp.sum(prod[head * HEAD : (head + 1) * HEAD], axis=0, keepdims=True),
                lse_ref[0, head : head + 1],
            )
        )
    acc_ref[...] = jnp.zeros_like(acc_ref)

    def clear(t, carry):
        rows = pl.ds(pl.multiple_of(t * tile_len, tile_len), tile_len)
        dk_ref[rows, :] = jnp.zeros((tile_len, LANES), BF16)
        dv_ref[rows, :] = jnp.zeros((tile_len, LANES), BF16)
        return carry

    lax.fori_loop(0, bounds_ref[0], clear, None)

    def tile(t, masked):
        base = t * tile_len
        rows = pl.ds(pl.multiple_of(base, tile_len), tile_len)
        lane_k = lax.broadcasted_iota(jnp.int32, (tile_len, LANES), 1)
        k_tile = jnp.where(lane_k < valid, k_ref[rows, :], jnp.zeros((), BF16))
        v_tile = jnp.where(lane_k < valid, v_ref[rows, :], jnp.zeros((), BF16))
        k_t = k_tile.T
        if masked:
            keep = keep_of(base, tile_len, low_ref[...], own_base)

        def one(head):
            qh_t, gh_t, qh, gh, delta, lse = part[head]
            scores = jnp.dot(k_tile, qh_t, preferred_element_type=F32)
            probs = jnp.exp(scores - lse)
            if masked:
                probs = jnp.where(keep, probs, 0.0)
            dprobs = jnp.dot(v_tile, gh_t, preferred_element_type=F32)
            dscores = (probs * (dprobs - delta)).astype(BF16)
            dv = jnp.dot(probs.astype(BF16), gh, preferred_element_type=F32)
            dk = jnp.dot(dscores, qh, preferred_element_type=F32)
            acc_ref[head] += jnp.dot(
                k_t[head * HEAD : (head + 1) * HEAD], dscores, preferred_element_type=F32
            )
            return dk, dv

        def write(dk, dv):
            dk_ref[rows, :] = dk.astype(BF16)
            dv_ref[rows, :] = dv.astype(BF16)

        @pl.when(valid > HEAD)
        def _():
            dk_a, dv_a = one(0)
            dk_b, dv_b = one(1)
            write(dk_a + dk_b, dv_a + dv_b)

        @pl.when(valid <= HEAD)
        def _():
            write(*one(0))

    tile_loops(bounds_ref, tile, own_base // tile_len, key_len // tile_len)
    dq_ref[...] = (jnp.concatenate([acc_ref[0], acc_ref[1]], axis=0).T * SCALE).astype(BF16)


def attend_specs(span_len, key_len, width):
    pairs = pl.cdiv(width, LANES)
    tile_len = 256 if span_len % 256 == 0 else span_len
    last_half = width - (pairs - 1) * LANES
    own = pl.BlockSpec((span_len, LANES), lambda p, b: (0, p))
    keys = pl.BlockSpec((key_len, LANES), lambda p, b: (0, p))
    low = pl.BlockSpec((1, span_len), lambda p, b: (0, 0))
    lse = pl.BlockSpec((1, 2, span_len), lambda p, b: (p, 0, 0))
    return pairs, tile_len, last_half, own, keys, low, lse


def attend_forward(queries, keys, values, low_row, bounds):
    span_len, width = queries.shape
    key_len = keys.shape[0]
    pairs, tile_len, last_half, own, key_spec, low_spec, lse_spec = attend_specs(span_len, key_len, width)
    return pl.pallas_call(
        partial(forward_kernel, tile_len, last_half),
        out_shape=(
            jax.ShapeDtypeStruct((span_len, width), BF16),
            jax.ShapeDtypeStruct((pairs, 2, span_len), F32),
        ),
        grid_spec=pltpu.PrefetchScalarGridSpec(
            num_scalar_prefetch=1,
            grid=(pairs,),
            in_specs=[own, key_spec, key_spec, low_spec],
            out_specs=(own, lse_spec),
            scratch_shapes=[
                pltpu.VMEM((2, 1, span_len), F32),
                pltpu.VMEM((2, 1, span_len), F32),
                pltpu.VMEM((2, HEAD, span_len), F32),
            ],
        ),
        cost_estimate=pl.CostEstimate(
            flops=4 * span_len * key_len * width, bytes_accessed=4 * key_len * width, transcendentals=span_len * key_len * 17
        ),
        compiler_params=pltpu.CompilerParams(vmem_limit_bytes=40 * 1024 * 1024),
        name="attend_forward",
    )(bounds, queries, keys, values, low_row)


def attend_backward(queries, keys, values, out_grad, attended, lse, low_row, bounds):
    span_len, width = queries.shape
    key_len = keys.shape[0]
    pairs, tile_len, last_half, own, key_spec, low_spec, lse_spec = attend_specs(span_len, key_len, width)
    return pl.pallas_call(
        partial(backward_kernel, tile_len, last_half),
        out_shape=(
            jax.ShapeDtypeStruct((span_len, width), BF16),
            jax.ShapeDtypeStruct((key_len, width), BF16),
            jax.ShapeDtypeStruct((key_len, width), BF16),
        ),
        grid_spec=pltpu.PrefetchScalarGridSpec(
            num_scalar_prefetch=1,
            grid=(pairs,),
            in_specs=[own, key_spec, key_spec, own, own, lse_spec, low_spec],
            out_specs=(own, key_spec, key_spec),
            scratch_shapes=[pltpu.VMEM((2, HEAD, span_len), F32)],
        ),
        cost_estimate=pl.CostEstimate(
            flops=10 * span_len * key_len * width, bytes_accessed=8 * key_len * width, transcendentals=span_len * key_len * 17
        ),
        compiler_params=pltpu.CompilerParams(vmem_limit_bytes=40 * 1024 * 1024),
        name="attend_backward",
    )(bounds, queries, keys, values, out_grad, attended, lse, low_row)


def along_group(x, step, count, wrap):
    pairs = [(i, (i + step) % count) for i in range(count) if wrap or 0 <= i + step < count]
    return lax.ppermute(x, "group", pairs)


def flip(x, bit, count):
    return lax.ppermute(x, "dp", [(i, i ^ bit) for i in range(count)])


CORE, ACROSS, DOWN = 1, 2, 4


def pick(x, index, axis=0):
    return lax.dynamic_index_in_dim(x, index, axis, keepdims=False)


def put(x, part, index):
    start = tuple(index) + (0,) * (x.ndim - len(index))
    part = part.reshape((1,) * len(index) + part.shape)
    return lax.dynamic_update_slice(x, part, start)


def plane_share(mine, count):
    cut = (mine.shape[1] // 2 + 7) // 8 * 8
    from_x = flip(mine, ACROSS, count)
    from_y = flip(mine, DOWN, count)
    diag_low = flip(from_x[:, :cut], DOWN, count)
    diag_high = flip(from_y[:, cut:], ACROSS, count)
    return mine, from_x, from_y, jnp.concatenate([diag_low, diag_high], axis=1)


def fast_gather(own, place, count, groups, here):
    chip, core, z = here
    piece = pick(pick(own, chip), core)
    ring = []
    hop = piece
    for _ in range(groups - 1):
        hop = along_group(hop, 1, groups, True)
        ring.append(hop)
    shares = plane_share(jnp.stack(ring), count)
    mine = jnp.stack(shares)
    other = flip(mine, CORE, count)
    rows, cols = piece.shape
    whole = jnp.zeros((4, groups, 2, rows, cols), piece.dtype)
    whole = lax.dynamic_update_slice(whole, own[:, None], (0, z, 0, 0, 0))
    for k in range(4):
        for step in range(groups - 1):
            plane = lax.rem(z - step - 1 + groups, groups)
            whole = put(whole, mine[k, step], (chip ^ k, plane, core))
            whole = put(whole, other[k, step], (chip ^ k, plane, 1 - core))
    return whole


def fast_reduce(parts, count, groups, here):
    chip, core, z = here
    got = flip(pick(parts, 1 - core, 2), CORE, count)
    half = (pick(parts, core, 2).astype(F32) + got.astype(F32)).astype(BF16)
    cut = groups // 2
    to_own, to_x, to_y, to_diag = (pick(half, chip ^ k) for k in range(4))
    via_x = flip(to_diag[:cut], ACROSS, count)
    via_y = flip(to_diag[cut:], DOWN, count)
    send_y = jnp.concatenate([to_y[:cut] + via_x, to_y[cut:]])
    send_x = jnp.concatenate([to_x[:cut], to_x[cut:] + via_y])
    from_x = flip(send_x, ACROSS, count)
    from_y = flip(send_y, DOWN, count)
    mine = to_own.astype(F32) + from_x.astype(F32) + from_y.astype(F32)
    hop = None
    for step in range(1, groups):
        term = pick(mine, lax.rem(z - step + groups, groups))
        if hop is not None:
            term = term + hop.astype(F32)
        hop = along_group(term.astype(BF16), 1, groups, True)
    total = (pick(mine, z) + hop.astype(F32)).astype(BF16)
    shares = jnp.concatenate(plane_share(total[None], count))
    other = flip(shares, CORE, count)
    out = jnp.zeros((4, 2) + total.shape, BF16)
    for k in range(4):
        out = put(out, shares[k], (chip ^ k, core))
        out = put(out, other[k], (chip ^ k, 1 - core))
    return out


def mean_spread(values):
    center = values - jnp.mean(values, axis=-1, keepdims=True)
    spread = jnp.mean(center * center, axis=-1, keepdims=True)
    return center, lax.rsqrt(spread + EPSILON)


def layer_norm(values, gain, shift):
    center, scale = mean_spread(values)
    return center * scale * gain + shift


def layer_norm_back(values, gain, grad):
    center, scale = mean_spread(values)
    unit = center * scale
    inner = grad * gain
    back = scale * (
        inner
        - jnp.mean(inner, axis=-1, keepdims=True)
        - unit * jnp.mean(inner * unit, axis=-1, keepdims=True)
    )
    return back, jnp.sum(grad * unit, axis=0), jnp.sum(grad, axis=0)


def row_sum(values):
    return jnp.sum(values.astype(F32), axis=0)


def matmul(left, right):
    return jnp.dot(left, right, preferred_element_type=F32)


def weight_grad(left, right):
    return jnp.einsum("ra,rb->ab", left, right, preferred_element_type=F32).astype(BF16)


def back_through(grad_rows, weight):
    return jnp.einsum("rb,ab->ra", grad_rows, weight, preferred_element_type=F32)


def on_device(
    count,
    groups,
    tokens,
    segments,
    out_grad,
    norm1_gain,
    norm1_bias,
    w_query,
    query_bias,
    w_key,
    w_value,
    value_bias,
    w_out,
    out_bias,
    norm2_gain,
    norm2_bias,
    w_fc,
    fc_bias,
    w_proj,
    proj_bias,
):
    _, span_len, width = tokens.shape
    shard = width // groups
    chunks = w_fc.shape[1] // width
    key_len = segments.shape[1]
    z = lax.axis_index("group")
    place = lax.axis_index("dp")
    fast = count == 8 and groups == 4 and chunks == 4
    here = (place // 2, lax.rem(place, 2), z)

    small = jnp.concatenate(
        [norm1_gain, norm1_bias, query_bias, value_bias, out_bias, norm2_gain, norm2_bias, proj_bias, fc_bias]
    )
    small_all = lax.all_gather(small, "group")
    vectors = small_all[:, : 8 * shard].reshape(groups, 8, shard).transpose(1, 0, 2).reshape(8, width)
    gain_one, shift_one, bias_q, bias_v, bias_o, gain_two, shift_two, bias_p = vectors.astype(F32)
    bias_fc = small_all[:, 8 * shard :].astype(F32).reshape(chunks, 1, width)

    if fast:
        half = shard // 2
        attn_own = jnp.stack([w_query, w_key, w_value, w_out]).reshape(4, 2, half, width)
        fc_own = w_fc.reshape(2, half, chunks, width).transpose(2, 0, 1, 3)
        proj_own = w_proj.reshape(4, 2, half, width)
        attn = fast_gather(attn_own, place, count, groups, here).reshape(4, width, width)
        full_fc = fast_gather(fc_own, place, count, groups, here).reshape(4, width, width)
        full_proj = fast_gather(proj_own, place, count, groups, here).transpose(1, 0, 2, 3, 4).reshape(4, width, width)
        full_q, full_k, full_v, full_o = attn[0], attn[1], attn[2], attn[3]
    else:
        gather = partial(lax.all_gather, axis_name="group", axis=0, tiled=True)
        full_q, full_k, full_v, full_o = (gather(w) for w in (w_query, w_key, w_value, w_out))
        full_fc = gather(w_fc).reshape(width, chunks, width).transpose(1, 0, 2)
        full_proj = gather(w_proj).reshape(chunks, width, width)

    mine = tokens[0]
    hops = [mine]
    for _ in range(groups - 1):
        hops.append(along_group(hops[-1], 1, groups, False))
    reach = jnp.concatenate(hops[::-1]).astype(F32)
    own_base = key_len - span_len
    inputs = mine.astype(F32)

    seg = segments[0]
    seg_mine = lax.dynamic_slice_in_dim(seg, z * span_len, span_len)
    low_row = jnp.sum((seg[None, :] < seg_mine[:, None]).astype(jnp.int32), axis=1)
    low_row = low_row + (groups - 1 - z) * span_len
    tile_len = 256 if span_len % 256 == 0 else span_len
    low_tile = low_row[0] // tile_len
    mid_tile = jnp.clip((low_row[-1] + tile_len - 1) // tile_len, low_tile, own_base // tile_len)
    bounds = jnp.stack([low_tile, mid_tile]).astype(jnp.int32)
    low_row = low_row[None]

    normed_all = layer_norm(reach, gain_one, shift_one).astype(BF16)
    normed_one = layer_norm(inputs, gain_one, shift_one).astype(BF16)
    queries = (matmul(normed_one, full_q) + bias_q).astype(BF16)
    keys = matmul(normed_all, full_k).astype(BF16)
    values = (matmul(normed_all, full_v) + bias_v).astype(BF16)
    attended, lse = attend_forward(queries, keys, values, low_row, bounds)
    resid = inputs + matmul(attended, full_o) + bias_o
    normed_two = layer_norm(resid, gain_two, shift_two).astype(BF16)
    pre_act = jnp.einsum("td,jdf->jtf", normed_two, full_fc, preferred_element_type=F32) + bias_fc
    gelu_tanh = partial(jax.nn.gelu, approximate=True)
    hidden, gelu_back = jax.vjp(gelu_tanh, pre_act)
    hidden = hidden.astype(BF16)
    activations = resid + jnp.einsum("jtf,jfd->td", hidden, full_proj, preferred_element_type=F32) + bias_p

    cot = out_grad[0]
    proj_bias_grad = row_sum(cot)
    proj_grad = jnp.einsum("jtf,td->jfd", hidden, cot, preferred_element_type=F32).astype(BF16)
    hidden_grad = jnp.einsum("td,jfd->jtf", cot, full_proj, preferred_element_type=F32)
    pre_grad = gelu_back(hidden_grad)[0].astype(BF16)
    fc_bias_grad = jnp.sum(pre_grad.astype(F32), axis=1)
    fc_grad = jnp.einsum("td,jtf->jdf", normed_two, pre_grad, preferred_element_type=F32).astype(BF16)
    normed_two_grad = jnp.einsum("jtf,jdf->td", pre_grad, full_fc, preferred_element_type=F32)
    resid_part, gain_two_grad, shift_two_grad = layer_norm_back(resid, gain_two, normed_two_grad)
    resid_grad = cot.astype(F32) + resid_part
    resid_low = resid_grad.astype(BF16)
    out_bias_grad = row_sum(resid_low)
    out_w_grad = weight_grad(attended, resid_low)
    attended_grad = back_through(resid_low, full_o).astype(BF16)
    dqueries, dkeys, dvalues = attend_backward(queries, keys, values, attended_grad, attended, lse, low_row, bounds)
    query_bias_grad = row_sum(dqueries)
    value_bias_grad = row_sum(dvalues)
    q_grad = weight_grad(normed_one, dqueries)
    k_grad = weight_grad(normed_all, dkeys)
    v_grad = weight_grad(normed_all, dvalues)
    norm_terms = back_through(dkeys, full_k) + back_through(dvalues, full_v)
    moving = None
    for step in range(groups - 1):
        term = norm_terms[step * span_len : (step + 1) * span_len]
        if moving is not None:
            term = term + moving.astype(F32)
        moving = along_group(term.astype(BF16), -1, groups, False)
    normed_one_grad = back_through(dqueries, full_q) + norm_terms[own_base:] + moving.astype(F32)
    input_part, gain_one_grad, shift_one_grad = layer_norm_back(inputs, gain_one, normed_one_grad)
    tokens_grad = resid_grad + input_part

    vector_grads = jnp.stack(
        [
            gain_one_grad,
            shift_one_grad,
            query_bias_grad,
            value_bias_grad,
            out_bias_grad,
            gain_two_grad,
            shift_two_grad,
            proj_bias_grad,
        ]
    )
    vector_grads = vector_grads.reshape(8, groups, shard).transpose(1, 0, 2).reshape(groups, 8 * shard)
    vector_grads = jnp.concatenate([vector_grads, fc_bias_grad.reshape(groups, -1)], axis=1)
    vector_sums = pick(lax.psum(vector_grads, ("dp", "group")), z)
    eight = vector_sums[: 8 * shard].reshape(8, shard)
    fc_bias_sum = vector_sums[8 * shard :]
    if fast:
        proj_parts = proj_grad.reshape(groups, 4, 2, half, width).transpose(1, 0, 2, 3, 4)
        proj_sum = fast_reduce(proj_parts, count, groups, here).reshape(4 * shard, width).astype(F32)
        fc_sum = fast_reduce(fc_grad.reshape(4, groups, 2, half, width), count, groups, here)
        fc_sum = fc_sum.reshape(4, shard, width).transpose(1, 0, 2).reshape(shard, 4 * width).astype(F32)
        attn_parts = jnp.stack([q_grad, k_grad, v_grad, out_w_grad]).reshape(4, groups, 2, half, width)
        attn_sum = fast_reduce(attn_parts, count, groups, here).reshape(4, shard, width).astype(F32)
        q_sum, k_sum, v_sum, out_sum = attn_sum[0], attn_sum[1], attn_sum[2], attn_sum[3]
    else:

        def whole_sum(part):
            part = lax.psum_scatter(part, "group", scatter_dimension=0, tiled=True)
            return lax.psum(part.astype(F32), "dp")

        proj_sum = whole_sum(proj_grad.reshape(chunks * width, width))
        fc_sum = whole_sum(fc_grad.transpose(1, 0, 2).reshape(width, chunks * width))
        q_sum, k_sum, v_sum, out_sum = (whole_sum(g) for g in (q_grad, k_grad, v_grad, out_w_grad))
    return (
        activations[None],
        tokens_grad[None],
        eight[0],
        eight[1],
        q_sum,
        eight[2],
        k_sum,
        v_sum,
        eight[3],
        out_sum,
        eight[4],
        eight[5],
        eight[6],
        fc_sum,
        fc_bias_sum,
        proj_sum,
        eight[7],
    )


def solution(mesh):
    rows, vec, mat = P("dp", "group", None), P("group"), P("group", None)
    weights = (vec, vec, mat, vec, mat, mat, vec, mat, vec, vec, vec, mat, vec, mat, vec)
    return jax.shard_map(
        partial(on_device, mesh.shape["dp"], mesh.shape["group"]),
        mesh=mesh,
        in_specs=(rows, P("dp", None), rows) + weights,
        out_specs=(rows, rows) + weights,
        check_vma=False,
    )
```

time: 1950 us -> 921 us (0.47)
  waiting for transfers between devices: 1260 us -> 192 us
  matrix products: 347 us -> 136 us
  starting transfers between devices: 1.19 us -> 205 us
  Pallas kernels: 0 us -> 44.5 us
  local copies, waits for them, and re-layouts: 132 us -> 171 us
  blocking collectives: 110 us -> 82.7 us
    reduce_scatter x8 -> x0, waiting for transfers between devices: 650 us -> none  [the longest x1 172 us: on_device(): lax.psum_scatter(full_grads[13].astype(jnp.bfloat16), 'group', scatter_di...]
    all_gather x10 -> x0, waiting for transfers between devices: 505 us -> none  [the longest x1 164 us: on_device(): lax.all_gather(shards[13], 'group', axis=0, tiled=True)]
    dot_general x46 -> x18, matrix products: 347 us -> 136 us  [the longest x4 24.4 us: back_through(): jnp.einsum('rb,ab->ra', grad_rows, weight, preferred_element_type=F32)]
    ppermute x0 -> x69, starting transfers between devices: none -> 205 us  [the longest x24 106 us: along_group(): return lax.ppermute(x, 'group', pairs)]
    ppermute x0 -> x69, waiting for transfers between devices: none -> 192 us  [the longest x45 113 us: flip(): return lax.ppermute(x, 'dp', [(i, i ^ bit) for i in range(count)])]
    unnamed x22 -> x0, waiting for transfers between devices: 105 us -> none
    dynamic_update_slice x0 -> x95, local copies, waits for them, and re-layouts: none -> 75.1 us  [the longest x93 73 us: put(): return lax.dynamic_update_slice(x, part, start)]
    pallas_call x0 -> x2, Pallas kernels: none -> 44.5 us  [the longest x1 24.7 us: attend_backward(): pl.pallas_call(partial(backward_kernel, tile_len, last_half), out_shape=(...]
  transfers between devices with their start and end apart: 20 -> 69, of which waited for: 17 -> 32; matrix products, arithmetic and copies ran while one was open for 16% -> 26% of each run, Pallas kernels for 0% -> 0%
where the time goes in v1:
time: 921 us; the launch traced here: 911 us
  starting transfers between devices  205 us (22%)
  waiting for transfers between devices  192 us (21%)
  local copies, waits for them, and re-layouts  171 us (19%)
  matrix products  136 us (15%)
  blocking collectives  82.7 us (9%)
  other arithmetic  73.4 us (8%)
  Pallas kernels  44.5 us (5%)
    ppermute x45, waiting for transfers between devices, flip(): return lax.ppermute(x, 'dp', [(i, i ^ bit) for i in range(count)])  113 us
    ppermute x24, starting transfers between devices, along_group(): return lax.ppermute(x, 'group', pairs)  106 us
    ppermute x45, starting transfers between devices, flip(): return lax.ppermute(x, 'dp', [(i, i ^ bit) for i in range(count)])  98.7 us
    ppermute x24, waiting for transfers between devices, along_group(): return lax.ppermute(x, 'group', pairs)  79.4 us
    dynamic_update_slice x93, local copies, waits for them, and re-layouts, put(): return lax.dynamic_update_slice(x, part, start)  73 us
    psum x1, blocking collectives, on_device(): vector_sums = pick(lax.psum(vector_grads, ('dp', 'group')), z)  42.9 us
    unnamed x1, blocking collectives  39.8 us
    pallas_call x1, Pallas kernels, attend_backward(): pl.pallas_call(partial(backward_kernel, tile_len, last_half), out_shape=(...  24.7 us
  transfers between devices with their start and end apart: 69, of which 32 were waited for; matrix products, arithmetic and copies ran while one was open for 26% of the time, Pallas kernels for 0%

profile of v1, /device:TPU:0, one launch (start us, length us, event | category | flops | bytes accessed | tf_op | source)
XLA Modules:
  0.0 910.8 jit_solution(2791455828735501290)
XLA Ops:
  23.7 39.8 %all-reduce = bf16[13056]{0:T(1024)(128)(2,1)S(1)} all-reduce(bf16[13056]{0:T(1024)(128)(2,1)S(1)} %dynamic-update-slice), channel_id=2, replica_groups=mesh['dp'=8,'group'=4] {'group'}, use_global_device_ids=true, to_apply=%add | all-reduce | flops 13056 | bytes 52224
  87.2 10.1 %collective-permute-done.1 = bf16[136,1088]{1,0:T(8,128)(2,1)} collective-permute-done((bf16[136,1088]{1,0:T(8,128)(2,1)S(1)}, bf16[136,1088]{1,0:T(8,128)(2,1)}, u32[]{:S(2)}, u32[]{:S(2)}) %collective-permute-start.1) | collective-permute-done | bytes 295968 | tf_op jit(solution)/shard_map/ppermute | solution.py:243
  130.8 11.7 %collective-permute-done.4 = bf16[3,136,1088]{2,1,0:T(8,128)(2,1)S(1)} collective-permute-done((bf16[3,136,1088]{2,1,0:T(8,128)(2,1)S(1)}, bf16[3,136,1088]{2,1,0:T(8,128)(2,1)S(1)}, u32[]{:S(2)}, u32[]{:S(2)}) %collective-permute-start.4) | collective-permute-done | bytes 887840 | tf_op jit(solution)/shard_map/ppermute | solution.py:247
  146.3 16.3 %collective-permute-done.23 = bf16[3,136,1088]{2,1,0:T(8,128)(2,1)S(1)} collective-permute-done((bf16[3,136,1088]{2,1,0:T(8,128)(2,1)S(1)}, bf16[3,136,1088]{2,1,0:T(8,128)(2,1)S(1)}, u32[]{:S(2)}, u32[]{:S(2)}) %collective-permute-start.23) | collective-permute-done | bytes 887840 | tf_op jit(solution)/shard_map/ppermute | solution.py:247
  166.5 16.3 %collective-permute-done.15 = bf16[3,136,1088]{2,1,0:T(8,128)(2,1)S(1)} collective-permute-done((bf16[3,136,1088]{2,1,0:T(8,128)(2,1)S(1)}, bf16[3,136,1088]{2,1,0:T(8,128)(2,1)S(1)}, u32[]{:S(2)}, u32[]{:S(2)}) %collective-permute-start.15) | collective-permute-done | bytes 887840 | tf_op jit(solution)/shard_map/ppermute | solution.py:247
  186.0 7.2 collective-permute-done.6
  246.2 8.6 copy.178
  262.0 7.1 fusion.181
  283.4 7.5 convolution_convert_fusion.6.k_ref
  290.9 7.3 add_convert_fusion.v_ref
  300.4 19.8 %attend_forward.1 = (bf16[512,1088]{1,0:T(8,128)(2,1)S(1)}, f32[9,2,512]{2,1,0:T(2,128)S(1)}) custom-call(s32[2]{0:T(128)S(1)} %pad_add_fusion.bounds_ref, bf16[512,1088]{1,0:T(8,128)(2,1)S(1)} %fusion.24.q_ref, bf16[2048,1088]{1,0:T(8,128)(2,1)S(1)} %convolution_convert_fusion.6.k_ref, bf16[2048,1088]{1,0:T(8,128)(2,1)S(1)} %add_convert_fusion.v_ref, ...), custom_call_target="tpu_custom_call" | custom-call | flops 4563402752 | bytes 8912896 | tf_op jit(solution)/shard_map/attend_forward/pallas_call | solution.py:190
  326.1 8.7 fusion.170
  334.8 15.8 %convert_reduce_fusion.2 = (f32[4,1088]{1,0:T(4,128)}, bf16[4,512,1088]{1,2,0:T(8,128)(2,1)}) fusion(f32[4,1088,512]{2,1,0:T(8,128)} %fusion.170, f32[4,1088]{1,0:T(4,128)S(1)} %copy-done.57, bf16[4,1088,1088]{2,1,0:T(8,128)(2,1)S(1)} %bitcast.694, bf16[1,512,1088]{1,2,0:T(8,128)(2,1)} %param.20), kind=kOutput, calls=%fused_computation.36 | convolution fusion | flops 4899860480 | bytes 23988224 | tf_op jit(solution)/shard_map/td,jfd->jtf/dot_general | solution.py:451
  350.6 9.9 %multiply_reduce_fusion = (f32[1088]{0:T(1024)}, f32[512]{0:T(512)S(1)}, f32[512]{0:T(512)S(1)}, f32[1088]{0:T(1024)}, f32[512,1088]{0,1:T(8,128)S(1)}) fusion(f32[512,1088]{0,1:T(8,128)S(1)} %copy-done.15, f32[512]{0:T(512)S(1)} %add_rsqrt_fusion.1, f32[512]{0:T(512)S(1)} %broadcast_multiply_fusion.5, f32[1088]{0:T(1024)S(1)} %mul.199, ...), kind=kOutput, calls=%fused_computation.101 | convolution fusion | flops 4853625856 | bytes 18404096 | tf_op jit(solution)/shard_map/jtf,jdf->td/dot_general | solution.py:455
  370.2 24.7 %attend_backward.1 = (bf16[512,1088]{1,0:T(8,128)(2,1)S(1)}, bf16[2048,1088]{1,0:T(8,128)(2,1)S(1)}, bf16[2048,1088]{1,0:T(8,128)(2,1)S(1)}) custom-call(s32[2]{0:T(128)S(1)} %pad_add_fusion.bounds_ref, bf16[512,1088]{1,0:T(8,128)(2,1)S(1)} %copy-done.2, bf16[2048,1088]{1,0:T(8,128)(2,1)} %copy-done.3, bf16[2048,1088]{1,0:T(8,128)(2,1)} %copy-done.4, ...), custom_call_target="tpu_custom_call" | custom-call | flops 11408506880 | bytes 17825792 | tf_op jit(solution)/shard_map/attend_backward/pallas_call | solution.py:219
  395.0 8.2 fusion.185
  403.2 7.9 convolution_convert_fusion.4
  411.1 7.1 convolution_convert_fusion.3
  418.3 8.6 convolution_add_fusion
  441.4 8.2 convolution_convert_fusion.1
  455.1 15.2 %collective-permute-done.27 = bf16[512,1088]{0,1:T(8,128)(2,1)S(1)} collective-permute-done((bf16[512,1088]{0,1:T(8,128)(2,1)}, bf16[512,1088]{0,1:T(8,128)(2,1)S(1)}, u32[]{:S(2)}, u32[]{:S(2)}) %collective-permute-start.27) | collective-permute-done | bytes 1114144 | tf_op jit(solution)/shard_map/ppermute | solution.py:243
  472.9 14.7 %fusion.23 = f32[1,512,1088]{1,2,0:T(8,128)} fusion(f32[512,1088]{0,1:T(8,128)S(1)} %copy-done.16, bf16[4,1088,1088]{2,1,0:T(8,128)(2,1)} %bitcast.691, f32[1088]{0:T(1024)S(1)} %copy-done.65, f32[4,1088,512]{2,1,0:T(8,128)} %fusion.170, f32[4,1088]{1,0:T(4,128)S(1)} %copy-done.58), kind=kOutput, calls=%fused_computation.60 | convolution fusion | flops 4872011776 | bytes 22861056 | tf_op jit(solution)/shard_map/jtf,jfd->td/dot_general | solution.py:446
  495.0 13.5 %convolution_convert_fusion = bf16[4,1088,1088]{2,1,0:T(8,128)(2,1)} fusion(bf16[1,512,1088]{1,2,0:T(8,128)(2,1)S(1)} %copy-done.47, f32[4,1088,512]{2,1,0:T(8,128)} %fusion.170, f32[4,1088]{1,0:T(4,128)S(1)} %copy-done.58), kind=kOutput, calls=%fused_computation | convolution fusion | flops 4875632640 | bytes 19514368 | tf_op jit(solution)/shard_map/jtf,td->jfd/dot_general | solution.py:450
  513.9 15.1 %collective-permute-start.56 = (bf16[4,4,136,1088]{3,2,0,1:T(8,128)(2,1)}, bf16[4,4,136,1088]{3,2,0,1:T(8,128)(2,1)}, u32[]{:S(2)}, u32[]{:S(2)}) collective-permute-start(bf16[4,4,136,1088]{3,2,0,1:T(8,128)(2,1)} %dynamic-slice_bitcast_fusion), channel_id=1, source_target_pairs={{0,4},{4,0},{8,12},{12,8},{16,20},{20,16},{24,28},{28,24},{1,5},{5... | collective-permute-start | bytes 14204936 | tf_op jit(solution)/shard_map/ppermute | solution.py:247
  554.4 45.2 %collective-permute-start.31 = (bf16[2,136,1088]{2,1,0:T(8,128)(2,1)}, bf16[2,136,1088]{2,1,0:T(8,128)(2,1)}, u32[]{:S(2)}, u32[]{:S(2)}) collective-permute-start(bf16[2,136,1088]{2,1,0:T(8,128)(2,1)} %get-tuple-element.74), channel_id=1, source_target_pairs={{0,16},{4,20},{8,24},{12,28},{16,0},{20,4},{24,8},{28,12},{1,17},{... | collective-permute-start | bytes 1775624 | tf_op jit(solution)/shard_map/ppermute | solution.py:247
  618.9 9.5 %collective-permute-done.44 = bf16[2,136,1088]{2,1,0:T(8,128)(2,1)} collective-permute-done((bf16[2,136,1088]{2,1,0:T(8,128)(2,1)}, bf16[2,136,1088]{2,1,0:T(8,128)(2,1)}, u32[]{:S(2)}, u32[]{:S(2)}) %collective-permute-start.44) | collective-permute-done | bytes 591904 | tf_op jit(solution)/shard_map/ppermute | solution.py:247
  632.3 11.5 %collective-permute-done.59 = bf16[2,136,1088]{2,1,0:T(8,128)(2,1)S(1)} collective-permute-done((bf16[2,136,1088]{2,1,0:T(8,128)(2,1)S(1)}, bf16[2,136,1088]{2,1,0:T(8,128)(2,1)S(1)}, u32[]{:S(2)}, u32[]{:S(2)}) %collective-permute-start.59) | collective-permute-done | bytes 591904 | tf_op jit(solution)/shard_map/ppermute | solution.py:247
  644.4 24.2 %collective-permute-done.34 = bf16[4,136,1088]{2,1,0:T(8,128)(2,1)S(1)} collective-permute-done((bf16[4,136,1088]{2,1,0:T(8,128)(2,1)S(1)}, bf16[4,136,1088]{2,1,0:T(8,128)(2,1)S(1)}, u32[]{:S(2)}, u32[]{:S(2)}) %collective-permute-start.34) | collective-permute-done | bytes 1183776 | tf_op jit(solution)/shard_map/ppermute | solution.py:247
  671.3 30.3 %collective-permute-start.35 = (bf16[136,1088]{1,0:T(8,128)(2,1)S(1)}, bf16[136,1088]{1,0:T(8,128)(2,1)S(1)}, u32[]{:S(2)}, u32[]{:S(2)}) collective-permute-start(bf16[136,1088]{1,0:T(8,128)(2,1)S(1)} %fusion.77), channel_id=1, source_target_pairs={{0,1},{1,2},{2,3},{3,0},{4,5},{5,6},{6,7},{7,4},{8,9},{9,10},{10,1... | collective-permute-start | bytes 887816 | tf_op jit(solution)/shard_map/ppermute | solution.py:243
  702.2 24.1 %collective-permute-start.48 = (bf16[136,1088]{1,0:T(8,128)(2,1)S(1)}, bf16[136,1088]{1,0:T(8,128)(2,1)S(1)}, u32[]{:S(2)}, u32[]{:S(2)}) collective-permute-start(bf16[136,1088]{1,0:T(8,128)(2,1)S(1)} %fusion.78), channel_id=1, source_target_pairs={{0,1},{1,2},{2,3},{3,0},{4,5},{5,6},{6,7},{7,4},{8,9},{9,10},{10,1... | collective-permute-start | bytes 887816 | tf_op jit(solution)/shard_map/ppermute | solution.py:243
  726.8 24.9 %collective-permute-start.61 = (bf16[136,1088]{1,0:T(8,128)(2,1)S(1)}, bf16[136,1088]{1,0:T(8,128)(2,1)S(1)}, u32[]{:S(2)}, u32[]{:S(2)}) collective-permute-start(bf16[136,1088]{1,0:T(8,128)(2,1)S(1)} %fusion.79), channel_id=1, source_target_pairs={{0,1},{1,2},{2,3},{3,0},{4,5},{5,6},{6,7},{7,4},{8,9},{9,10},{10,1... | collective-permute-start | bytes 887816 | tf_op jit(solution)/shard_map/ppermute | solution.py:243
  808.5 42.9 %psum.7 = f32[4,3264]{1,0:T(4,128)} all-reduce(f32[4,3264]{1,0:T(4,128)S(1)} %pad_maximum_fusion.17), channel_id=1, replica_groups=mesh['dp'=8,'group'=4] {'dp','group'}, use_global_device_ids=true, to_apply=%region_20.21 | all-reduce | flops 13056 | bytes 104448 | tf_op jit(solution)/shard_map/psum | solution.py:493
  (556 shorter events, 382.4 us)
Async XLA Ops:
  2.7 82.3 %collective-permute-start = (bf16[136,1088]{1,0:T(8,128)(2,1)}, bf16[136,1088]{1,0:T(8,128)(2,1)S(1)}, u32[]{:S(2)}, u32[]{:S(2)}) collective-permute-start(bf16[136,1088]{1,0:T(8,128)(2,1)} %fusion.164), channel_id=1, source_target_pairs={{0,1},{1,2},{2,3},{3,0},{4,5},{5,6},{6,7},{7,4},{8,9},{9,10},{10,1... | collective-permute-start | bytes 887816 | tf_op jit(solution)/shard_map/ppermute | solution.py:243
  5.7 122.5 %collective-permute-start.8 = (bf16[512,1088]{0,1:T(8,128)(2,1)}, bf16[512,1088]{0,1:T(8,128)(2,1)S(1)}, u32[]{:S(2)}, u32[]{:S(2)}) collective-permute-start(bf16[512,1088]{0,1:T(8,128)(2,1)} %bitcast.686), channel_id=1, source_target_pairs={{0,1},{1,2},{2,3},{4,5},{5,6},{6,7},{8,9},{9,10},{10,11},{12,13},{... | collective-permute-start | bytes 3342344 | tf_op jit(solution)/shard_map/ppermute | solution.py:243
  11.2 74.3 %collective-permute-start.19 = (bf16[136,1088]{1,0:T(8,128)(2,1)}, bf16[136,1088]{1,0:T(8,128)(2,1)S(1)}, u32[]{:S(2)}, u32[]{:S(2)}) collective-permute-start(bf16[136,1088]{1,0:T(8,128)(2,1)} %dynamic-slice_bitcast_fusion.21), channel_id=1, source_target_pairs={{0,1},{1,2},{2,3},{3,0},{4,5},{5,6},{6,7},{7,4},{8,9},{9,10},{10,1... | collective-permute-start | bytes 887816 | tf_op jit(solution)/shard_map/ppermute | solution.py:243
  21.7 65.2 %collective-permute-start.11 = (bf16[136,1088]{1,0:T(8,128)(2,1)}, bf16[136,1088]{1,0:T(8,128)(2,1)S(1)}, u32[]{:S(2)}, u32[]{:S(2)}) collective-permute-start(bf16[136,1088]{1,0:T(8,128)(2,1)} %bitcast.683), channel_id=1, source_target_pairs={{0,1},{1,2},{2,3},{3,0},{4,5},{5,6},{6,7},{7,4},{8,9},{9,10},{10,1... | collective-permute-start | bytes 887816 | tf_op jit(solution)/shard_map/ppermute | solution.py:243
  124.0 38.7 %collective-permute-start.23 = (bf16[3,136,1088]{2,1,0:T(8,128)(2,1)S(1)}, bf16[3,136,1088]{2,1,0:T(8,128)(2,1)S(1)}, u32[]{:S(2)}, u32[]{:S(2)}) collective-permute-start(bf16[3,136,1088]{2,1,0:T(8,128)(2,1)S(1)} %get-tuple-element.86), channel_id=1, source_target_pairs={{0,16},{4,20},{8,24},{12,28},{16,0},{20,4},{24,8},{28,12},{1,17},{... | collective-permute-start | bytes 2663432 | tf_op jit(solution)/shard_map/ppermute | solution.py:247
  126.0 38.1 %collective-permute-start.22 = (bf16[3,136,1088]{2,1,0:T(8,128)(2,1)S(1)}, bf16[3,136,1088]{2,1,0:T(8,128)(2,1)S(1)}, u32[]{:S(2)}, u32[]{:S(2)}) collective-permute-start(bf16[3,136,1088]{2,1,0:T(8,128)(2,1)S(1)} %get-tuple-element.86), channel_id=1, source_target_pairs={{0,8},{4,12},{8,0},{12,4},{16,24},{20,28},{24,16},{28,20},{1,9},{5... | collective-permute-start | bytes 2663432 | tf_op jit(solution)/shard_map/ppermute | solution.py:247
  128.2 66.4 %collective-permute-start.9 = (bf16[512,1088]{0,1:T(8,128)(2,1)S(1)}, bf16[512,1088]{0,1:T(8,128)(2,1)S(1)}, u32[]{:S(2)}, u32[]{:S(2)}) collective-permute-start(bf16[512,1088]{0,1:T(8,128)(2,1)S(1)} %collective-permute-done.8), channel_id=1, source_target_pairs={{0,1},{1,2},{2,3},{4,5},{5,6},{6,7},{8,9},{9,10},{10,11},{12,13},{... | collective-permute-start | bytes 3342344 | tf_op jit(solution)/shard_map/ppermute | solution.py:243
  142.5 40.3 %collective-permute-start.15 = (bf16[3,136,1088]{2,1,0:T(8,128)(2,1)S(1)}, bf16[3,136,1088]{2,1,0:T(8,128)(2,1)S(1)}, u32[]{:S(2)}, u32[]{:S(2)}) collective-permute-start(bf16[3,136,1088]{2,1,0:T(8,128)(2,1)S(1)} %get-tuple-element.84), channel_id=1, source_target_pairs={{0,16},{4,20},{8,24},{12,28},{16,0},{20,4},{24,8},{28,12},{1,17},{... | collective-permute-start | bytes 2663432 | tf_op jit(solution)/shard_map/ppermute | solution.py:247
  144.0 40.3 %collective-permute-start.14 = (bf16[3,136,1088]{2,1,0:T(8,128)(2,1)S(1)}, bf16[3,136,1088]{2,1,0:T(8,128)(2,1)S(1)}, u32[]{:S(2)}, u32[]{:S(2)}) collective-permute-start(bf16[3,136,1088]{2,1,0:T(8,128)(2,1)S(1)} %get-tuple-element.84), channel_id=1, source_target_pairs={{0,8},{4,12},{8,0},{12,4},{16,24},{20,28},{24,16},{28,20},{1,9},{5... | collective-permute-start | bytes 2663432 | tf_op jit(solution)/shard_map/ppermute | solution.py:247
  162.6 30.5 %collective-permute-start.6 = (bf16[3,64,1088]{2,1,0:T(8,128)(2,1)S(1)}, bf16[3,64,1088]{2,1,0:T(8,128)(2,1)S(1)}, u32[]{:S(2)}, u32[]{:S(2)}) collective-permute-start(bf16[3,64,1088]{2,1,0:T(8,128)(2,1)S(1)} %slice.670), channel_id=1, source_target_pairs={{0,8},{4,12},{8,0},{12,4},{16,24},{20,28},{24,16},{28,20},{1,9},{5... | collective-permute-start | bytes 1253384 | tf_op jit(solution)/shard_map/ppermute | solution.py:247
  164.1 30.5 %collective-permute-start.5 = (bf16[3,72,1088]{2,1,0:T(8,128)(2,1)S(1)}, bf16[3,72,1088]{2,1,0:T(8,128)(2,1)S(1)}, u32[]{:S(2)}, u32[]{:S(2)}) collective-permute-start(bf16[3,72,1088]{2,1,0:T(8,128)(2,1)S(1)} %slice.669), channel_id=1, source_target_pairs={{0,16},{4,20},{8,24},{12,28},{16,0},{20,4},{24,8},{28,12},{1,17},{... | collective-permute-start | bytes 1410056 | tf_op jit(solution)/shard_map/ppermute | solution.py:247
  208.7 60.3 %collective-permute-start.18 = (bf16[4,3,136,1088]{3,2,1,0:T(8,128)(2,1)}, bf16[4,3,136,1088]{3,2,1,0:T(8,128)(2,1)}, u32[]{:S(2)}, u32[]{:S(2)}) collective-permute-start(bf16[4,3,136,1088]{3,2,1,0:T(8,128)(2,1)} %pad_maximum_fusion.3), channel_id=1, source_target_pairs={{0,4},{4,0},{8,12},{12,8},{16,20},{20,16},{24,28},{28,24},{1,5},{5... | collective-permute-start | bytes 10653704 | tf_op jit(solution)/shard_map/ppermute | solution.py:247
  428.2 42.0 %collective-permute-start.27 = (bf16[512,1088]{0,1:T(8,128)(2,1)}, bf16[512,1088]{0,1:T(8,128)(2,1)S(1)}, u32[]{:S(2)}, u32[]{:S(2)}) collective-permute-start(bf16[512,1088]{0,1:T(8,128)(2,1)} %slice.1043), channel_id=1, source_target_pairs={{1,0},{2,1},{3,2},{5,4},{6,5},{7,6},{9,8},{10,9},{11,10},{13,12},{... | collective-permute-start | bytes 3342344 | tf_op jit(solution)/shard_map/ppermute | solution.py:243
  441.0 106.7 %collective-permute-start.30 = (bf16[4,4,136,1088]{3,2,1,0:T(8,128)(2,1)}, bf16[4,4,136,1088]{3,2,1,0:T(8,128)(2,1)}, u32[]{:S(2)}, u32[]{:S(2)}) collective-permute-start(bf16[4,4,136,1088]{3,2,1,0:T(8,128)(2,1)} %dynamic-slice_bitcast_fusion.2), channel_id=1, source_target_pairs={{0,4},{4,0},{8,12},{12,8},{16,20},{20,16},{24,28},{28,24},{1,5},{5... | collective-permute-start | bytes 14204936 | tf_op jit(solution)/shard_map/ppermute | solution.py:247
  454.9 144.8 %collective-permute-start.43 = (bf16[4,4,136,1088]{3,2,1,0:T(8,128)(2,1)}, bf16[4,4,136,1088]{3,2,1,0:T(8,128)(2,1)}, u32[]{:S(2)}, u32[]{:S(2)}) collective-permute-start(bf16[4,4,136,1088]{3,2,1,0:T(8,128)(2,1)} %dynamic-slice_bitcast_fusion.1), channel_id=1, source_target_pairs={{0,4},{4,0},{8,12},{12,8},{16,20},{20,16},{24,28},{28,24},{1,5},{5... | collective-permute-start | bytes 14204936 | tf_op jit(solution)/shard_map/ppermute | solution.py:247
  493.7 43.1 %collective-permute-start.29 = (bf16[512,1088]{0,1:T(8,128)(2,1)}, bf16[512,1088]{0,1:T(8,128)(2,1)S(1)}, u32[]{:S(2)}, u32[]{:S(2)}) collective-permute-start(bf16[512,1088]{0,1:T(8,128)(2,1)} %fusion.44), channel_id=1, source_target_pairs={{1,0},{2,1},{3,2},{5,4},{6,5},{7,6},{9,8},{10,9},{11,10},{13,12},{... | collective-permute-start | bytes 3342344 | tf_op jit(solution)/shard_map/ppermute | solution.py:243
  513.9 94.3 %collective-permute-start.56 = (bf16[4,4,136,1088]{3,2,0,1:T(8,128)(2,1)}, bf16[4,4,136,1088]{3,2,0,1:T(8,128)(2,1)}, u32[]{:S(2)}, u32[]{:S(2)}) collective-permute-start(bf16[4,4,136,1088]{3,2,0,1:T(8,128)(2,1)} %dynamic-slice_bitcast_fusion), channel_id=1, source_target_pairs={{0,4},{4,0},{8,12},{12,8},{16,20},{20,16},{24,28},{28,24},{1,5},{5... | collective-permute-start | bytes 14204936 | tf_op jit(solution)/shard_map/ppermute | solution.py:247
  554.4 60.6 %collective-permute-start.31 = (bf16[2,136,1088]{2,1,0:T(8,128)(2,1)}, bf16[2,136,1088]{2,1,0:T(8,128)(2,1)}, u32[]{:S(2)}, u32[]{:S(2)}) collective-permute-start(bf16[2,136,1088]{2,1,0:T(8,128)(2,1)} %get-tuple-element.74), channel_id=1, source_target_pairs={{0,16},{4,20},{8,24},{12,28},{16,0},{20,4},{24,8},{28,12},{1,17},{... | collective-permute-start | bytes 1775624 | tf_op jit(solution)/shard_map/ppermute | solution.py:247
  618.7 49.9 %collective-permute-start.34 = (bf16[4,136,1088]{2,1,0:T(8,128)(2,1)S(1)}, bf16[4,136,1088]{2,1,0:T(8,128)(2,1)S(1)}, u32[]{:S(2)}, u32[]{:S(2)}) collective-permute-start(bf16[4,136,1088]{2,1,0:T(8,128)(2,1)S(1)} %pad_maximum_fusion.6), channel_id=1, source_target_pairs={{0,16},{4,20},{8,24},{12,28},{16,0},{20,4},{24,8},{28,12},{1,17},{... | collective-permute-start | bytes 3551240 | tf_op jit(solution)/shard_map/ppermute | solution.py:247
  628.4 42.2 %collective-permute-start.32 = (bf16[4,136,1088]{2,1,0:T(8,128)(2,1)S(1)}, bf16[4,136,1088]{2,1,0:T(8,128)(2,1)S(1)}, u32[]{:S(2)}, u32[]{:S(2)}) collective-permute-start(bf16[4,136,1088]{2,1,0:T(8,128)(2,1)S(1)} %pad_maximum_fusion.5), channel_id=1, source_target_pairs={{0,8},{4,12},{8,0},{12,4},{16,24},{20,28},{24,16},{28,20},{1,9},{5... | collective-permute-start | bytes 3551240 | tf_op jit(solution)/shard_map/ppermute | solution.py:247
  632.1 69.5 %collective-permute-start.47 = (bf16[4,136,1088]{2,1,0:T(8,128)(2,1)S(1)}, bf16[4,136,1088]{2,1,0:T(8,128)(2,1)S(1)}, u32[]{:S(2)}, u32[]{:S(2)}) collective-permute-start(bf16[4,136,1088]{2,1,0:T(8,128)(2,1)S(1)} %pad_maximum_fusion.9), channel_id=1, source_target_pairs={{0,16},{4,20},{8,24},{12,28},{16,0},{20,4},{24,8},{28,12},{1,17},{... | collective-permute-start | bytes 3551240 | tf_op jit(solution)/shard_map/ppermute | solution.py:247
  643.8 57.8 %collective-permute-start.45 = (bf16[4,136,1088]{2,1,0:T(8,128)(2,1)S(1)}, bf16[4,136,1088]{2,1,0:T(8,128)(2,1)S(1)}, u32[]{:S(2)}, u32[]{:S(2)}) collective-permute-start(bf16[4,136,1088]{2,1,0:T(8,128)(2,1)S(1)} %pad_maximum_fusion.8), channel_id=1, source_target_pairs={{0,8},{4,12},{8,0},{12,4},{16,24},{20,28},{24,16},{28,20},{1,9},{5... | collective-permute-start | bytes 3551240 | tf_op jit(solution)/shard_map/ppermute | solution.py:247
  644.0 82.2 %collective-permute-start.60 = (bf16[4,136,1088]{2,1,0:T(8,128)(2,1)S(1)}, bf16[4,136,1088]{2,1,0:T(8,128)(2,1)S(1)}, u32[]{:S(2)}, u32[]{:S(2)}) collective-permute-start(bf16[4,136,1088]{2,1,0:T(8,128)(2,1)S(1)} %pad_maximum_fusion.12), channel_id=1, source_target_pairs={{0,16},{4,20},{8,24},{12,28},{16,0},{20,4},{24,8},{28,12},{1,17},{... | collective-permute-start | bytes 3551240 | tf_op jit(solution)/shard_map/ppermute | solution.py:247
  668.6 57.7 %collective-permute-start.58 = (bf16[4,136,1088]{2,1,0:T(8,128)(2,1)S(1)}, bf16[4,136,1088]{2,1,0:T(8,128)(2,1)S(1)}, u32[]{:S(2)}, u32[]{:S(2)}) collective-permute-start(bf16[4,136,1088]{2,1,0:T(8,128)(2,1)S(1)} %pad_maximum_fusion.11), channel_id=1, source_target_pairs={{0,8},{4,12},{8,0},{12,4},{16,24},{20,28},{24,16},{28,20},{1,9},{5... | collective-permute-start | bytes 3551240 | tf_op jit(solution)/shard_map/ppermute | solution.py:247
  671.3 80.4 %collective-permute-start.35 = (bf16[136,1088]{1,0:T(8,128)(2,1)S(1)}, bf16[136,1088]{1,0:T(8,128)(2,1)S(1)}, u32[]{:S(2)}, u32[]{:S(2)}) collective-permute-start(bf16[136,1088]{1,0:T(8,128)(2,1)S(1)} %fusion.77), channel_id=1, source_target_pairs={{0,1},{1,2},{2,3},{3,0},{4,5},{5,6},{6,7},{7,4},{8,9},{9,10},{10,1... | collective-permute-start | bytes 887816 | tf_op jit(solution)/shard_map/ppermute | solution.py:243
  702.2 51.1 %collective-permute-start.48 = (bf16[136,1088]{1,0:T(8,128)(2,1)S(1)}, bf16[136,1088]{1,0:T(8,128)(2,1)S(1)}, u32[]{:S(2)}, u32[]{:S(2)}) collective-permute-start(bf16[136,1088]{1,0:T(8,128)(2,1)S(1)} %fusion.78), channel_id=1, source_target_pairs={{0,1},{1,2},{2,3},{3,0},{4,5},{5,6},{6,7},{7,4},{8,9},{9,10},{10,1... | collective-permute-start | bytes 887816 | tf_op jit(solution)/shard_map/ppermute | solution.py:243
  726.8 33.2 %collective-permute-start.61 = (bf16[136,1088]{1,0:T(8,128)(2,1)S(1)}, bf16[136,1088]{1,0:T(8,128)(2,1)S(1)}, u32[]{:S(2)}, u32[]{:S(2)}) collective-permute-start(bf16[136,1088]{1,0:T(8,128)(2,1)S(1)} %fusion.79), channel_id=1, source_target_pairs={{0,1},{1,2},{2,3},{3,0},{4,5},{5,6},{6,7},{7,4},{8,9},{9,10},{10,1... | collective-permute-start | bytes 887816 | tf_op jit(solution)/shard_map/ppermute | solution.py:243
  789.5 64.8 %collective-permute-start.39 = (bf16[1,136,1088]{2,1,0:T(8,128)(2,1)}, bf16[1,136,1088]{2,1,0:T(8,128)(2,1)}, u32[]{:S(2)}, u32[]{:S(2)}) collective-permute-start(bf16[1,136,1088]{2,1,0:T(8,128)(2,1)} %bitcast.153), channel_id=1, source_target_pairs={{0,16},{4,20},{8,24},{12,28},{16,0},{20,4},{24,8},{28,12},{1,17},{... | collective-permute-start | bytes 887816 | tf_op jit(solution)/shard_map/ppermute | solution.py:247
  797.8 59.8 %collective-permute-start.52 = (bf16[1,136,1088]{2,1,0:T(8,128)(2,1)}, bf16[1,136,1088]{2,1,0:T(8,128)(2,1)}, u32[]{:S(2)}, u32[]{:S(2)}) collective-permute-start(bf16[1,136,1088]{2,1,0:T(8,128)(2,1)} %bitcast.182), channel_id=1, source_target_pairs={{0,16},{4,20},{8,24},{12,28},{16,0},{20,4},{24,8},{28,12},{1,17},{... | collective-permute-start | bytes 887816 | tf_op jit(solution)/shard_map/ppermute | solution.py:247
  802.1 56.9 %collective-permute-start.64 = (bf16[1,136,1088]{2,1,0:T(8,128)(2,1)}, bf16[1,136,1088]{2,1,0:T(8,128)(2,1)S(1)}, u32[]{:S(2)}, u32[]{:S(2)}) collective-permute-start(bf16[1,136,1088]{2,1,0:T(8,128)(2,1)} %bitcast.210), channel_id=1, source_target_pairs={{0,8},{4,12},{8,0},{12,4},{16,24},{20,28},{24,16},{28,20},{1,9},{5... | collective-permute-start | bytes 887816 | tf_op jit(solution)/shard_map/ppermute | solution.py:247
  805.5 55.2 %collective-permute-start.65 = (bf16[1,136,1088]{2,1,0:T(8,128)(2,1)}, bf16[1,136,1088]{2,1,0:T(8,128)(2,1)}, u32[]{:S(2)}, u32[]{:S(2)}) collective-permute-start(bf16[1,136,1088]{2,1,0:T(8,128)(2,1)} %bitcast.210), channel_id=1, source_target_pairs={{0,16},{4,20},{8,24},{12,28},{16,0},{20,4},{24,8},{28,12},{1,17},{... | collective-permute-start | bytes 887816 | tf_op jit(solution)/shard_map/ppermute | solution.py:247
  808.4 53.3 %collective-permute-start.53 = (bf16[1,72,1088]{2,1,0:T(8,128)(2,1)}, bf16[1,72,1088]{2,1,0:T(8,128)(2,1)}, u32[]{:S(2)}, u32[]{:S(2)}) collective-permute-start(bf16[1,72,1088]{2,1,0:T(8,128)(2,1)} %slice.765), channel_id=1, source_target_pairs={{0,16},{4,20},{8,24},{12,28},{16,0},{20,4},{24,8},{28,12},{1,17},{... | collective-permute-start | bytes 470024 | tf_op jit(solution)/shard_map/ppermute | solution.py:247
  (130 other events, 2855.2 us)

commit v2 on v1

--- a/solution.py
+++ b/solution.py
@@ -38,13 +38,13 @@
 
 
 def forward_kernel(
-    tile_len, last_half, bounds_ref, q_ref, k_ref, v_ref, low_ref, o_ref, lse_ref, max_ref, sum_ref, acc_ref
+    first, pairs, tile_len, last_half, bounds_ref, q_ref, k_ref, v_ref, low_ref, *refs
 ):
+    o_ref, lse_ref, max_ref, sum_ref, acc_ref = refs[-5:]
     span_len = q_ref.shape[0]
     key_len = k_ref.shape[0]
     own_base = key_len - span_len
-    pair = pl.program_id(0)
-    last = pair == pl.num_programs(0) - 1
+    last = pl.program_id(0) + first == pairs - 1
     valid = jnp.where(last, last_half, LANES)
     q_t = (q_ref[...].astype(F32) * SCALE).T
     row = lax.broadcasted_iota(jnp.int32, q_t.shape, 0)
@@ -90,13 +90,13 @@
 
 
 def backward_kernel(
-    tile_len, last_half, bounds_ref, q_ref, k_ref, v_ref, g_ref, o_ref, lse_ref, low_ref, dq_ref, dk_ref, dv_ref, acc_ref
+    first, pairs, tile_len, last_half, bounds_ref, q_ref, k_ref, v_ref, g_ref, o_ref, lse_ref, low_ref, *refs
 ):
+    dq_ref, dk_ref, dv_ref, acc_ref = refs[-4:]
     span_len = q_ref.shape[0]
     key_len = k_ref.shape[0]
     own_base = key_len - span_len
-    pair = pl.program_id(0)
-    last = pair == pl.num_programs(0) - 1
+    last = pl.program_id(0) + first == pairs - 1
     valid = jnp.where(last, last_half, LANES)
     lane = lax.broadcasted_iota(jnp.int32, (span_len, LANES), 1)
     q_now = jnp.where(lane < valid, q_ref[...].astype(F32) * SCALE, 0.0)
@@ -172,70 +172,92 @@
     dq_ref[...] = (jnp.concatenate([acc_ref[0], acc_ref[1]], axis=0).T * SCALE).astype(BF16)
 
 
-def attend_specs(span_len, key_len, width):
+def attend_parts(pairs, number):
+    size = pl.cdiv(pairs, number)
+    return [(first, min(size, pairs - first)) for first in range(0, pairs, size)]
+
+
+def attend_specs(first, span_len, key_len):
+    own = pl.BlockSpec((span_len, LANES), lambda p, b: (0, p + first))
+    keys = pl.BlockSpec((key_len, LANES), lambda p, b: (0, p + first))
+    low = pl.BlockSpec((1, span_len), lambda p, b: (0, 0))
+    lse = pl.BlockSpec((1, 2, span_len), lambda p, b: (p + first, 0, 0))
+    return own, keys, low, lse
+
+
+def attend_call(kernel, name, part, span_len, key_len, width, inputs, in_kinds, outs, out_kinds, earlier, scratch, flops):
+    first, number = part
     pairs = pl.cdiv(width, LANES)
     tile_len = 256 if span_len % 256 == 0 else span_len
     last_half = width - (pairs - 1) * LANES
-    own = pl.BlockSpec((span_len, LANES), lambda p, b: (0, p))
-    keys = pl.BlockSpec((key_len, LANES), lambda p, b: (0, p))
-    low = pl.BlockSpec((1, span_len), lambda p, b: (0, 0))
-    lse = pl.BlockSpec((1, 2, span_len), lambda p, b: (p, 0, 0))
-    return pairs, tile_len, last_half, own, keys, low, lse
-
-
-def attend_forward(queries, keys, values, low_row, bounds):
+    specs = dict(zip(("own", "keys", "low", "lse"), attend_specs(first, span_len, key_len)))
+    earlier = () if earlier is None else tuple(earlier)
+    return pl.pallas_call(
+        partial(kernel, first, pairs, tile_len, last_half),
+        out_shape=outs,
+        grid_spec=pltpu.PrefetchScalarGridSpec(
+            num_scalar_prefetch=1,
+            grid=(number,),
+            in_specs=[specs[kind] for kind in in_kinds] + [pl.BlockSpec(memory_space=pl.ANY)] * len(earlier),
+            out_specs=tuple(specs[kind] for kind in out_kinds),
+            scratch_shapes=scratch,
+        ),
+        input_output_aliases={len(inputs) + i: i for i in range(len(earlier))},
+        cost_estimate=pl.CostEstimate(flops=flops * span_len * LANES, bytes_accessed=span_len * width, transcendentals=0),
+        compiler_params=pltpu.CompilerParams(vmem_limit_bytes=40 * 1024 * 1024),
+        name=name,
+    )(*inputs, *earlier)
+
+
+def attend_forward(part, queries, keys, values, low_row, bounds, earlier=None):
     span_len, width = queries.shape
     key_len = keys.shape[0]
-    pairs, tile_len, last_half, own, key_spec, low_spec, lse_spec = attend_specs(span_len, key_len, width)
-    return pl.pallas_call(
-        partial(forward_kernel, tile_len, last_half),
-        out_shape=(
+    return attend_call(
+        forward_kernel,
+        "attend_forward",
+        part,
+        span_len,
+        key_len,
+        width,
+        (bounds, queries, keys, values, low_row),
+        ("own", "keys", "keys", "low"),
+        (
             jax.ShapeDtypeStruct((span_len, width), BF16),
-            jax.ShapeDtypeStruct((pairs, 2, span_len), F32),
+            jax.ShapeDtypeStruct((pl.cdiv(width, LANES), 2, span_len), F32),
         ),
-        grid_spec=pltpu.PrefetchScalarGridSpec(
-            num_scalar_prefetch=1,
-            grid=(pairs,),
-            in_specs=[own, key_spec, key_spec, low_spec],
-            out_specs=(own, lse_spec),
-            scratch_shapes=[
-                pltpu.VMEM((2, 1, span_len), F32),
-                pltpu.VMEM((2, 1, span_len), F32),
-                pltpu.VMEM((2, HEAD, span_len), F32),
-            ],
-        ),
-        cost_estimate=pl.CostEstimate(
-            flops=4 * span_len * key_len * width, bytes_accessed=4 * key_len * width, transcendentals=span_len * key_len * 17
-        ),
-        compiler_params=pltpu.CompilerParams(vmem_limit_bytes=40 * 1024 * 1024),
-        name="attend_forward",
-    )(bounds, queries, keys, values, low_row)
-
-
-def attend_backward(queries, keys, values, out_grad, attended, lse, low_row, bounds):
+        ("own", "lse"),
+        earlier,
+        [
+            pltpu.VMEM((2, 1, span_len), F32),
+            pltpu.VMEM((2, 1, span_len), F32),
+            pltpu.VMEM((2, HEAD, span_len), F32),
+        ],
+        16,
+    )
+
+
+def attend_backward(part, queries, keys, values, out_grad, attended, lse, low_row, bounds, earlier=None):
     span_len, width = queries.shape
     key_len = keys.shape[0]
-    pairs, tile_len, last_half, own, key_spec, low_spec, lse_spec = attend_specs(span_len, key_len, width)
-    return pl.pallas_call(
-        partial(backward_kernel, tile_len, last_half),
-        out_shape=(
+    return attend_call(
+        backward_kernel,
+        "attend_backward",
+        part,
+        span_len,
+        key_len,
+        width,
+        (bounds, queries, keys, values, out_grad, attended, lse, low_row),
+        ("own", "keys", "keys", "own", "own", "lse", "low"),
+        (
             jax.ShapeDtypeStruct((span_len, width), BF16),
             jax.ShapeDtypeStruct((key_len, width), BF16),
             jax.ShapeDtypeStruct((key_len, width), BF16),
         ),
-        grid_spec=pltpu.PrefetchScalarGridSpec(
-            num_scalar_prefetch=1,
-            grid=(pairs,),
-            in_specs=[own, key_spec, key_spec, own, own, lse_spec, low_spec],
-            out_specs=(own, key_spec, key_spec),
-            scratch_shapes=[pltpu.VMEM((2, HEAD, span_len), F32)],
-        ),
-        cost_estimate=pl.CostEstimate(
-            flops=10 * span_len * key_len * width, bytes_accessed=8 * key_len * width, transcendentals=span_len * key_len * 17
-        ),
-        compiler_params=pltpu.CompilerParams(vmem_limit_bytes=40 * 1024 * 1024),
-        name="attend_backward",
-    )(bounds, queries, keys, values, out_grad, attended, lse, low_row)
+        ("own", "keys", "keys"),
+        earlier,
+        [pltpu.VMEM((2, HEAD, span_len), F32)],
+        40,
+    )
 
 
 def along_group(x, step, count, wrap):
@@ -260,60 +282,134 @@
     return lax.dynamic_update_slice(x, part, start)
 
 
-def plane_share(mine, count):
-    cut = (mine.shape[1] // 2 + 7) // 8 * 8
-    from_x = flip(mine, ACROSS, count)
-    from_y = flip(mine, DOWN, count)
-    diag_low = flip(from_x[:, :cut], DOWN, count)
-    diag_high = flip(from_y[:, cut:], ACROSS, count)
-    return mine, from_x, from_y, jnp.concatenate([diag_low, diag_high], axis=1)
-
-
-def fast_gather(own, place, count, groups, here):
-    chip, core, z = here
-    piece = pick(pick(own, chip), core)
-    ring = []
-    hop = piece
-    for _ in range(groups - 1):
-        hop = along_group(hop, 1, groups, True)
-        ring.append(hop)
-    shares = plane_share(jnp.stack(ring), count)
-    mine = jnp.stack(shares)
-    other = flip(mine, CORE, count)
-    rows, cols = piece.shape
-    whole = jnp.zeros((4, groups, 2, rows, cols), piece.dtype)
-    whole = lax.dynamic_update_slice(whole, own[:, None], (0, z, 0, 0, 0))
-    for k in range(4):
-        for step in range(groups - 1):
-            plane = lax.rem(z - step - 1 + groups, groups)
-            whole = put(whole, mine[k, step], (chip ^ k, plane, core))
-            whole = put(whole, other[k, step], (chip ^ k, plane, 1 - core))
-    return whole
-
-
-def fast_reduce(parts, count, groups, here):
-    chip, core, z = here
-    got = flip(pick(parts, 1 - core, 2), CORE, count)
-    half = (pick(parts, core, 2).astype(F32) + got.astype(F32)).astype(BF16)
-    cut = groups // 2
-    to_own, to_x, to_y, to_diag = (pick(half, chip ^ k) for k in range(4))
-    via_x = flip(to_diag[:cut], ACROSS, count)
-    via_y = flip(to_diag[cut:], DOWN, count)
-    send_y = jnp.concatenate([to_y[:cut] + via_x, to_y[cut:]])
-    send_x = jnp.concatenate([to_x[:cut], to_x[cut:] + via_y])
-    from_x = flip(send_x, ACROSS, count)
-    from_y = flip(send_y, DOWN, count)
-    mine = to_own.astype(F32) + from_x.astype(F32) + from_y.astype(F32)
-    hop = None
+def after(x, *before):
+    return lax.optimization_barrier((x,) + before)[0]
+
+
+def plane_share_near(mine, count):
+    return flip(mine, ACROSS, count), flip(mine, DOWN, count)
+
+
+def plane_share_far(from_x, from_y, count):
+    cut = cut_of(from_x)
+    return flip(from_x[:, :cut], DOWN, count), flip(from_y[:, cut:], ACROSS, count)
+
+
+def cut_of(part):
+    return (part.shape[1] // 2 + 7) // 8 * 8
+
+
+def assemble_kernel(groups, kind, here_ref, own_ref, *refs):
+    sources, outs, sems = refs[:10], refs[10:-1], refs[-1]
+    chip, core, z = here_ref[0], here_ref[1], here_ref[2]
+    cut = sources[3].shape[1]
+
+    def place(index, plane, half):
+        if kind == "plane":
+            return outs[0].at[plane, index, half]
+        if kind == "chip":
+            return outs[0].at[index, plane, half]
+        return outs[index].at[plane, half]
+
+    def move(index, k, wait):
+        n = 1 + k * 2 * (groups - 1)
+        for side in range(2):
+            half = core if side == 0 else 1 - core
+            for step in range(groups - 1):
+                target = place(index, lax.rem(z - step - 1 + groups, groups), half)
+                if k < 3:
+                    pairs = [(sources[side * 5 + k].at[step], target)]
+                else:
+                    pairs = [
+                        (sources[side * 5 + 3].at[step], target.at[:cut]),
+                        (sources[side * 5 + 4].at[step], target.at[cut:]),
+                    ]
+                for src, dst in pairs:
+                    copy = pltpu.make_async_copy(src, dst, sems.at[n])
+                    copy.wait() if wait else copy.start()
+                    n += 1
+
+    if kind == "plane":
+        owns = [(own_ref, outs[0].at[z])]
+    elif kind == "chip":
+        owns = [(own_ref, outs[0].at[:, z])]
+    else:
+        owns = [(own_ref.at[m], outs[m].at[z]) for m in range(4)]
+    last = sems.shape[0] - len(owns)
+    owns = [pltpu.make_async_copy(src, dst, sems.at[last + i]) for i, (src, dst) in enumerate(owns)]
+    for copy in owns:
+        copy.start()
+    for wait in (False, True):
+        for k in range(4):
+            if kind == "apart":
+                for m in range(4):
+                    pl.when(chip == m ^ k)(partial(move, m, k, wait))
+            else:
+                move(chip ^ k, k, wait)
+    for copy in owns:
+        copy.wait()
+
+
+def assemble(own, sources, here, groups, kind):
+    rows, cols = own.shape[2:]
+    if kind == "apart":
+        shapes = [(groups, 2, rows, cols)] * 4
+    else:
+        shapes = [(groups, 4, 2, rows, cols) if kind == "plane" else (4, groups, 2, rows, cols)]
+    return pl.pallas_call(
+        partial(assemble_kernel, groups, kind),
+        out_shape=[jax.ShapeDtypeStruct(shape, own.dtype) for shape in shapes],
+        grid_spec=pltpu.PrefetchScalarGridSpec(
+            num_scalar_prefetch=1,
+            grid=(1,),
+            in_specs=[pl.BlockSpec(memory_space=pl.ANY)] * 11,
+            out_specs=[pl.BlockSpec(shape, lambda i, h, n=len(shape): (0,) * n) for shape in shapes],
+            scratch_shapes=[pltpu.SemaphoreType.DMA((1 + 10 * (groups - 1) + 4,))],
+        ),
+        compiler_params=pltpu.CompilerParams(vmem_limit_bytes=40 * 1024 * 1024),
+        cost_estimate=pl.CostEstimate(flops=0, bytes_accessed=own.size, transcendentals=0),
+        name="assemble",
+    )(jnp.stack(here).astype(jnp.int32), own, *sources)
+
+
+def from_planes(piece, groups):
+    return jnp.stack([along_group(piece, step, groups, True) for step in range(1, groups)])
+
+
+def chip_sum(parts, core, count, axis):
+    got = flip(pick(parts, 1 - core, axis), CORE, count)
+    return (pick(parts, core, axis).astype(F32) + got.astype(F32)).astype(BF16)
+
+
+def plane_first_step(half, chip, count, axis):
+    to_diag = pick(half, chip ^ 3, axis)
+    cut = to_diag.shape[0] // 2
+    return flip(to_diag[:cut], ACROSS, count), flip(to_diag[cut:], DOWN, count)
+
+
+def plane_second_step(half, via, chip, count, axis):
+    to_own, to_x, to_y = (pick(half, chip ^ k, axis) for k in range(3))
+    cut = to_own.shape[0] // 2
+    from_y = flip(jnp.concatenate([to_y[:cut] + via[0], to_y[cut:]]), DOWN, count)
+    from_x = flip(jnp.concatenate([to_x[:cut], to_x[cut:] + via[1]]), ACROSS, count)
+    return (to_own.astype(F32) + from_x.astype(F32) + from_y.astype(F32)).astype(BF16)
+
+
+def line_sum(mine, z, groups):
+    total = pick(mine, z).astype(F32)
     for step in range(1, groups):
-        term = pick(mine, lax.rem(z - step + groups, groups))
-        if hop is not None:
-            term = term + hop.astype(F32)
-        hop = along_group(term.astype(BF16), 1, groups, True)
-    total = (pick(mine, z) + hop.astype(F32)).astype(BF16)
-    shares = jnp.concatenate(plane_share(total[None], count))
+        sent = pick(mine, lax.rem(z + step, groups))
+        total = total + along_group(sent, step, groups, True).astype(F32)
+    return total
+
+
+def shares_of(mine, near, far):
+    return jnp.concatenate((mine,) + near + (jnp.concatenate(far, axis=1),))
+
+
+def core_copies(shares, chip, core, count):
     other = flip(shares, CORE, count)
-    out = jnp.zeros((4, 2) + total.shape, BF16)
+    out = jnp.zeros((4, 2) + shares.shape[1:], shares.dtype)
     for k in range(4):
         out = put(out, shares[k], (chip ^ k, core))
         out = put(out, other[k], (chip ^ k, 1 - core))
@@ -383,43 +479,59 @@
 ):
     _, span_len, width = tokens.shape
     shard = width // groups
+    half = shard // 2
     chunks = w_fc.shape[1] // width
     key_len = segments.shape[1]
     z = lax.axis_index("group")
     place = lax.axis_index("dp")
     fast = count == 8 and groups == 4 and chunks == 4
-    here = (place // 2, lax.rem(place, 2), z)
+    chip, core = place // 2, lax.rem(place, 2)
+    here = (chip, core, z)
+    forward_parts = attend_parts(pl.cdiv(width, LANES), 3)
+    parts = attend_parts(pl.cdiv(width, LANES), 5)
 
     small = jnp.concatenate(
         [norm1_gain, norm1_bias, query_bias, value_bias, out_bias, norm2_gain, norm2_bias, proj_bias, fc_bias]
     )
-    small_all = lax.all_gather(small, "group")
+    small_rel = jnp.stack([small] + [along_group(small, step, groups, True) for step in range(1, groups)])
+    small_all = jnp.take(small_rel, lax.rem(z - jnp.arange(groups) + groups, groups), axis=0)
     vectors = small_all[:, : 8 * shard].reshape(groups, 8, shard).transpose(1, 0, 2).reshape(8, width)
     gain_one, shift_one, bias_q, bias_v, bias_o, gain_two, shift_two, bias_p = vectors.astype(F32)
     bias_fc = small_all[:, 8 * shard :].astype(F32).reshape(chunks, 1, width)
 
-    if fast:
-        half = shard // 2
+    mine = tokens[0]
+    inputs = mine.astype(F32)
+    normed_one = layer_norm(inputs, gain_one, shift_one).astype(BF16)
+    own_base = key_len - span_len
+    if fast:
         attn_own = jnp.stack([w_query, w_key, w_value, w_out]).reshape(4, 2, half, width)
+        attn_ring = from_planes(pick(pick(attn_own, chip), core), groups)
+        attn_near = plane_share_near(attn_ring, count)
+        hops = [mine, along_group(after(mine, attn_ring), 1, groups, False)]
+        attn_three = (attn_ring,) + attn_near
+        attn_far = plane_share_far(*attn_near, count)
+        attn_other = tuple(flip(after(part, *attn_near), CORE, count) for part in attn_three)
+        attn_other += tuple(flip(after(part, hops[1]), CORE, count) for part in attn_far)
+        hops.append(along_group(after(hops[1], *attn_far), 1, groups, False))
+        attn = assemble(attn_own, attn_three + attn_far + attn_other, here, groups, "apart")
+        full_q, full_k, full_v, full_o = (part.reshape(width, width) for part in attn)
+        queries = (matmul(normed_one, full_q) + bias_q).astype(BF16)
         fc_own = w_fc.reshape(2, half, chunks, width).transpose(2, 0, 1, 3)
+        fc_piece = pick(pick(fc_own, chip), core)
         proj_own = w_proj.reshape(4, 2, half, width)
-        attn = fast_gather(attn_own, place, count, groups, here).reshape(4, width, width)
-        full_fc = fast_gather(fc_own, place, count, groups, here).reshape(4, width, width)
-        full_proj = fast_gather(proj_own, place, count, groups, here).transpose(1, 0, 2, 3, 4).reshape(4, width, width)
-        full_q, full_k, full_v, full_o = attn[0], attn[1], attn[2], attn[3]
+        proj_piece = pick(pick(proj_own, chip), core)
+        hops.append(along_group(after(hops[2], queries), 1, groups, False))
+        fc_ring = from_planes(after(fc_piece, hops[3]), groups)
     else:
         gather = partial(lax.all_gather, axis_name="group", axis=0, tiled=True)
         full_q, full_k, full_v, full_o = (gather(w) for w in (w_query, w_key, w_value, w_out))
         full_fc = gather(w_fc).reshape(width, chunks, width).transpose(1, 0, 2)
         full_proj = gather(w_proj).reshape(chunks, width, width)
-
-    mine = tokens[0]
-    hops = [mine]
-    for _ in range(groups - 1):
-        hops.append(along_group(hops[-1], 1, groups, False))
+        queries = (matmul(normed_one, full_q) + bias_q).astype(BF16)
+        hops = [mine]
+        for _ in range(groups - 1):
+            hops.append(along_group(hops[-1], 1, groups, False))
     reach = jnp.concatenate(hops[::-1]).astype(F32)
-    own_base = key_len - span_len
-    inputs = mine.astype(F32)
 
     seg = segments[0]
     seg_mine = lax.dynamic_slice_in_dim(seg, z * span_len, span_len)
@@ -432,39 +544,95 @@
     low_row = low_row[None]
 
     normed_all = layer_norm(reach, gain_one, shift_one).astype(BF16)
-    normed_one = layer_norm(inputs, gain_one, shift_one).astype(BF16)
-    queries = (matmul(normed_one, full_q) + bias_q).astype(BF16)
     keys = matmul(normed_all, full_k).astype(BF16)
     values = (matmul(normed_all, full_v) + bias_v).astype(BF16)
-    attended, lse = attend_forward(queries, keys, values, low_row, bounds)
+    state = None
+    for number, part in enumerate(forward_parts):
+        row_now = low_row
+        if fast and number == 1:
+            fc_near = plane_share_near(after(fc_ring, state[0]), count)
+            proj_ring = from_planes(after(proj_piece, fc_ring, state[0]), groups)
+            row_now = after(low_row, fc_ring)
+        if fast and number == 2:
+            fc_three = (fc_ring,) + fc_near
+            fc_far = plane_share_far(*(after(part, state[0]) for part in fc_near), count)
+            fc_other = tuple(flip(after(part, state[0], *fc_near), CORE, count) for part in fc_three)
+            row_now = after(low_row, *fc_near)
+        state = attend_forward(part, queries, keys, values, row_now, bounds, state)
+    attended, lse = state
+    if fast:
+        fc_other += tuple(flip(after(part, attended), CORE, count) for part in fc_far)
+        proj_near = plane_share_near(after(proj_ring, attended, *fc_far), count)
+        attended = after(attended, proj_ring, *fc_far)
     resid = inputs + matmul(attended, full_o) + bias_o
     normed_two = layer_norm(resid, gain_two, shift_two).astype(BF16)
+    if fast:
+        full_fc = assemble(after(fc_own, normed_two), fc_three + fc_far + fc_other, here, groups, "chip")
+        full_fc = full_fc[0].reshape(4, width, width)
     pre_act = jnp.einsum("td,jdf->jtf", normed_two, full_fc, preferred_element_type=F32) + bias_fc
     gelu_tanh = partial(jax.nn.gelu, approximate=True)
     hidden, gelu_back = jax.vjp(gelu_tanh, pre_act)
     hidden = hidden.astype(BF16)
-    activations = resid + jnp.einsum("jtf,jfd->td", hidden, full_proj, preferred_element_type=F32) + bias_p
 
     cot = out_grad[0]
     proj_bias_grad = row_sum(cot)
-    proj_grad = jnp.einsum("jtf,td->jfd", hidden, cot, preferred_element_type=F32).astype(BF16)
-    hidden_grad = jnp.einsum("td,jfd->jtf", cot, full_proj, preferred_element_type=F32)
+    cot_now = cot
+    if fast:
+        proj_three = (proj_ring,) + proj_near
+        proj_far = plane_share_far(*(after(part, hidden) for part in proj_near), count)
+        proj_other = tuple(flip(after(part, hidden, *proj_near), CORE, count) for part in proj_three)
+        cot_now = after(cot, *proj_near)
+    proj_grad = jnp.einsum("jtf,td->jfd", hidden, cot_now, preferred_element_type=F32).astype(BF16)
+    cot_now = after(cot, proj_grad)
+    if fast:
+        proj_chip = chip_sum(proj_grad.reshape(groups, 4, 2, half, width), core, count, 2)
+        proj_other += tuple(flip(after(part, proj_grad), CORE, count) for part in proj_far)
+        full_proj = assemble(proj_own, proj_three + proj_far + proj_other, here, groups, "plane")
+        full_proj = full_proj[0].reshape(4, width, width)
+        proj_via = plane_first_step(proj_chip, chip, count, 1)
+        cot_now = after(cot, proj_chip)
+    hidden_grad = jnp.einsum("td,jfd->jtf", cot_now, full_proj, preferred_element_type=F32)
     pre_grad = gelu_back(hidden_grad)[0].astype(BF16)
     fc_bias_grad = jnp.sum(pre_grad.astype(F32), axis=1)
-    fc_grad = jnp.einsum("td,jtf->jdf", normed_two, pre_grad, preferred_element_type=F32).astype(BF16)
-    normed_two_grad = jnp.einsum("jtf,jdf->td", pre_grad, full_fc, preferred_element_type=F32)
+    normed_two_now = after(normed_two, *proj_via) if fast else normed_two
+    fc_grad = jnp.einsum("td,jtf->jdf", normed_two_now, pre_grad, preferred_element_type=F32).astype(BF16)
+    normed_two_grad = jnp.einsum("jtf,jdf->td", after(pre_grad, fc_grad), full_fc, preferred_element_type=F32)
     resid_part, gain_two_grad, shift_two_grad = layer_norm_back(resid, gain_two, normed_two_grad)
     resid_grad = cot.astype(F32) + resid_part
     resid_low = resid_grad.astype(BF16)
     out_bias_grad = row_sum(resid_low)
+    attended_grad = back_through(resid_low, full_o).astype(BF16)
     out_w_grad = weight_grad(attended, resid_low)
-    attended_grad = back_through(resid_low, full_o).astype(BF16)
-    dqueries, dkeys, dvalues = attend_backward(queries, keys, values, attended_grad, attended, lse, low_row, bounds)
+    if fast:
+        proj_mine = plane_second_step(after(proj_chip, pre_grad), proj_via, chip, count, 1)
+        fc_chip = chip_sum(fc_grad.reshape(4, groups, 2, half, width), core, count, 2)
+        fc_via = plane_first_step(after(fc_chip, proj_mine, attended_grad), chip, count, 0)
+        proj_line = line_sum(after(proj_mine, attended_grad), z, groups).astype(BF16)
+    state = None
+    for number, part in enumerate(parts):
+        row_now = low_row
+        if fast and number == 0:
+            row_now = after(low_row, proj_mine, fc_chip)
+        if fast and number == 1:
+            fc_mine = plane_second_step(after(fc_chip, state[0]), fc_via, chip, count, 0)
+            row_now = after(low_row, *fc_via)
+        if fast and number == 2:
+            proj_line_near = plane_share_near(after(proj_line, state[0])[None], count)
+            row_now = after(low_row, proj_line)
+        if fast and number == 3:
+            proj_line_far = plane_share_far(*(after(part, state[0]) for part in proj_line_near), count)
+            fc_line = line_sum(after(fc_mine, state[0]), z, groups).astype(BF16)
+            row_now = after(low_row, fc_mine, *proj_line_near)
+        if fast and number == 4:
+            proj_shares = shares_of(after(proj_line, state[0])[None], proj_line_near, proj_line_far)
+            proj_copies = core_copies(proj_shares, chip, core, count)
+            row_now = after(low_row, *proj_line_far)
+        state = attend_backward(part, queries, keys, values, attended_grad, attended, lse, row_now, bounds, state)
+    dqueries, dkeys, dvalues = state
     query_bias_grad = row_sum(dqueries)
     value_bias_grad = row_sum(dvalues)
-    q_grad = weight_grad(normed_one, dqueries)
-    k_grad = weight_grad(normed_all, dkeys)
-    v_grad = weight_grad(normed_all, dvalues)
+    if fast:
+        fc_line_near = plane_share_near(after(fc_line, dkeys)[None], count)
     norm_terms = back_through(dkeys, full_k) + back_through(dvalues, full_v)
     moving = None
     for step in range(groups - 1):
@@ -472,6 +640,27 @@
         if moving is not None:
             term = term + moving.astype(F32)
         moving = along_group(term.astype(BF16), -1, groups, False)
+    normed_now = after(normed_all, norm_terms)
+    if fast:
+        normed_now = after(normed_now, *fc_line_near)
+        fc_line_far = plane_share_far(*(after(part, norm_terms) for part in fc_line_near), count)
+        fc_shares = shares_of(fc_line[None], fc_line_near, fc_line_far)
+        fc_copies = core_copies(fc_shares, chip, core, count)
+    q_grad = weight_grad(normed_one, dqueries)
+    k_grad = weight_grad(normed_now, dkeys)
+    v_grad = weight_grad(normed_now, dvalues)
+    hidden_now = hidden
+    if fast:
+        attn_grads = jnp.stack([q_grad, k_grad, v_grad, out_w_grad]).reshape(4, groups, 2, half, width)
+        attn_chip = chip_sum(attn_grads, core, count, 2)
+        attn_via = plane_first_step(attn_chip, chip, count, 0)
+        hidden_now = after(hidden, attn_chip)
+        attn_mine = plane_second_step(attn_chip, attn_via, chip, count, 0)
+        attn_line = line_sum(attn_mine, z, groups).astype(BF16)
+        attn_near = plane_share_near(attn_line[None], count)
+        attn_far = plane_share_far(*attn_near, count)
+        attn_sum = core_copies(shares_of(attn_line[None], attn_near, attn_far), chip, core, count)
+    activations = resid + jnp.einsum("jtf,jfd->td", hidden_now, full_proj, preferred_element_type=F32) + bias_p
     normed_one_grad = back_through(dqueries, full_q) + norm_terms[own_base:] + moving.astype(F32)
     input_part, gain_one_grad, shift_one_grad = layer_norm_back(inputs, gain_one, normed_one_grad)
     tokens_grad = resid_grad + input_part
@@ -490,16 +679,17 @@
     )
     vector_grads = vector_grads.reshape(8, groups, shard).transpose(1, 0, 2).reshape(groups, 8 * shard)
     vector_grads = jnp.concatenate([vector_grads, fc_bias_grad.reshape(groups, -1)], axis=1)
-    vector_sums = pick(lax.psum(vector_grads, ("dp", "group")), z)
+    bit = 1
+    while bit < count:
+        vector_grads = vector_grads + flip(vector_grads, bit, count)
+        bit *= 2
+    vector_sums = line_sum(vector_grads, z, groups)
     eight = vector_sums[: 8 * shard].reshape(8, shard)
     fc_bias_sum = vector_sums[8 * shard :]
     if fast:
-        proj_parts = proj_grad.reshape(groups, 4, 2, half, width).transpose(1, 0, 2, 3, 4)
-        proj_sum = fast_reduce(proj_parts, count, groups, here).reshape(4 * shard, width).astype(F32)
-        fc_sum = fast_reduce(fc_grad.reshape(4, groups, 2, half, width), count, groups, here)
-        fc_sum = fc_sum.reshape(4, shard, width).transpose(1, 0, 2).reshape(shard, 4 * width).astype(F32)
-        attn_parts = jnp.stack([q_grad, k_grad, v_grad, out_w_grad]).reshape(4, groups, 2, half, width)
-        attn_sum = fast_reduce(attn_parts, count, groups, here).reshape(4, shard, width).astype(F32)
+        attn_sum = attn_sum.reshape(4, shard, width).astype(F32)
+        proj_sum = proj_copies.reshape(4 * shard, width).astype(F32)
+        fc_sum = fc_copies.reshape(4, shard, width).transpose(1, 0, 2).reshape(shard, 4 * width).astype(F32)
         q_sum, k_sum, v_sum, out_sum = attn_sum[0], attn_sum[1], attn_sum[2], attn_sum[3]
     else:
 

time: 921 us -> 797 us (0.87)
  the two profiles are of different devices: /device:TPU:0 before, /device:TPU:15 now
where the time goes in v2:
time: 797 us; the launch traced here: 783 us
  waiting for transfers between devices  220 us (28%)
  starting transfers between devices  133 us (17%)
  matrix products  131 us (16%)
  local copies, waits for them, and re-layouts  115 us (14%)
  Pallas kernels  107 us (13%)
  other arithmetic  70.8 us (9%)
    ppermute x30, waiting for transfers between devices, along_group(): return lax.ppermute(x, 'group', pairs)  118 us
    ppermute x60, waiting for transfers between devices, flip(): return lax.ppermute(x, 'dp', [(i, i ^ bit) for i in range(count)])  102 us
    pallas_call x8, Pallas kernels, attend_call(): pl.pallas_call(partial(kernel, first, pairs, tile_len, last_half), out_sh...  85.4 us
    ppermute x30, starting transfers between devices, along_group(): return lax.ppermute(x, 'group', pairs)  79.6 us
    ppermute x60, starting transfers between devices, flip(): return lax.ppermute(x, 'dp', [(i, i ^ bit) for i in range(count)])  53.1 us
    unnamed x226, local copies, waits for them, and re-layouts  45.8 us
    dot_general x4, matrix products, back_through(): jnp.einsum('rb,ab->ra', grad_rows, weight, preferred_element_type=F32)  24.5 us
    pallas_call x3, Pallas kernels, assemble(): pl.pallas_call(partial(assemble_kernel, groups, kind), out_shape=[jax.Sha...  21.9 us
  transfers between devices with their start and end apart: 90, of which 32 were waited for; matrix products, arithmetic and copies ran while one was open for 27% of the time, Pallas kernels for 12%

profile of v2, /device:TPU:15, one launch (start us, length us, event | category | flops | bytes accessed | tf_op | source)
XLA Modules:
  0.0 782.5 jit_solution(11582113572882346509)
XLA Ops:
  12.8 19.4 %collective-permute-done.4 = bf16[136,1088]{1,0:T(8,128)(2,1)S(1)} collective-permute-done((bf16[136,1088]{1,0:T(8,128)(2,1)S(1)}, bf16[136,1088]{1,0:T(8,128)(2,1)S(1)}, u32[]{:S(2)}, u32[]{:S(2)}) %collective-permute-start.4) | collective-permute-done | bytes 295968 | tf_op jit(solution)/shard_map/ppermute | solution.py:265
  42.9 14.5 %collective-permute-done.7.refs_2_ = bf16[3,136,1088]{2,1,0:T(8,128)(2,1)S(1)} collective-permute-done((bf16[3,136,1088]{2,1,0:T(8,128)(2,1)S(1)}, bf16[3,136,1088]{2,1,0:T(8,128)(2,1)S(1)}, u32[]{:S(2)}, u32[]{:S(2)}) %collective-permute-start.7) | collective-permute-done | bytes 887840 | tf_op jit(solution)/shard_map/ppermute | solution.py:269
  88.1 17.2 %collective-permute-done.16 = bf16[512,1088]{0,1:T(8,128)(2,1)} collective-permute-done((bf16[512,1088]{0,1:T(8,128)(2,1)}, bf16[512,1088]{0,1:T(8,128)(2,1)}, u32[]{:S(2)}, u32[]{:S(2)}) %collective-permute-start.16) | collective-permute-done | bytes 1114144 | tf_op jit(solution)/shard_map/ppermute | solution.py:265
  122.7 10.3 %collective-permute-done.17 = bf16[512,1088]{0,1:T(8,128)(2,1)} collective-permute-done((bf16[512,1088]{0,1:T(8,128)(2,1)}, bf16[512,1088]{0,1:T(8,128)(2,1)}, u32[]{:S(2)}, u32[]{:S(2)}) %collective-permute-start.17) | collective-permute-done | bytes 1114144 | tf_op jit(solution)/shard_map/ppermute | solution.py:265
  147.7 7.2 add_convert_fusion.v_ref
  162.1 12.7 %attend_forward.3 = (bf16[512,1088]{1,0:T(8,128)(2,1)S(1)}, f32[9,2,512]{2,1,0:T(2,128)S(1)}) custom-call(s32[2]{0:T(128)S(1)} %pad_add_fusion.bounds_ref, bf16[512,1088]{1,0:T(8,128)(2,1)S(1)} %fusion.25.q_ref, bf16[2048,1088]{1,0:T(8,128)(2,1)S(1)} %convolution_convert_fusion.6.k_ref, bf16[2048,1088]{1,0:T(8,128)(2,1)S(1)} %add_convert_fusion.v_ref, ...), custom_call_target="tpu_custom_call" | custom-call | flops 1048576 | bytes 557056 | tf_op jit(solution)/shard_map/attend_forward/pallas_call | solution.py:195
  198.4 12.7 %attend_forward.4 = (bf16[512,1088]{1,0:T(8,128)(2,1)S(1)}, f32[9,2,512]{2,1,0:T(2,128)S(1)}) custom-call(s32[2]{0:T(128)S(1)} %pad_add_fusion.bounds_ref, bf16[512,1088]{1,0:T(8,128)(2,1)S(1)} %fusion.25.q_ref, bf16[2048,1088]{1,0:T(8,128)(2,1)S(1)} %copy-done.4, bf16[2048,1088]{1,0:T(8,128)(2,1)S(1)} %copy-done.1, ...), custom_call_target="tpu_custom_call", output_to_operand_aliasing={{0}: (5, {}), {1}: (6, {})} | custom-call | flops 1048576 | bytes 557056 | tf_op jit(solution)/shard_map/attend_forward/pallas_call | solution.py:195
  221.7 10.9 %attend_forward.5 = (bf16[512,1088]{1,0:T(8,128)(2,1)S(1)}, f32[9,2,512]{2,1,0:T(2,128)S(1)}) custom-call(s32[2]{0:T(128)S(1)} %pad_add_fusion.bounds_ref, bf16[512,1088]{1,0:T(8,128)(2,1)S(1)} %fusion.25.q_ref, bf16[2048,1088]{1,0:T(8,128)(2,1)S(1)} %copy-done.5, bf16[2048,1088]{1,0:T(8,128)(2,1)S(1)} %copy-done.2, ...), custom_call_target="tpu_custom_call", output_to_operand_aliasing={{0}: (5, {}), {1}: (6, {})} | custom-call | flops 1048576 | bytes 557056 | tf_op jit(solution)/shard_map/attend_forward/pallas_call | solution.py:195
  239.2 7.5 assemble.4
  246.7 13.3 %fusion.19 = (bf16[4,512,1088]{1,2,0:T(8,128)(2,1)S(1)}, f32[4,1088,512]{2,1,0:T(8,128)}) fusion(f32[4,1088]{1,0:T(4,128)S(1)} %slice_convert_fusion.2, bf16[4,1088,1088]{2,1,0:T(8,128)(2,1)} %bitcast.378, bf16[512,1088]{0,1:T(8,128)(2,1)S(1)} %add_convert_fusion.1), kind=kOutput, calls=%fused_computation.36 | convolution fusion | flops 4870897664 | bytes 23970816 | tf_op jit(solution)/shard_map/td,jdf->jtf/dot_general | solution.py:572
  277.0 10.9 %collective-permute-done.36.refs_4_ = bf16[3,64,1088]{2,1,0:T(8,128)(2,1)S(1)} collective-permute-done((bf16[3,64,1088]{2,1,0:T(8,128)(2,1)S(1)}, bf16[3,64,1088]{2,1,0:T(8,128)(2,1)S(1)}, u32[]{:S(2)}, u32[]{:S(2)}) %collective-permute-start.36) | collective-permute-done | bytes 417824 | tf_op jit(solution)/shard_map/ppermute | solution.py:269
  297.1 8.1 %assemble.5 = bf16[4,4,2,136,1088]{4,3,2,1,0:T(8,128)(2,1)} custom-call(s32[3]{0:T(128)S(1)} %pad_add_fusion.1.here_ref, bf16[4,2,136,1088]{3,2,1,0:T(8,128)(2,1)S(1)} %bitcast.358, bf16[3,136,1088]{2,1,0:T(8,128)(2,1)S(1)} %pad_maximum_fusion.14.refs_0_, bf16[3,136,1088]{2,1,0:T(8,128)(2,1)} %collective-permute-done.33.refs_1_, ...), custom_call_target="tpu_custom_call" | custom-call | bytes 1183744 | tf_op jit(solution)/shard_map/assemble/pallas_call | solution.py:359
  311.6 16.8 %convert_reduce_fusion.2 = (f32[4,1088]{1,0:T(4,128)}, bf16[4,512,1088]{1,2,0:T(8,128)(2,1)S(1)}) fusion(f32[4,1088,512]{2,1,0:T(8,128)} %get-tuple-element.242, f32[4,1088]{1,0:T(4,128)S(1)} %slice_convert_fusion.2, bf16[4,1088,1088]{2,1,0:T(8,128)(2,1)} %bitcast.376, bf16[512,1088]{0,1:T(8,128)(2,1)S(1)} %bitcast.403), kind=kOutput, calls=%fused_computation.37 | convolution fusion | flops 4899860480 | bytes 23988224 | tf_op jit(solution)/shard_map/td,jfd->jtf/dot_general | solution.py:594
  328.5 8.0 %convolution_convert_fusion = bf16[4,1088,1088]{1,2,0:T(8,128)(2,1)} fusion(bf16[4,512,1088]{1,2,0:T(8,128)(2,1)S(1)} %get-tuple-element.138, bf16[512,1088]{0,1:T(8,128)(2,1)S(1)} %copy-done.69), kind=kOutput, calls=%fused_computation.1 | convolution fusion | flops 4853350400 | bytes 15040512 | tf_op jit(solution)/shard_map/td,jtf->jdf/dot_general | solution.py:598
  342.1 9.6 %multiply_reduce_fusion = (f32[1088]{0:T(1024)}, f32[512]{0:T(512)S(1)}, f32[512]{0:T(512)S(1)}, f32[1088]{0:T(1024)}, f32[512,1088]{0,1:T(8,128)S(1)}) fusion(f32[512,1088]{0,1:T(8,128)S(1)} %copy-done.47, f32[512]{0:T(512)S(1)} %add_rsqrt_fusion.1, f32[512]{0:T(512)S(1)} %broadcast_multiply_fusion.5, f32[1088]{0:T(1024)S(1)} %mul.199, ...), kind=kOutput, calls=%fused_computation.99 | convolution fusion | flops 4853625856 | bytes 18404096 | tf_op jit(solution)/shard_map/jtf,jdf->td/dot_general | solution.py:599
  358.7 22.6 %collective-permute-done.45 = bf16[4,136,1088]{2,1,0:T(8,128)(2,1)S(1)} collective-permute-done((bf16[4,136,1088]{2,1,0:T(8,128)(2,1)S(1)}, bf16[4,136,1088]{2,1,0:T(8,128)(2,1)S(1)}, u32[]{:S(2)}, u32[]{:S(2)}) %collective-permute-start.45) | collective-permute-done | bytes 1183776 | tf_op jit(solution)/shard_map/ppermute | solution.py:269
  395.4 10.2 %collective-permute-start.47 = (bf16[136,1088]{1,0:T(8,128)(2,1)S(1)}, bf16[136,1088]{1,0:T(8,128)(2,1)S(1)}, u32[]{:S(2)}, u32[]{:S(2)}) collective-permute-start(bf16[136,1088]{1,0:T(8,128)(2,1)S(1)} %get-tuple-element.225), channel_id=1, source_target_pairs={{0,1},{1,2},{2,3},{3,0},{4,5},{5,6},{6,7},{7,4},{8,9},{9,10},{10,1... | collective-permute-start | bytes 887816 | tf_op jit(solution)/shard_map/ppermute | solution.py:265
  414.9 11.8 %attend_backward.5 = (bf16[512,1088]{1,0:T(8,128)(2,1)S(1)}, bf16[2048,1088]{1,0:T(8,128)(2,1)S(1)}, bf16[2048,1088]{1,0:T(8,128)(2,1)S(1)}) custom-call(s32[2]{0:T(128)S(1)} %pad_add_fusion.bounds_ref, bf16[512,1088]{1,0:T(8,128)(2,1)S(1)} %fusion.25.q_ref, bf16[2048,1088]{1,0:T(8,128)(2,1)} %copy-done.3, bf16[2048,1088]{1,0:T(8,128)(2,1)} %copy-done, ...), custom_call_target="tpu_custom_call" | custom-call | flops 2621440 | bytes 557056 | tf_op jit(solution)/shard_map/attend_backward/pallas_call | solution.py:195
  432.2 8.6 %collective-permute-done.49 = bf16[136,1088]{1,0:T(8,128)(2,1)S(1)} collective-permute-done((bf16[136,1088]{1,0:T(8,128)(2,1)S(1)}, bf16[136,1088]{1,0:T(8,128)(2,1)S(1)}, u32[]{:S(2)}, u32[]{:S(2)}) %collective-permute-start.49) | collective-permute-done | bytes 295968 | tf_op jit(solution)/shard_map/ppermute | solution.py:265
  442.7 10.9 %attend_backward.6 = (bf16[512,1088]{1,0:T(8,128)(2,1)S(1)}, bf16[2048,1088]{1,0:T(8,128)(2,1)S(1)}, bf16[2048,1088]{1,0:T(8,128)(2,1)S(1)}) custom-call(s32[2]{0:T(128)S(1)} %pad_add_fusion.bounds_ref, bf16[512,1088]{1,0:T(8,128)(2,1)S(1)} %fusion.25.q_ref, ...), custom_call_target="tpu_custom_call", output_to_operand_aliasing={{0}: (8, {}), {1}: (9, {}), {2}: (10, {})} | custom-call | flops 2621440 | bytes 557056 | tf_op jit(solution)/shard_map/attend_backward/pallas_call | solution.py:195
  468.0 11.1 %attend_backward.7 = (bf16[512,1088]{1,0:T(8,128)(2,1)S(1)}, bf16[2048,1088]{1,0:T(8,128)(2,1)S(1)}, bf16[2048,1088]{1,0:T(8,128)(2,1)S(1)}) custom-call(s32[2]{0:T(128)S(1)} %pad_add_fusion.bounds_ref, bf16[512,1088]{1,0:T(8,128)(2,1)S(1)} %fusion.25.q_ref, ...), custom_call_target="tpu_custom_call", output_to_operand_aliasing={{0}: (8, {}), {1}: (9, {}), {2}: (10, {})} | custom-call | flops 2621440 | bytes 557056 | tf_op jit(solution)/shard_map/attend_backward/pallas_call | solution.py:195
  501.2 11.1 %attend_backward.8 = (bf16[512,1088]{1,0:T(8,128)(2,1)S(1)}, bf16[2048,1088]{1,0:T(8,128)(2,1)S(1)}, bf16[2048,1088]{1,0:T(8,128)(2,1)S(1)}) custom-call(s32[2]{0:T(128)S(1)} %pad_add_fusion.bounds_ref, bf16[512,1088]{1,0:T(8,128)(2,1)S(1)} %fusion.25.q_ref, ...), custom_call_target="tpu_custom_call", output_to_operand_aliasing={{0}: (8, {}), {1}: (9, {}), {2}: (10, {})} | custom-call | flops 2621440 | bytes 557056 | tf_op jit(solution)/shard_map/attend_backward/pallas_call | solution.py:195
  516.7 8.4 %fusion.109 = f32[2048,1088]{0,1:T(8,128)} fusion(bf16[2048,1088]{1,0:T(8,128)(2,1)S(1)} %get-tuple-element.166, bf16[1088,1088]{1,0:T(8,128)(2,1)S(1)} %bitcast.422), kind=kOutput, calls=%fused_computation.281 | convolution fusion | flops 4848615424 | bytes 15736832 | tf_op jit(solution)/shard_map/rb,ab->ra/dot_general | solution.py:455
  525.1 8.5 %convolution_add_fusion = f32[2048,1088]{0,1:T(8,128)S(1)} fusion(f32[2048,1088]{0,1:T(8,128)} %fusion.109, bf16[2048,1088]{1,0:T(8,128)(2,1)S(1)} %get-tuple-element.165, bf16[1088,1088]{1,0:T(8,128)(2,1)S(1)} %bitcast.370), kind=kOutput, calls=%fused_computation.18 | convolution fusion | flops 4850843648 | bytes 24649728 | tf_op jit(solution)/shard_map/rb,ab->ra/dot_general | solution.py:455
  537.3 7.4 collective-permute-start.59
  555.0 10.7 %collective-permute-done.59 = bf16[136,1088]{1,0:T(8,128)(2,1)} collective-permute-done((bf16[136,1088]{1,0:T(8,128)(2,1)}, bf16[136,1088]{1,0:T(8,128)(2,1)}, u32[]{:S(2)}, u32[]{:S(2)}) %collective-permute-start.59) | collective-permute-done | bytes 295968 | tf_op jit(solution)/shard_map/ppermute | solution.py:265
  573.3 9.0 %collective-permute-start.62 = (bf16[1,136,1088]{2,1,0:T(8,128)(2,1)S(1)}, bf16[1,136,1088]{2,1,0:T(8,128)(2,1)S(1)}, u32[]{:S(2)}, u32[]{:S(2)}) collective-permute-start(bf16[1,136,1088]{2,1,0:T(8,128)(2,1)S(1)} %bitcast.400), channel_id=1, source_target_pairs={{0,8},{4,12},{8,0},{12,4},{16,24},{20,28},{24,16},{28,20},{1,9},{5... | collective-permute-start | bytes 887816 | tf_op jit(solution)/shard_map/ppermute | solution.py:269
  587.1 7.6 convolution_convert_fusion.4
  624.9 17.3 %collective-permute-done.66 = bf16[512,1088]{0,1:T(8,128)(2,1)S(1)} collective-permute-done((bf16[512,1088]{0,1:T(8,128)(2,1)S(1)}, bf16[512,1088]{0,1:T(8,128)(2,1)S(1)}, u32[]{:S(2)}, u32[]{:S(2)}) %collective-permute-start.66) | collective-permute-done | bytes 1114144 | tf_op jit(solution)/shard_map/ppermute | solution.py:265
  656.1 15.5 %collective-permute-done.67 = bf16[512,1088]{0,1:T(8,128)(2,1)} collective-permute-done((bf16[512,1088]{0,1:T(8,128)(2,1)S(1)}, bf16[512,1088]{0,1:T(8,128)(2,1)}, u32[]{:S(2)}, u32[]{:S(2)}) %collective-permute-start.67) | collective-permute-done | bytes 1114144 | tf_op jit(solution)/shard_map/ppermute | solution.py:265
  684.2 26.2 %collective-permute-done.75 = bf16[4,136,1088]{2,1,0:T(8,128)(2,1)S(1)} collective-permute-done((bf16[4,136,1088]{2,1,0:T(8,128)(2,1)S(1)}, bf16[4,136,1088]{2,1,0:T(8,128)(2,1)S(1)}, u32[]{:S(2)}, u32[]{:S(2)}) %collective-permute-start.75) | collective-permute-done | bytes 1183776 | tf_op jit(solution)/shard_map/ppermute | solution.py:269
  766.1 13.5 %fusion.24 = f32[1,512,1088]{1,2,0:T(8,128)} fusion(f32[512,1088]{0,1:T(8,128)S(1)} %copy-done.48, bf16[4,512,1088]{1,2,0:T(8,128)(2,1)} %copy-done.100, bf16[4,1088,1088]{2,1,0:T(8,128)(2,1)} %bitcast.377, f32[1088]{0:T(1024)S(1)} %copy-done.84), kind=kOutput, calls=%fused_computation.59 | convolution fusion | flops 4849729536 | bytes 18387200 | tf_op jit(solution)/shard_map/jtf,jfd->td/dot_general | solution.py:663
  (566 shorter events, 387.1 us)
Async XLA Ops:
  6.9 28.3 %collective-permute-start.5 = (bf16[136,1088]{1,0:T(8,128)(2,1)S(1)}, bf16[136,1088]{1,0:T(8,128)(2,1)S(1)}, u32[]{:S(2)}, u32[]{:S(2)}) collective-permute-start(bf16[136,1088]{1,0:T(8,128)(2,1)S(1)} %dynamic-slice_bitcast_fusion.31), channel_id=1, source_target_pairs={{0,3},{1,0},{2,1},{3,2},{4,7},{5,4},{6,5},{7,6},{8,11},{9,8},{10,9... | collective-permute-start | bytes 887816 | tf_op jit(solution)/shard_map/ppermute | solution.py:265
  8.4 31.1 %collective-permute-start = (bf16[3264]{0:T(1024)(128)(2,1)S(1)}, bf16[3264]{0:T(1024)(128)(2,1)S(1)}, u32[]{:S(2)}, u32[]{:S(2)}) collective-permute-start(bf16[3264]{0:T(1024)(128)(2,1)S(1)} %concatenate.48), channel_id=1, source_target_pairs={{0,1},{1,2},{2,3},{3,0},{4,5},{5,6},{6,7},{7,4},{8,9},{9,10},{10,1... | collective-permute-start | bytes 19592 | tf_op jit(solution)/shard_map/ppermute | solution.py:265
  8.6 33.6 %collective-permute-start.1 = (bf16[3264]{0:T(1024)(128)(2,1)S(1)}, bf16[3264]{0:T(1024)(128)(2,1)S(1)}, u32[]{:S(2)}, u32[]{:S(2)}) collective-permute-start(bf16[3264]{0:T(1024)(128)(2,1)S(1)} %concatenate.48), channel_id=1, source_target_pairs={{0,2},{1,3},{2,0},{3,1},{4,6},{5,7},{6,4},{7,5},{8,10},{9,11},{10,... | collective-permute-start | bytes 19592 | tf_op jit(solution)/shard_map/ppermute | solution.py:265
  35.7 29.9 %collective-permute-start.13 = (bf16[512,1088]{0,1:T(8,128)(2,1)}, bf16[512,1088]{0,1:T(8,128)(2,1)}, u32[]{:S(2)}, u32[]{:S(2)}) collective-permute-start(bf16[512,1088]{0,1:T(8,128)(2,1)} %bitcast.371), channel_id=1, source_target_pairs={{0,1},{1,2},{2,3},{4,5},{5,6},{6,7},{8,9},{9,10},{10,11},{12,13},{... | collective-permute-start | bytes 3342344 | tf_op jit(solution)/shard_map/ppermute | solution.py:265
  75.5 29.7 %collective-permute-start.16 = (bf16[512,1088]{0,1:T(8,128)(2,1)}, bf16[512,1088]{0,1:T(8,128)(2,1)}, u32[]{:S(2)}, u32[]{:S(2)}) collective-permute-start(bf16[512,1088]{0,1:T(8,128)(2,1)} %collective-permute-done.13), channel_id=1, source_target_pairs={{0,1},{1,2},{2,3},{4,5},{5,6},{6,7},{8,9},{9,10},{10,11},{12,13},{... | collective-permute-start | bytes 3342344 | tf_op jit(solution)/shard_map/ppermute | solution.py:265
  105.2 27.7 %collective-permute-start.17 = (bf16[512,1088]{0,1:T(8,128)(2,1)}, bf16[512,1088]{0,1:T(8,128)(2,1)}, u32[]{:S(2)}, u32[]{:S(2)}) collective-permute-start(bf16[512,1088]{0,1:T(8,128)(2,1)} %collective-permute-done.16), channel_id=1, source_target_pairs={{0,1},{1,2},{2,3},{4,5},{5,6},{6,7},{8,9},{9,10},{10,11},{12,13},{... | collective-permute-start | bytes 3342344 | tf_op jit(solution)/shard_map/ppermute | solution.py:265
  132.9 41.9 %collective-permute-start.18 = (bf16[136,1088]{1,0:T(8,128)(2,1)S(1)}, bf16[136,1088]{1,0:T(8,128)(2,1)S(1)}, u32[]{:S(2)}, u32[]{:S(2)}) collective-permute-start(bf16[136,1088]{1,0:T(8,128)(2,1)S(1)} %bitcast.414), channel_id=1, source_target_pairs={{0,1},{1,2},{2,3},{3,0},{4,5},{5,6},{6,7},{7,4},{8,9},{9,10},{10,1... | collective-permute-start | bytes 887816 | tf_op jit(solution)/shard_map/ppermute | solution.py:265
  135.1 39.7 %collective-permute-start.19 = (bf16[136,1088]{1,0:T(8,128)(2,1)S(1)}, bf16[136,1088]{1,0:T(8,128)(2,1)S(1)}, u32[]{:S(2)}, u32[]{:S(2)}) collective-permute-start(bf16[136,1088]{1,0:T(8,128)(2,1)S(1)} %bitcast.415), channel_id=1, source_target_pairs={{0,2},{1,3},{2,0},{3,1},{4,6},{5,7},{6,4},{7,5},{8,10},{9,11},{10,... | collective-permute-start | bytes 887816 | tf_op jit(solution)/shard_map/ppermute | solution.py:265
  137.1 37.8 %collective-permute-start.20 = (bf16[136,1088]{1,0:T(8,128)(2,1)S(1)}, bf16[136,1088]{1,0:T(8,128)(2,1)S(1)}, u32[]{:S(2)}, u32[]{:S(2)}) collective-permute-start(bf16[136,1088]{1,0:T(8,128)(2,1)S(1)} %bitcast.416), channel_id=1, source_target_pairs={{0,3},{1,0},{2,1},{3,2},{4,7},{5,4},{6,5},{7,6},{8,11},{9,8},{10,9... | collective-permute-start | bytes 887816 | tf_op jit(solution)/shard_map/ppermute | solution.py:265
  175.0 36.1 %collective-permute-start.21 = (bf16[3,136,1088]{2,1,0:T(8,128)(2,1)S(1)}, bf16[3,136,1088]{2,1,0:T(8,128)(2,1)}, u32[]{:S(2)}, u32[]{:S(2)}) collective-permute-start(bf16[3,136,1088]{2,1,0:T(8,128)(2,1)S(1)} %pad_maximum_fusion.13.refs_0_), channel_id=1, source_target_pairs={{0,8},{4,12},{8,0},{12,4},{16,24},{20,28},{24,16},{28,20},{1,9},{5... | collective-permute-start | bytes 2663432 | tf_op jit(solution)/shard_map/ppermute | solution.py:269
  176.4 34.7 %collective-permute-start.22 = (bf16[3,136,1088]{2,1,0:T(8,128)(2,1)S(1)}, bf16[3,136,1088]{2,1,0:T(8,128)(2,1)}, u32[]{:S(2)}, u32[]{:S(2)}) collective-permute-start(bf16[3,136,1088]{2,1,0:T(8,128)(2,1)S(1)} %pad_maximum_fusion.13.refs_0_), channel_id=1, source_target_pairs={{0,16},{4,20},{8,24},{12,28},{16,0},{20,4},{24,8},{28,12},{1,17},{... | collective-permute-start | bytes 2663432 | tf_op jit(solution)/shard_map/ppermute | solution.py:269
  181.1 34.0 %collective-permute-start.23 = (bf16[136,1088]{1,0:T(8,128)(2,1)}, bf16[136,1088]{1,0:T(8,128)(2,1)}, u32[]{:S(2)}, u32[]{:S(2)}) collective-permute-start(bf16[136,1088]{1,0:T(8,128)(2,1)} %dynamic-slice_bitcast_fusion.30), channel_id=1, source_target_pairs={{0,1},{1,2},{2,3},{3,0},{4,5},{5,6},{6,7},{7,4},{8,9},{9,10},{10,1... | collective-permute-start | bytes 887816 | tf_op jit(solution)/shard_map/ppermute | solution.py:265
  186.7 28.4 %collective-permute-start.24 = (bf16[136,1088]{1,0:T(8,128)(2,1)}, bf16[136,1088]{1,0:T(8,128)(2,1)}, u32[]{:S(2)}, u32[]{:S(2)}) collective-permute-start(bf16[136,1088]{1,0:T(8,128)(2,1)} %dynamic-slice_bitcast_fusion.30), channel_id=1, source_target_pairs={{0,2},{1,3},{2,0},{3,1},{4,6},{5,7},{6,4},{7,5},{8,10},{9,11},{10,... | collective-permute-start | bytes 887816 | tf_op jit(solution)/shard_map/ppermute | solution.py:265
  271.6 33.5 %collective-permute-start.42 = (bf16[4,4,136,1088]{3,2,1,0:T(8,128)(2,1)}, bf16[4,4,136,1088]{3,2,1,0:T(8,128)(2,1)}, u32[]{:S(2)}, u32[]{:S(2)}) collective-permute-start(bf16[4,4,136,1088]{3,2,1,0:T(8,128)(2,1)} %dynamic-slice_bitcast_fusion.2), channel_id=1, source_target_pairs={{0,4},{4,0},{8,12},{12,8},{16,20},{20,16},{24,28},{28,24},{1,5},{5... | collective-permute-start | bytes 14204936 | tf_op jit(solution)/shard_map/ppermute | solution.py:269
  341.7 42.3 %collective-permute-start.50 = (bf16[4,4,136,1088]{3,2,1,0:T(8,128)(2,1)}, bf16[4,4,136,1088]{3,2,1,0:T(8,128)(2,1)}, u32[]{:S(2)}, u32[]{:S(2)}) collective-permute-start(bf16[4,4,136,1088]{3,2,1,0:T(8,128)(2,1)} %dynamic-slice_bitcast_fusion.1), channel_id=1, source_target_pairs={{0,4},{4,0},{8,12},{12,8},{16,20},{20,16},{24,28},{28,24},{1,5},{5... | collective-permute-start | bytes 14204936 | tf_op jit(solution)/shard_map/ppermute | solution.py:269
  352.2 29.1 %collective-permute-start.45 = (bf16[4,136,1088]{2,1,0:T(8,128)(2,1)S(1)}, bf16[4,136,1088]{2,1,0:T(8,128)(2,1)S(1)}, u32[]{:S(2)}, u32[]{:S(2)}) collective-permute-start(bf16[4,136,1088]{2,1,0:T(8,128)(2,1)S(1)} %pad_maximum_fusion.3), channel_id=1, source_target_pairs={{0,8},{4,12},{8,0},{12,4},{16,24},{20,28},{24,16},{28,20},{1,9},{5... | collective-permute-start | bytes 3551240 | tf_op jit(solution)/shard_map/ppermute | solution.py:269
  353.5 28.9 %collective-permute-start.46 = (bf16[4,136,1088]{2,1,0:T(8,128)(2,1)S(1)}, bf16[4,136,1088]{2,1,0:T(8,128)(2,1)S(1)}, u32[]{:S(2)}, u32[]{:S(2)}) collective-permute-start(bf16[4,136,1088]{2,1,0:T(8,128)(2,1)S(1)} %pad_maximum_fusion.4), channel_id=1, source_target_pairs={{0,16},{4,20},{8,24},{12,28},{16,0},{20,4},{24,8},{28,12},{1,17},{... | collective-permute-start | bytes 3551240 | tf_op jit(solution)/shard_map/ppermute | solution.py:269
  392.6 34.2 %collective-permute-start.51 = (bf16[2,136,1088]{2,1,0:T(8,128)(2,1)}, bf16[2,136,1088]{2,1,0:T(8,128)(2,1)}, u32[]{:S(2)}, u32[]{:S(2)}) collective-permute-start(bf16[2,136,1088]{2,1,0:T(8,128)(2,1)} %get-tuple-element.212), channel_id=1, source_target_pairs={{0,8},{4,12},{8,0},{12,4},{16,24},{20,28},{24,16},{28,20},{1,9},{5... | collective-permute-start | bytes 1775624 | tf_op jit(solution)/shard_map/ppermute | solution.py:269
  392.9 33.9 %collective-permute-start.52 = (bf16[2,136,1088]{2,1,0:T(8,128)(2,1)}, bf16[2,136,1088]{2,1,0:T(8,128)(2,1)}, u32[]{:S(2)}, u32[]{:S(2)}) collective-permute-start(bf16[2,136,1088]{2,1,0:T(8,128)(2,1)} %get-tuple-element.211), channel_id=1, source_target_pairs={{0,16},{4,20},{8,24},{12,28},{16,0},{20,4},{24,8},{28,12},{1,17},{... | collective-permute-start | bytes 1775624 | tf_op jit(solution)/shard_map/ppermute | solution.py:269
  395.4 36.4 %collective-permute-start.47 = (bf16[136,1088]{1,0:T(8,128)(2,1)S(1)}, bf16[136,1088]{1,0:T(8,128)(2,1)S(1)}, u32[]{:S(2)}, u32[]{:S(2)}) collective-permute-start(bf16[136,1088]{1,0:T(8,128)(2,1)S(1)} %get-tuple-element.225), channel_id=1, source_target_pairs={{0,1},{1,2},{2,3},{3,0},{4,5},{5,6},{6,7},{7,4},{8,9},{9,10},{10,1... | collective-permute-start | bytes 887816 | tf_op jit(solution)/shard_map/ppermute | solution.py:265
  412.7 28.1 %collective-permute-start.49 = (bf16[136,1088]{1,0:T(8,128)(2,1)S(1)}, bf16[136,1088]{1,0:T(8,128)(2,1)S(1)}, u32[]{:S(2)}, u32[]{:S(2)}) collective-permute-start(bf16[136,1088]{1,0:T(8,128)(2,1)S(1)} %get-tuple-element.226), channel_id=1, source_target_pairs={{0,3},{1,0},{2,1},{3,2},{4,7},{5,4},{6,5},{7,6},{8,11},{9,8},{10,9... | collective-permute-start | bytes 887816 | tf_op jit(solution)/shard_map/ppermute | solution.py:265
  429.4 64.6 %collective-permute-start.57 = (bf16[4,136,1088]{2,1,0:T(8,128)(2,1)}, bf16[4,136,1088]{2,1,0:T(8,128)(2,1)}, u32[]{:S(2)}, u32[]{:S(2)}) collective-permute-start(bf16[4,136,1088]{2,1,0:T(8,128)(2,1)} %pad_maximum_fusion.5), channel_id=1, source_target_pairs={{0,8},{4,12},{8,0},{12,4},{16,24},{20,28},{24,16},{28,20},{1,9},{5... | collective-permute-start | bytes 3551240 | tf_op jit(solution)/shard_map/ppermute | solution.py:269
  431.8 62.2 %collective-permute-start.58 = (bf16[4,136,1088]{2,1,0:T(8,128)(2,1)}, bf16[4,136,1088]{2,1,0:T(8,128)(2,1)}, u32[]{:S(2)}, u32[]{:S(2)}) collective-permute-start(bf16[4,136,1088]{2,1,0:T(8,128)(2,1)} %pad_maximum_fusion.6), channel_id=1, source_target_pairs={{0,16},{4,20},{8,24},{12,28},{16,0},{20,4},{24,8},{28,12},{1,17},{... | collective-permute-start | bytes 3551240 | tf_op jit(solution)/shard_map/ppermute | solution.py:269
  537.3 28.4 %collective-permute-start.59 = (bf16[136,1088]{1,0:T(8,128)(2,1)}, bf16[136,1088]{1,0:T(8,128)(2,1)}, u32[]{:S(2)}, u32[]{:S(2)}) collective-permute-start(bf16[136,1088]{1,0:T(8,128)(2,1)} %get-tuple-element.222), channel_id=1, source_target_pairs={{0,1},{1,2},{2,3},{3,0},{4,5},{5,6},{6,7},{7,4},{8,9},{9,10},{10,1... | collective-permute-start | bytes 887816 | tf_op jit(solution)/shard_map/ppermute | solution.py:265
  551.3 64.8 %collective-permute-start.89 = (bf16[4,136,1088]{2,1,0:T(8,128)(2,1)}, bf16[4,136,1088]{2,1,0:T(8,128)(2,1)S(1)}, u32[]{:S(2)}, u32[]{:S(2)}) collective-permute-start(bf16[4,136,1088]{2,1,0:T(8,128)(2,1)} %pad_maximum_fusion.11), channel_id=1, source_target_pairs={{0,4},{4,0},{8,12},{12,8},{16,20},{20,16},{24,28},{28,24},{1,5},{5... | collective-permute-start | bytes 3551240 | tf_op jit(solution)/shard_map/ppermute | solution.py:269
  551.3 60.6 %collective-permute-start.65 = (bf16[512,1088]{0,1:T(8,128)(2,1)S(1)}, bf16[512,1088]{0,1:T(8,128)(2,1)}, u32[]{:S(2)}, u32[]{:S(2)}) collective-permute-start(bf16[512,1088]{0,1:T(8,128)(2,1)S(1)} %slice.441), channel_id=1, source_target_pairs={{1,0},{2,1},{3,2},{5,4},{6,5},{7,6},{9,8},{10,9},{11,10},{13,12},{... | collective-permute-start | bytes 3342344 | tf_op jit(solution)/shard_map/ppermute | solution.py:265
  610.9 35.7 %collective-permute-start.64 = (bf16[4,4,136,1088]{3,2,1,0:T(8,128)(2,1)S(1)}, bf16[4,4,136,1088]{3,2,1,0:T(8,128)(2,1)}, u32[]{:S(2)}, u32[]{:S(2)}) collective-permute-start(bf16[4,4,136,1088]{3,2,1,0:T(8,128)(2,1)S(1)} %dynamic-slice_bitcast_fusion), channel_id=1, source_target_pairs={{0,4},{4,0},{8,12},{12,8},{16,20},{20,16},{24,28},{28,24},{1,5},{5... | collective-permute-start | bytes 14204936 | tf_op jit(solution)/shard_map/ppermute | solution.py:269
  614.2 28.1 %collective-permute-start.66 = (bf16[512,1088]{0,1:T(8,128)(2,1)S(1)}, bf16[512,1088]{0,1:T(8,128)(2,1)S(1)}, u32[]{:S(2)}, u32[]{:S(2)}) collective-permute-start(bf16[512,1088]{0,1:T(8,128)(2,1)S(1)} %fusion.47), channel_id=1, source_target_pairs={{1,0},{2,1},{3,2},{5,4},{6,5},{7,6},{9,8},{10,9},{11,10},{13,12},{... | collective-permute-start | bytes 3342344 | tf_op jit(solution)/shard_map/ppermute | solution.py:265
  681.2 29.2 %collective-permute-start.75 = (bf16[4,136,1088]{2,1,0:T(8,128)(2,1)S(1)}, bf16[4,136,1088]{2,1,0:T(8,128)(2,1)S(1)}, u32[]{:S(2)}, u32[]{:S(2)}) collective-permute-start(bf16[4,136,1088]{2,1,0:T(8,128)(2,1)S(1)} %pad_maximum_fusion.7), channel_id=1, source_target_pairs={{0,8},{4,12},{8,0},{12,4},{16,24},{20,28},{24,16},{28,20},{1,9},{5... | collective-permute-start | bytes 3551240 | tf_op jit(solution)/shard_map/ppermute | solution.py:269
  681.5 29.0 %collective-permute-start.77 = (bf16[4,136,1088]{2,1,0:T(8,128)(2,1)S(1)}, bf16[4,136,1088]{2,1,0:T(8,128)(2,1)S(1)}, u32[]{:S(2)}, u32[]{:S(2)}) collective-permute-start(bf16[4,136,1088]{2,1,0:T(8,128)(2,1)S(1)} %pad_maximum_fusion.8), channel_id=1, source_target_pairs={{0,16},{4,20},{8,24},{12,28},{16,0},{20,4},{24,8},{28,12},{1,17},{... | collective-permute-start | bytes 3551240 | tf_op jit(solution)/shard_map/ppermute | solution.py:269
  683.8 42.8 %collective-permute-start.69 = (f32[4,3264]{1,0:T(4,128)S(1)}, f32[4,3264]{1,0:T(4,128)S(1)}, u32[]{:S(2)}, u32[]{:S(2)}) collective-permute-start(f32[4,3264]{1,0:T(4,128)S(1)} %fusion.102), channel_id=1, source_target_pairs={{0,8},{4,12},{8,0},{12,4},{16,24},{20,28},{24,16},{28,20},{1,9},{5... | collective-permute-start | bytes 156680 | tf_op jit(solution)/shard_map/ppermute | solution.py:269
  715.4 29.1 %collective-permute-start.80 = (bf16[136,1088]{1,0:T(8,128)(2,1)S(1)}, bf16[136,1088]{1,0:T(8,128)(2,1)}, u32[]{:S(2)}, u32[]{:S(2)}) collective-permute-start(bf16[136,1088]{1,0:T(8,128)(2,1)S(1)} %get-tuple-element.220), channel_id=1, source_target_pairs={{0,3},{1,0},{2,1},{3,2},{4,7},{5,4},{6,5},{7,6},{8,11},{9,8},{10,9... | collective-permute-start | bytes 887816 | tf_op jit(solution)/shard_map/ppermute | solution.py:265
  (169 other events, 2200.1 us)

commit v3 on v2

v3 whole, which is shorter than its diff:
```python
from functools import partial

import jax
import jax.numpy as jnp
from jax import lax
from jax.experimental import pallas as pl
from jax.experimental.pallas import tpu as pltpu
from jax.sharding import PartitionSpec as P

HEAD = 64
LANES = 128
EPSILON = 1e-05
NEG_FILL = -1e30
F32 = jnp.float32
BF16 = jnp.bfloat16
SCALE = HEAD ** (-0.5)
VMEM_BYTES = 40 * 1024 * 1024
ATTEND_BYTES = 20 * 1024 * 1024


def tile_length(span_len):
    return 256 if span_len % 256 == 0 else span_len


def keep_of(tile_base, tile_len, low_row, own_base):
    span_len = low_row.shape[1]
    key_pos = tile_base + lax.broadcasted_iota(jnp.int32, (tile_len, span_len), 0)
    query_pos = own_base + lax.broadcasted_iota(jnp.int32, (tile_len, span_len), 1)
    return (key_pos >= low_row) & (key_pos <= query_pos)


def tile_loops(bounds_ref, tile, base_tile, count, own_tile):
    low_tile = bounds_ref[0]
    mid_tile = bounds_ref[1]
    clear_end = min(max(own_tile - base_tile, 0), count)
    begin = jnp.clip(low_tile - base_tile, 0, clear_end)
    middle = jnp.clip(mid_tile - base_tile, begin, clear_end)
    lax.fori_loop(begin, middle, lambda t, c: tile(t, True), None)
    lax.fori_loop(middle, clear_end, lambda t, c: tile(t, False), None)
    for t in range(clear_end, count):
        tile(t, True)
    return begin


def inside(x, axis, valid):
    where = lax.broadcasted_iota(jnp.int32, x.shape, axis)
    return jnp.where(where < valid, x, jnp.zeros((), x.dtype))


def halves(x, axis):
    where = lax.broadcasted_iota(jnp.int32, x.shape, axis)
    zero = jnp.zeros((), x.dtype)
    return jnp.where(where < HEAD, x, zero), jnp.where(where >= HEAD, x, zero)


def forward_kernel(first, pairs, last_half, lengths, bounds_ref, qt_ref, low_ref, *refs):
    blocks = len(lengths)
    k_refs, v_refs = refs[:blocks], refs[blocks : 2 * blocks]
    ot_ref, lse_ref, max_ref, sum_ref, acc_ref = refs[-5:]
    span_len = qt_ref.shape[1]
    tile_len = tile_length(span_len)
    own_base = sum(lengths) - span_len
    last = pl.program_id(0) + first == pairs - 1
    valid = jnp.where(last, last_half, LANES)
    heads = halves(inside((qt_ref[...].astype(F32) * SCALE).astype(BF16), 0, valid), 0)
    max_ref[...] = jnp.full_like(max_ref, NEG_FILL)
    sum_ref[...] = jnp.zeros_like(sum_ref)
    acc_ref[...] = jnp.zeros_like(acc_ref)
    base = 0
    for k_ref, v_ref, length in zip(k_refs, v_refs, lengths):

        def tile(t, masked, k_ref=k_ref, v_ref=v_ref, base=base):
            rows = pl.ds(pl.multiple_of(t * tile_len, tile_len), tile_len)
            k_tile = inside(k_ref[rows, :], 1, valid)
            v_t = v_ref[rows, :].T
            if masked:
                keep = keep_of(base + t * tile_len, tile_len, low_ref[...], own_base)

            def one(head):
                scores = jnp.dot(k_tile, heads[head], preferred_element_type=F32)
                if masked:
                    scores = jnp.where(keep, scores, NEG_FILL)
                old_max = max_ref[head]
                new_max = jnp.maximum(old_max, jnp.max(scores, axis=0, keepdims=True))
                shrink = jnp.exp(old_max - new_max)
                probs = jnp.exp(scores - new_max)
                max_ref[head] = new_max
                sum_ref[head] = sum_ref[head] * shrink + jnp.sum(probs, axis=0, keepdims=True)
                acc_ref[head] = acc_ref[head] * shrink + jnp.dot(
                    v_t[head * HEAD : (head + 1) * HEAD], probs.astype(BF16), preferred_element_type=F32
                )

            @pl.when(valid > HEAD)
            def _():
                one(0)
                one(1)

            @pl.when(valid <= HEAD)
            def _():
                one(0)

        tile_loops(bounds_ref, tile, base // tile_len, length // tile_len, own_base // tile_len)
        base += length
    safe = jnp.where(sum_ref[...] > 0, sum_ref[...], 1.0)
    ot_ref[...] = jnp.concatenate([acc_ref[0] / safe[0], acc_ref[1] / safe[1]], axis=0).astype(BF16)
    lse_ref[0] = jnp.concatenate([max_ref[0] + jnp.log(safe[0]), max_ref[1] + jnp.log(safe[1])], axis=0)


def backward_kernel(
    base, final, pairs, last_half, own_base, bounds_ref, q_ref, qt_ref, g_ref, gt_ref, ot_ref, lse_ref, low_ref, k_ref, v_ref, *refs
):
    first = base == 0
    acc_in = None if first else refs[0]
    acc_out, dk_ref, dv_ref, sums_ref, acc_ref = refs[-5:]
    span_len = q_ref.shape[0]
    tile_len = tile_length(span_len)
    last = pl.program_id(0) == pairs - 1
    valid = jnp.where(last, last_half, LANES)
    q_heads = halves(inside((q_ref[...].astype(F32) * SCALE).astype(BF16), 1, valid), 1)
    qt_heads = halves(inside((qt_ref[...].astype(F32) * SCALE).astype(BF16), 0, valid), 0)
    g_heads = halves(inside(g_ref[...], 1, valid), 1)
    gt_now = inside(gt_ref[...], 0, valid)
    gt_heads = halves(gt_now, 0)
    prod = gt_now.astype(F32) * inside(ot_ref[...], 0, valid).astype(F32)
    deltas = [jnp.sum(prod[h * HEAD : (h + 1) * HEAD], axis=0, keepdims=True) for h in range(2)]
    if first:
        acc_ref[...] = jnp.zeros_like(acc_ref)
    else:
        acc_ref[...] = acc_in[0]

    def tile(t, masked):
        rows = pl.ds(pl.multiple_of(t * tile_len, tile_len), tile_len)
        k_tile = inside(k_ref[rows, :], 1, valid)
        v_tile = inside(v_ref[rows, :], 1, valid)
        k_t = k_tile.T
        if masked:
            keep = keep_of(base + t * tile_len, tile_len, low_ref[...], own_base)

        def one(head):
            scores = jnp.dot(k_tile, qt_heads[head], preferred_element_type=F32)
            probs = jnp.exp(scores - lse_ref[0, head : head + 1])
            if masked:
                probs = jnp.where(keep, probs, 0.0)
            dprobs = jnp.dot(v_tile, gt_heads[head], preferred_element_type=F32)
            dscores = (probs * (dprobs - deltas[head])).astype(BF16)
            dv = jnp.dot(probs.astype(BF16), g_heads[head], preferred_element_type=F32)
            dk = jnp.dot(dscores, q_heads[head], preferred_element_type=F32)
            acc_ref[head] += jnp.dot(k_t[head * HEAD : (head + 1) * HEAD], dscores, preferred_element_type=F32)
            return dk, dv

        def write(dk, dv):
            dk_ref[rows, :] = dk.astype(BF16)
            dv_ref[rows, :] = dv.astype(BF16)

        @pl.when(valid > HEAD)
        def _():
            dk_a, dv_a = one(0)
            dk_b, dv_b = one(1)
            write(dk_a + dk_b, dv_a + dv_b)

        @pl.when(valid <= HEAD)
        def _():
            write(*one(0))

    begin = tile_loops(bounds_ref, tile, base // tile_len, k_ref.shape[0] // tile_len, own_base // tile_len)

    def clear(t, carry):
        rows = pl.ds(pl.multiple_of(t * tile_len, tile_len), tile_len)
        dk_ref[rows, :] = jnp.zeros((tile_len, LANES), BF16)
        dv_ref[rows, :] = jnp.zeros((tile_len, LANES), BF16)
        return carry

    lax.fori_loop(0, begin, clear, None)
    dv_sum = jnp.sum(dv_ref[...].astype(F32), axis=0, keepdims=True)
    if final:
        dq = (jnp.concatenate([acc_ref[0], acc_ref[1]], axis=0).T * SCALE).astype(BF16)
        acc_out[...] = dq
        sums_ref[...] = jnp.concatenate([dv_sum, jnp.sum(dq.astype(F32), axis=0, keepdims=True)], axis=0)
    else:
        acc_out[0] = acc_ref[...]
        sums_ref[...] = jnp.concatenate([dv_sum, jnp.zeros_like(dv_sum)], axis=0)


def attend_parts(pairs, number):
    size = pl.cdiv(pairs, number)
    return [(first, min(size, pairs - first)) for first in range(0, pairs, size)]


def attend_forward(part, queries_t, keys, values, low_row, bounds, earlier):
    first, number = part
    width, span_len = queries_t.shape
    pairs = pl.cdiv(width, LANES)
    lengths = tuple(block.shape[0] for block in keys)
    turned = pl.BlockSpec((LANES, span_len), lambda p, b: (p + first, 0))
    low_spec = pl.BlockSpec((1, span_len), lambda p, b: (0, 0))
    key_specs = [pl.BlockSpec((length, LANES), lambda p, b: (0, p + first)) for length in lengths]
    lse_spec = pl.BlockSpec((1, 2, span_len), lambda p, b: (p + first, 0, 0))
    inputs = (bounds, queries_t, low_row) + tuple(keys) + tuple(values)
    earlier = () if earlier is None else tuple(earlier)
    return pl.pallas_call(
        partial(forward_kernel, first, pairs, width - (pairs - 1) * LANES, lengths),
        out_shape=(
            jax.ShapeDtypeStruct((width, span_len), BF16),
            jax.ShapeDtypeStruct((pairs, 2, span_len), F32),
        ),
        grid_spec=pltpu.PrefetchScalarGridSpec(
            num_scalar_prefetch=1,
            grid=(number,),
            in_specs=[turned, low_spec] + key_specs + key_specs + [pl.BlockSpec(memory_space=pl.ANY)] * len(earlier),
            out_specs=(turned, lse_spec),
            scratch_shapes=[
                pltpu.VMEM((2, 1, span_len), F32),
                pltpu.VMEM((2, 1, span_len), F32),
                pltpu.VMEM((2, HEAD, span_len), F32),
            ],
        ),
        input_output_aliases={len(inputs) + i: i for i in range(len(earlier))},
        cost_estimate=pl.CostEstimate(
            flops=40 * span_len * sum(lengths) * number * LANES, bytes_accessed=span_len * width, transcendentals=0
        ),
        compiler_params=pltpu.CompilerParams(vmem_limit_bytes=ATTEND_BYTES),
        name="attend_forward",
    )(*inputs, *earlier)


def attend_backward(base, final, key_len, queries, queries_t, grad, grad_t, attended_t, lse, low_row, bounds, k, v, acc):
    span_len, width = queries.shape
    pairs = pl.cdiv(width, LANES)
    plain = pl.BlockSpec((span_len, LANES), lambda p, b: (0, p))
    turned = pl.BlockSpec((LANES, span_len), lambda p, b: (p, 0))
    low_spec = pl.BlockSpec((1, span_len), lambda p, b: (0, 0))
    key_spec = pl.BlockSpec((k.shape[0], LANES), lambda p, b: (0, p))
    lse_spec = pl.BlockSpec((1, 2, span_len), lambda p, b: (p, 0, 0))
    acc_spec = pl.BlockSpec((1, 2, HEAD, span_len), lambda p, b: (p, 0, 0, 0))
    sums_spec = pl.BlockSpec((2, LANES), lambda p, b: (0, p))
    inputs = (bounds, queries, queries_t, grad, grad_t, attended_t, lse, low_row, k, v)
    specs = [plain, turned, plain, turned, turned, lse_spec, low_spec, key_spec, key_spec]
    if acc is not None:
        inputs += (acc,)
        specs.append(acc_spec)
    sums = jax.ShapeDtypeStruct((span_len, width), BF16) if final else jax.ShapeDtypeStruct((pairs, 2, HEAD, span_len), F32)
    return pl.pallas_call(
        partial(backward_kernel, base, final, pairs, width - (pairs - 1) * LANES, key_len - span_len),
        out_shape=(
            sums,
            jax.ShapeDtypeStruct(k.shape, BF16),
            jax.ShapeDtypeStruct(k.shape, BF16),
            jax.ShapeDtypeStruct((2, width), F32),
        ),
        grid_spec=pltpu.PrefetchScalarGridSpec(
            num_scalar_prefetch=1,
            grid=(pairs,),
            in_specs=specs,
            out_specs=(plain if final else acc_spec, key_spec, key_spec, sums_spec),
            scratch_shapes=[pltpu.VMEM((2, HEAD, span_len), F32)],
        ),
        cost_estimate=pl.CostEstimate(
            flops=40 * span_len * k.shape[0] * width, bytes_accessed=span_len * width, transcendentals=0
        ),
        compiler_params=pltpu.CompilerParams(vmem_limit_bytes=ATTEND_BYTES),
        name="attend_backward",
    )(*inputs)


def along_group(x, step, count, wrap):
    pairs = [(i, (i + step) % count) for i in range(count) if wrap or 0 <= i + step < count]
    return lax.ppermute(x, "group", pairs)


def hop(rows, step, count):
    bands = rows.reshape(-1, 64, rows.shape[1])
    return along_group(bands, step, count, False).reshape(rows.shape)


def flip(x, bit, count):
    return lax.ppermute(x, "dp", [(i, i ^ bit) for i in range(count)])


CORE, ACROSS, DOWN = 1, 2, 4


def pick(x, index, axis=0):
    return lax.dynamic_index_in_dim(x, index, axis, keepdims=False)


def put(x, part, index):
    start = tuple(index) + (0,) * (x.ndim - len(index))
    part = part.reshape((1,) * len(index) + part.shape)
    return lax.dynamic_update_slice(x, part, start)


def matmul_t(left, right):
    return lax.dot_general(left, right, (((1,), (1,)), ((), ())), preferred_element_type=F32)


def split_rows(core, total_ref, keep_ref, send_ref):
    rows = keep_ref.shape[2]

    def give(first, second):
        for i in range(keep_ref.shape[1]):
            first[0, i] = total_ref[2 * i * rows : (2 * i + 1) * rows, :].astype(BF16)
            second[0, i] = total_ref[(2 * i + 1) * rows : (2 * i + 2) * rows, :].astype(BF16)

    pl.when(core == 0)(lambda: give(keep_ref, send_ref))
    pl.when(core != 0)(lambda: give(send_ref, keep_ref))


def outer_into(left_t, right, total_ref):
    band = total_ref.shape[0] // 4
    for i in range(4):
        total_ref[i * band : (i + 1) * band, :] = jnp.dot(
            left_t[i * band : (i + 1) * band, :], right, preferred_element_type=F32
        )


def feed_kernel(core_ref, x_ref, w_ref, b_ref, g_ref, hidden_ref, slope_ref, keep_ref, send_ref, xt_ref, total_ref):
    @pl.when(pl.program_id(0) == 0)
    def _():
        xt_ref[...] = x_ref[...].T

    span_len = x_ref.shape[0]
    band = span_len // 4
    for i in range(4):
        rows = slice(i * band, (i + 1) * band)
        u = jnp.dot(x_ref[rows, :], w_ref[0], preferred_element_type=F32) + b_ref[0]
        inner = 0.7978845608028654 * (u + 0.044715 * (u * u * u))
        t = jnp.tanh(inner)
        hidden_ref[0, rows, :] = (0.5 * u * (1.0 + t)).astype(BF16)
        slope = 0.5 * (1.0 + t) + 0.5 * u * (1.0 - t * t) * (0.7978845608028654 * (1.0 + 0.134145 * (u * u)))
        slope_ref[0, rows, :] = slope.astype(BF16)
    outer_into(hidden_ref[0].T, g_ref[...], total_ref)
    split_rows(core_ref[0], total_ref, keep_ref, send_ref)


def feed_back_kernel(core_ref, g_ref, wp_ref, slope_ref, xt_ref, wf_ref, keep_ref, send_ref, xg_ref, bg_ref, total_ref):
    grad = matmul_t(g_ref[...], wp_ref[0]) * slope_ref[0].astype(F32)
    low = grad.astype(BF16)
    bg_ref[0] = jnp.sum(low.astype(F32), axis=0, keepdims=True)
    outer_into(xt_ref[...], low, total_ref)
    split_rows(core_ref[0], total_ref, keep_ref, send_ref)
    part = matmul_t(low, wf_ref[0])

    @pl.when(pl.program_id(0) == 0)
    def _():
        xg_ref[...] = part

    @pl.when(pl.program_id(0) != 0)
    def _():
        xg_ref[...] += part


def project_kernel(h_ref, w_ref, r_ref, b_ref, o_ref, total_ref):
    part = jnp.dot(h_ref[0], w_ref[0], preferred_element_type=F32)
    step = pl.program_id(0)

    @pl.when(step == 0)
    def _():
        total_ref[...] = part + (r_ref[...] + b_ref[...])

    @pl.when(step != 0)
    def _():
        total_ref[...] += part

    @pl.when(step == pl.num_programs(0) - 1)
    def _():
        o_ref[...] = total_ref[...].T


def chunk_spec(*shape):
    return pl.BlockSpec((1,) + shape, lambda j, *s: (j,) + (0,) * len(shape))


def whole_spec(*shape):
    return pl.BlockSpec(shape, lambda j, *s: (0,) * len(shape))


def feed_call(kernel, name, scalars, inputs, in_specs, outs, out_specs, scratch, chunks):
    return pl.pallas_call(
        kernel,
        out_shape=outs,
        grid_spec=pltpu.PrefetchScalarGridSpec(
            num_scalar_prefetch=len(scalars),
            grid=(chunks,),
            in_specs=in_specs,
            out_specs=out_specs,
            scratch_shapes=scratch,
        ),
        cost_estimate=pl.CostEstimate(flops=20 * inputs[0].size * inputs[1].shape[-1], bytes_accessed=1024, transcendentals=0),
        compiler_params=pltpu.CompilerParams(vmem_limit_bytes=56 * 1024 * 1024),
        name=name,
    )(*scalars, *inputs)


def feed(core, x, full_fc, bias, grad):
    span_len, width = x.shape
    chunks = full_fc.shape[0]
    rows = width // 8
    part = jax.ShapeDtypeStruct((chunks, 4, rows, width), BF16)
    tall = jax.ShapeDtypeStruct((chunks, span_len, width), BF16)
    return feed_call(
        feed_kernel,
        "feed",
        (core,),
        (x, full_fc, bias, grad),
        [whole_spec(span_len, width), chunk_spec(width, width), chunk_spec(1, width), whole_spec(span_len, width)],
        (tall, tall, part, part, jax.ShapeDtypeStruct((width, span_len), BF16)),
        (
            chunk_spec(span_len, width),
            chunk_spec(span_len, width),
            chunk_spec(4, rows, width),
            chunk_spec(4, rows, width),
            whole_spec(width, span_len),
        ),
        [pltpu.VMEM((width, width), F32)],
        chunks,
    )


def feed_back(core, grad, full_proj, slope, x_t, full_fc):
    span_len, width = grad.shape
    chunks = full_fc.shape[0]
    rows = width // 8
    part = jax.ShapeDtypeStruct((chunks, 4, rows, width), BF16)
    return feed_call(
        feed_back_kernel,
        "feed_back",
        (core,),
        (grad, full_proj, slope, x_t, full_fc),
        [
            whole_spec(span_len, width),
            chunk_spec(width, width),
            chunk_spec(span_len, width),
            whole_spec(width, span_len),
            chunk_spec(width, width),
        ],
        (part, part, jax.ShapeDtypeStruct((span_len, width), F32), jax.ShapeDtypeStruct((chunks, 1, width), F32)),
        (chunk_spec(4, rows, width), chunk_spec(4, rows, width), whole_spec(span_len, width), chunk_spec(1, width)),
        [pltpu.VMEM((width, width), F32)],
        chunks,
    )


def project(hidden, full_proj, resid, bias):
    chunks, span_len, width = hidden.shape
    return feed_call(
        project_kernel,
        "project",
        (),
        (hidden, full_proj, resid, bias),
        [chunk_spec(span_len, width), chunk_spec(width, width), whole_spec(span_len, width), whole_spec(1, width)],
        jax.ShapeDtypeStruct((width, span_len), F32),
        whole_spec(width, span_len),
        [pltpu.VMEM((span_len, width), F32)],
        chunks,
    )


def after(x, *before):
    return lax.optimization_barrier((x,) + before)[0]


def plane_share_near(mine, count):
    return flip(mine, ACROSS, count), flip(mine, DOWN, count)


def plane_share_far(from_x, from_y, count):
    cut = cut_of(from_x)
    return flip(from_x[:, :, :cut], DOWN, count), flip(from_y[:, :, cut:], ACROSS, count)


def cut_of(part):
    return part.shape[2] // 2 // LANES * LANES


def assemble_kernel(groups, kind, here_ref, own_ref, *refs):
    sources, outs, sems = refs[:10], refs[10:-1], refs[-1]
    chip, core, z = here_ref[0], here_ref[1], here_ref[2]
    cut = sources[3].shape[2]

    def place(index, plane, half):
        if kind == "plane":
            return outs[0].at[plane, index, half]
        if kind == "chip":
            return outs[0].at[index, plane, half]
        return outs[index].at[plane, half]

    def move(index, k, wait):
        n = 1 + k * 2 * (groups - 1)
        for side in range(2):
            half = core if side == 0 else 1 - core
            for step in range(groups - 1):
                target = place(index, lax.rem(z - step - 1 + groups, groups), half)
                if k < 3:
                    pairs = [(sources[side * 5 + k].at[step], target)]
                else:
                    pairs = [
                        (sources[side * 5 + 3].at[step], target.at[:, :cut]),
                        (sources[side * 5 + 4].at[step], target.at[:, cut:]),
                    ]
                for src, dst in pairs:
                    copy = pltpu.make_async_copy(src, dst, sems.at[n])
                    copy.wait() if wait else copy.start()
                    n += 1

    if kind == "plane":
        owns = [(own_ref, outs[0].at[z])]
    elif kind == "chip":
        owns = [(own_ref, outs[0].at[:, z])]
    else:
        owns = [(own_ref.at[m], outs[m].at[z]) for m in range(4)]
    last = sems.shape[0] - len(owns)
    owns = [pltpu.make_async_copy(src, dst, sems.at[last + i]) for i, (src, dst) in enumerate(owns)]
    for copy in owns:
        copy.start()
    for wait in (False, True):
        for k in range(4):
            if kind == "apart":
                for m in range(4):
                    pl.when(chip == m ^ k)(partial(move, m, k, wait))
            else:
                move(chip ^ k, k, wait)
    for copy in owns:
        copy.wait()


def assemble(own, sources, here, groups, kind):
    rows, cols = own.shape[2:]
    if kind == "apart":
        shapes = [(groups, 2, rows, cols)] * 4
    else:
        shapes = [(groups, 4, 2, rows, cols) if kind == "plane" else (4, groups, 2, rows, cols)]
    return pl.pallas_call(
        partial(assemble_kernel, groups, kind),
        out_shape=[jax.ShapeDtypeStruct(shape, own.dtype) for shape in shapes],
        grid_spec=pltpu.PrefetchScalarGridSpec(
            num_scalar_prefetch=1,
            grid=(1,),
            in_specs=[pl.BlockSpec(memory_space=pl.ANY)] * 11,
            out_specs=[pl.BlockSpec(shape, lambda i, h, n=len(shape): (0,) * n) for shape in shapes],
            scratch_shapes=[pltpu.SemaphoreType.DMA((1 + 10 * (groups - 1) + 4,))],
        ),
        compiler_params=pltpu.CompilerParams(vmem_limit_bytes=VMEM_BYTES),
        cost_estimate=pl.CostEstimate(flops=0, bytes_accessed=own.size, transcendentals=0),
        name="assemble",
    )(jnp.stack(here).astype(jnp.int32), own, *sources)


def from_planes(piece, groups):
    return jnp.stack([along_group(piece, step, groups, True) for step in range(1, groups)])


def chip_sum(keep, send, count, *during):
    got = flip(send, CORE, count)
    got = after(got, *during) if during else got
    return (keep.astype(F32) + got.astype(F32)).astype(BF16)


def joined(core, keep, send):
    first, second = jnp.where(core == 0, keep, send), jnp.where(core == 0, send, keep)
    both = jnp.stack([first, second], axis=2)
    return both.reshape(both.shape[0], -1, both.shape[-1])


def plane_first_step(half, chip, count, axis):
    to_diag = pick(half, chip ^ 3, axis)
    cut = to_diag.shape[0] // 2
    return flip(to_diag[:cut], ACROSS, count), flip(to_diag[cut:], DOWN, count)


def plane_second_step(half, via, chip, count, axis):
    to_own, to_x, to_y = (pick(half, chip ^ k, axis) for k in range(3))
    cut = to_own.shape[0] // 2
    from_y = flip(jnp.concatenate([to_y[:cut] + via[0], to_y[cut:]]), DOWN, count)
    from_x = flip(jnp.concatenate([to_x[:cut], to_x[cut:] + via[1]]), ACROSS, count)
    return to_own, from_x, from_y


def second_sum(to_own, from_x, from_y):
    return (to_own.astype(F32) + from_x.astype(F32) + from_y.astype(F32)).astype(BF16)


def line_parts(mine, z, groups):
    sent = [(pick(mine, lax.rem(z + step, groups)), step) for step in range(1, groups)]
    return [pick(mine, z)] + [along_group(part, step, groups, True) for part, step in sent]


def parts_sum(parts):
    total = parts[0].astype(F32)
    for part in parts[1:]:
        total = total + part.astype(F32)
    return total


def line_sum(mine, z, groups):
    return parts_sum(line_parts(mine, z, groups))


def shares_of(mine, near, far):
    return jnp.concatenate((mine,) + near + (jnp.concatenate(far, axis=2),))


def in_vmem():
    return pl.BlockSpec(memory_space=pltpu.VMEM)


def norm_back_kernel(parts, turned, values_ref, gain_ref, base_ref, *refs):
    grads, (out_ref, low_ref, gain_sum_ref, shift_sum_ref, low_sum_ref) = refs[:parts], refs[parts:]
    values = values_ref[...].astype(F32)
    grad = grads[0][...].astype(F32)
    for other in grads[1:]:
        grad = grad + other[...].astype(F32)
    center = values - jnp.mean(values, axis=-1, keepdims=True)
    scale = lax.rsqrt(jnp.mean(center * center, axis=-1, keepdims=True) + EPSILON)
    unit = center * scale
    inner = grad * gain_ref[...]
    back = scale * (
        inner - jnp.mean(inner, axis=-1, keepdims=True) - unit * jnp.mean(inner * unit, axis=-1, keepdims=True)
    )
    out = base_ref[...].astype(F32) + back
    out_ref[...] = out.T if turned else out
    low = out.astype(BF16)
    low_ref[...] = low
    sums = (
        jnp.sum(grad * unit, axis=0, keepdims=True),
        jnp.sum(grad, axis=0, keepdims=True),
        jnp.sum(low.astype(F32), axis=0, keepdims=True),
    )
    begun = pl.program_id(0) != 0
    for ref, part in zip((gain_sum_ref, shift_sum_ref, low_sum_ref), sums):
        ref[...] = jnp.where(begun, ref[...], 0.0) + part


def norm_back(values, gain, base, *grads, turned=False):
    span_len, width = values.shape
    band = min(span_len, LANES)
    columns = pl.BlockSpec((width, band), lambda i: (0, i))
    rows = pl.BlockSpec((band, width), lambda i: (i, 0))
    line = pl.BlockSpec((1, width), lambda i: (0, 0))
    sums = jax.ShapeDtypeStruct((1, width), F32)
    out, low, gain_sum, shift_sum, low_sum = pl.pallas_call(
        partial(norm_back_kernel, len(grads), turned),
        out_shape=(
            jax.ShapeDtypeStruct((width, span_len) if turned else (span_len, width), F32),
            jax.ShapeDtypeStruct((span_len, width), BF16),
            sums,
            sums,
            sums,
        ),
        grid=(span_len // band,),
        in_specs=[rows, line, rows] + [rows] * len(grads),
        out_specs=(columns if turned else rows, rows, line, line, line),
        cost_estimate=pl.CostEstimate(flops=0, bytes_accessed=1024, transcendentals=0),
        compiler_params=pltpu.CompilerParams(vmem_limit_bytes=VMEM_BYTES),
        name="norm_back",
    )(values, gain[None], base, *grads)
    return out, low, gain_sum, shift_sum, low_sum


def key_back_kernel(dk_ref, dv_ref, wk_ref, wv_ref, *refs):
    out_ref = refs[-1]
    total = matmul_t(dk_ref[...], wk_ref[...]) + matmul_t(dv_ref[...], wv_ref[...])
    for other in refs[:-1]:
        total = total + other[...].astype(F32)
    out_ref[...] = total.astype(out_ref.dtype)


def key_back(dk, dv, full_k, full_v, moving, kind):
    more = () if moving is None else (moving,)
    return pl.pallas_call(
        key_back_kernel,
        out_shape=jax.ShapeDtypeStruct(dk.shape, kind),
        in_specs=[in_vmem()] * (4 + len(more)),
        out_specs=in_vmem(),
        cost_estimate=pl.CostEstimate(flops=0, bytes_accessed=1024, transcendentals=0),
        compiler_params=pltpu.CompilerParams(vmem_limit_bytes=VMEM_BYTES),
        name="key_back",
    )(dk, dv, full_k, full_v, *more)


def attn_grads_kernel(blocks, core_ref, *refs):
    normed, dks, dvs = refs[:blocks], refs[blocks : 2 * blocks], refs[2 * blocks : 3 * blocks]
    dq_ref, ot_ref, low_ref, keep_ref, send_ref, total_ref, turned_ref = refs[3 * blocks :]
    span_len = dq_ref.shape[0]
    step = pl.program_id(0)
    width = total_ref.shape[0]
    band = width // 4

    def sums(rights):
        for i in range(4):
            rows = slice(i * band, (i + 1) * band)
            total = None
            for b, right in enumerate(rights):
                if right is None:
                    continue
                part = jnp.dot(turned_ref[b, rows, :], right, preferred_element_type=F32)
                total = part if total is None else total + part
            total_ref[rows, :] = total

    @pl.when(step == 0)
    def _():
        begin = 0
        for ref in normed:
            for at in range(0, ref.shape[0], span_len):
                turned_ref[begin // span_len] = ref[at : at + span_len, :].T
                begin += span_len
        sums([None] * (turned_ref.shape[0] - 1) + [dq_ref[...]])

    def pieces(group):
        return [ref[at : at + span_len, :] for ref in group for at in range(0, ref.shape[0], span_len)]

    pl.when(step == 1)(lambda: sums(pieces(dks)))
    pl.when(step == 2)(lambda: sums(pieces(dvs)))

    @pl.when(step == 3)
    def _():
        outer_into(ot_ref[...], low_ref[...], total_ref)

    split_rows(core_ref[0], total_ref, keep_ref, send_ref)


def attn_grads(core, normed, dks, dvs, dq, attended_t, low):
    span_len, width = dq.shape
    rows = width // 8
    key_len = sum(block.shape[0] for block in normed)
    part = jax.ShapeDtypeStruct((4, 4, rows, width), BF16)
    inputs = (*normed, *dks, *dvs, dq, attended_t, low)
    return pl.pallas_call(
        partial(attn_grads_kernel, len(normed)),
        out_shape=(part, part),
        grid_spec=pltpu.PrefetchScalarGridSpec(
            num_scalar_prefetch=1,
            grid=(4,),
            in_specs=[in_vmem()] * len(inputs),
            out_specs=(chunk_spec(4, rows, width), chunk_spec(4, rows, width)),
            scratch_shapes=[
                pltpu.VMEM((width, width), F32),
                pltpu.VMEM((key_len // span_len, width, span_len), BF16),
            ],
        ),
        cost_estimate=pl.CostEstimate(flops=20 * span_len * width * width, bytes_accessed=1024, transcendentals=0),
        compiler_params=pltpu.CompilerParams(vmem_limit_bytes=56 * 1024 * 1024),
        name="attn_grads",
    )(core, *inputs)


def give_out_kernel(kind, here_ref, mine_ref, other_ref, *outs):
    chip, core = here_ref[0], here_ref[1]
    rows, cols = mine_ref.shape[1:]
    for side, ref in enumerate((mine_ref, other_ref)):
        half = core if side == 0 else 1 - core
        for k in range(4):
            piece = ref[k].astype(F32)
            if kind == "plane":
                at = pl.ds(pl.multiple_of(((chip ^ k) * 2 + half) * rows, 8), rows)
                outs[0][at, :] = piece
                continue
            at = pl.ds(pl.multiple_of(half * rows, 8), rows)
            for m in range(4):

                @pl.when(chip == m ^ k)
                def _(m=m, at=at, piece=piece):
                    if kind == "apart":
                        outs[m][at, :] = piece
                    else:
                        outs[0][at, m * cols : (m + 1) * cols] = piece


def give_out(shares, other, here, kind):
    rows, cols = shares.shape[1:]
    shapes = {"apart": [(2 * rows, cols)] * 4, "chip": [(2 * rows, 4 * cols)], "plane": [(8 * rows, cols)]}[kind]
    return pl.pallas_call(
        partial(give_out_kernel, kind),
        out_shape=[jax.ShapeDtypeStruct(shape, F32) for shape in shapes],
        grid_spec=pltpu.PrefetchScalarGridSpec(
            num_scalar_prefetch=1,
            grid=(1,),
            in_specs=[whole_spec(4, rows, cols)] * 2,
            out_specs=[whole_spec(*shape) for shape in shapes],
        ),
        cost_estimate=pl.CostEstimate(flops=0, bytes_accessed=1024, transcendentals=0),
        compiler_params=pltpu.CompilerParams(vmem_limit_bytes=VMEM_BYTES),
        name="give_out",
    )(jnp.stack(here).astype(jnp.int32), shares, other)


def mean_spread(values):
    center = values - jnp.mean(values, axis=-1, keepdims=True)
    spread = jnp.mean(center * center, axis=-1, keepdims=True)
    return center, lax.rsqrt(spread + EPSILON)


def layer_norm(values, gain, shift):
    center, scale = mean_spread(values)
    return center * scale * gain + shift


def layer_norm_back(values, gain, grad):
    center, scale = mean_spread(values)
    unit = center * scale
    inner = grad * gain
    back = scale * (
        inner
        - jnp.mean(inner, axis=-1, keepdims=True)
        - unit * jnp.mean(inner * unit, axis=-1, keepdims=True)
    )
    return back, jnp.sum(grad * unit, axis=0), jnp.sum(grad, axis=0)


def row_sum(values):
    return jnp.sum(values.astype(F32), axis=0)


def matmul(left, right):
    return jnp.dot(left, right, preferred_element_type=F32)


def weight_grad(left, right):
    return jnp.einsum("ra,rb->ab", left, right, preferred_element_type=F32).astype(BF16)


def back_through(grad_rows, weight):
    return jnp.einsum("rb,ab->ra", grad_rows, weight, preferred_element_type=F32)


def on_device(
    count,
    groups,
    tokens,
    segments,
    out_grad,
    norm1_gain,
    norm1_bias,
    w_query,
    query_bias,
    w_key,
    w_value,
    value_bias,
    w_out,
    out_bias,
    norm2_gain,
    norm2_bias,
    w_fc,
    fc_bias,
    w_proj,
    proj_bias,
):
    _, span_len, width = tokens.shape
    shard = width // groups
    half = shard // 2
    chunks = w_fc.shape[1] // width
    key_len = segments.shape[1]
    z = lax.axis_index("group")
    place = lax.axis_index("dp")
    fast = count == 8 and groups == 4 and chunks == 4
    chip, core = place // 2, lax.rem(place, 2)
    here = (chip, core, z)
    forward_parts = attend_parts(pl.cdiv(width, LANES), 3)

    small = jnp.concatenate(
        [norm1_gain, norm1_bias, query_bias, value_bias, out_bias, norm2_gain, norm2_bias, proj_bias, fc_bias]
    )
    small_rel = jnp.stack([small] + [along_group(small, step, groups, True) for step in range(1, groups)])
    small_all = jnp.take(small_rel, lax.rem(z - jnp.arange(groups) + groups, groups), axis=0)
    vectors = small_all[:, : 8 * shard].reshape(groups, 8, shard).transpose(1, 0, 2).reshape(8, width)
    gain_one, shift_one, bias_q, bias_v, bias_o, gain_two, shift_two, bias_p = vectors.astype(F32)
    bias_fc = small_all[:, 8 * shard :].astype(F32).reshape(chunks, 1, width)

    mine = tokens[0]
    inputs = mine.astype(F32)
    normed_one = layer_norm(inputs, gain_one, shift_one).astype(BF16)
    own_base = key_len - span_len
    if fast:
        attn_own = jnp.stack([w_query, w_key, w_value, w_out]).reshape(4, 2, half, width)
        attn_ring = from_planes(pick(pick(attn_own, chip), core), groups)
        attn_near = plane_share_near(attn_ring, count)
        hops = [mine, hop(after(mine, attn_ring, small_rel), 1, groups)]
        attn_three = (attn_ring,) + attn_near
        attn_far = plane_share_far(*attn_near, count)
        attn_other = tuple(flip(after(part, *attn_near), CORE, count) for part in attn_three)
        attn_other += tuple(flip(after(part, hops[1]), CORE, count) for part in attn_far)
        hops.append(hop(hops[1], 1, groups))
        attn = assemble(attn_own, attn_three + attn_far + attn_other, here, groups, "apart")
        full_q, full_k, full_v, full_o = (part.reshape(width, width) for part in attn)
        normed_one, hops[2] = lax.optimization_barrier((normed_one, hops[2]))
        hops.append(hop(hops[2], 1, groups))
    else:
        gather = partial(lax.all_gather, axis_name="group", axis=0, tiled=True)
        full_q, full_k, full_v, full_o = (gather(w) for w in (w_query, w_key, w_value, w_out))
        full_fc = gather(w_fc).reshape(width, chunks, width).transpose(1, 0, 2)
        full_proj = gather(w_proj).reshape(chunks, width, width)
    queries_t = (jnp.einsum("td,df->ft", normed_one, full_q, preferred_element_type=F32) + bias_q[:, None]).astype(BF16)
    queries = (matmul(normed_one, full_q) + bias_q).astype(BF16)

    def keys_of(normed):
        return matmul(normed, full_k).astype(BF16), (matmul(normed, full_v) + bias_v).astype(BF16)

    def norm_of(block):
        return layer_norm(block.astype(F32), gain_one, shift_one).astype(BF16)

    if fast:
        own_keys = keys_of(normed_one)
        fc_own = w_fc.reshape(2, half, chunks, width).transpose(2, 0, 1, 3)
        fc_piece = pick(pick(fc_own, chip), core)
        proj_own = w_proj.reshape(4, 2, half, width)
        proj_piece = pick(pick(proj_own, chip), core)
        normed = [normed_one, norm_of(hops[1]), norm_of(hops[2])]
        both = [own_keys] + [keys_of(block) for block in normed[1:]]
        hops[3] = after(hops[3], *both[1], *both[2])
        fc_ring = from_planes(after(fc_piece, hops[3]), groups)
        normed.append(norm_of(hops[3]))
        both.append(keys_of(normed[3]))
        normed, keys, values = normed[::-1], [b[0] for b in both[::-1]], [b[1] for b in both[::-1]]
    else:
        hops = [mine]
        for _ in range(groups - 1):
            hops.append(hop(hops[-1], 1, groups))
        normed = [norm_of(jnp.concatenate(hops[::-1]))]
        both = keys_of(normed[0])
        keys, values = [both[0]], [both[1]]

    seg = segments[0]
    seg_mine = lax.dynamic_slice_in_dim(seg, z * span_len, span_len)
    low_row = jnp.sum((seg[None, :] < seg_mine[:, None]).astype(jnp.int32), axis=1)
    low_row = low_row + (groups - 1 - z) * span_len
    tile_len = tile_length(span_len)
    low_tile = low_row[0] // tile_len
    mid_tile = jnp.clip((low_row[-1] + tile_len - 1) // tile_len, low_tile, own_base // tile_len)
    bounds = jnp.stack([low_tile, mid_tile]).astype(jnp.int32)
    low_row = low_row[None]

    state = None
    for number, part in enumerate(forward_parts):
        row_now = after(low_row, queries) if number == 0 else low_row
        if fast and number == 1:
            fc_near = plane_share_near(after(fc_ring, state[0]), count)
            proj_ring = from_planes(after(proj_piece, fc_ring, state[0]), groups)
            row_now = after(low_row, fc_ring)
        if fast and number == 2:
            fc_three = (fc_ring,) + fc_near
            fc_far = plane_share_far(*(after(part, state[0]) for part in fc_near), count)
            fc_other = tuple(flip(after(part, state[0], *fc_near), CORE, count) for part in fc_three)
            proj_near = plane_share_near(after(proj_ring, state[0], *fc_near), count)
            row_now = after(low_row, proj_ring, *fc_near)
        state = attend_forward(part, queries_t, keys, values, row_now, bounds, state)
    attended_t, lse = state
    if fast:
        fc_other += tuple(flip(after(part, attended_t), CORE, count) for part in fc_far)
        attended_t = after(attended_t, *fc_far)
    resid = inputs + jnp.einsum("ft,fd->td", attended_t, full_o, preferred_element_type=F32) + bias_o
    normed_two = layer_norm(resid, gain_two, shift_two).astype(BF16)
    if fast:
        full_fc = assemble(after(fc_own, normed_two), fc_three + fc_far + fc_other, here, groups, "chip")
        full_fc = full_fc[0].reshape(4, width, width)

    cot = out_grad[0]
    proj_bias_grad = row_sum(cot)
    which = jnp.reshape(core, (1,)).astype(jnp.int32)
    if fast:
        normed_two = after(normed_two, *proj_near)
    hidden, slope, proj_keep, proj_send, normed_two_t = feed(which, normed_two, full_fc, bias_fc, cot)
    cot_now = cot
    if fast:
        proj_three = (proj_ring,) + proj_near
        proj_far = plane_share_far(*(after(part, normed_two) for part in proj_near), count)
        proj_other = tuple(flip(after(part, normed_two, *proj_near), CORE, count) for part in proj_three)
        proj_send, *proj_moved = lax.optimization_barrier((proj_send, *proj_far, *proj_other))
        proj_far, proj_other = tuple(proj_moved[:2]), tuple(proj_moved[2:])
        proj_other += tuple(flip(part, CORE, count) for part in proj_far)
        full_proj = assemble(proj_own, proj_three + proj_far + proj_other, here, groups, "plane")
        full_proj = full_proj[0].reshape(4, width, width)
        proj_chip = chip_sum(proj_keep, proj_send, count)
        cot_now, proj_chip = lax.optimization_barrier((cot, proj_chip))
        proj_via = plane_first_step(proj_chip, chip, count, 1)
    fc_keep, fc_send, normed_two_grad, fc_bias_grad = feed_back(which, cot_now, full_proj, slope, normed_two_t, full_fc)
    if fast:
        normed_two_grad = after(normed_two_grad, *proj_via)
    resid_grad, resid_low, gain_two_grad, shift_two_grad, out_bias_grad = norm_back(
        resid, gain_two, cot, normed_two_grad
    )
    attended_grad = back_through(resid_low, full_o).astype(BF16)
    attended_grad_t = jnp.einsum("td,fd->ft", resid_low, full_o, preferred_element_type=F32).astype(BF16)
    if fast:
        proj_mine = plane_second_step(proj_chip, proj_via, chip, count, 1)
        fc_chip = chip_sum(fc_keep, after(fc_send, *proj_via), count, attended_grad)
        fc_via = plane_first_step(fc_chip, chip, count, 0)
    acc, moving, base = None, None, 0
    dks, dvs, value_bias_grad = [], [], 0.0
    for number, (k, v) in enumerate(zip(keys, values)):
        row_now = low_row
        final = number == len(keys) - 1
        if fast and number == 0:
            row_now = after(low_row, fc_chip)
        if fast and number == 1:
            row_now = after(low_row, sent, proj_mine)
        if fast and number == 2:
            row_now = after(low_row, sent, proj_line)
        if fast and number == 3:
            row_now = after(low_row, sent, fc_mine, *proj_line_near)
        acc, dk, dv, sums = attend_backward(
            base, final, key_len, queries, queries_t, attended_grad, attended_grad_t, attended_t, lse, row_now, bounds, k, v, acc
        )
        base += k.shape[0]
        dks.append(dk)
        dvs.append(dv)
        value_bias_grad = value_bias_grad + sums[:1]
        if final:
            break
        if number > 0:
            moving = after(moving, acc)
        sent = key_back(dk, dv, full_k, full_v, moving, BF16)
        if number == 0:
            sent = after(sent, *fc_via)
        moving = hop(sent, -1, groups)
        if number == 0:
            proj_mine = second_sum(*(after(part, sent) for part in proj_mine))
            proj_lines = line_parts(proj_mine, z, groups)
        if number == 1:
            proj_line = parts_sum([after(part, sent) for part in proj_lines]).astype(BF16)
            proj_line_near = plane_share_near(proj_line[None], count)
            fc_mine = plane_second_step(fc_chip, fc_via, chip, count, 0)
        if number == 2:
            fc_mine = second_sum(*(after(part, sent) for part in fc_mine))
            proj_line_near = tuple(after(part, sent) for part in proj_line_near)
            proj_line_far = plane_share_far(*proj_line_near, count)
    dqueries, query_bias_grad = acc, sums[1:]
    dqueries_now = dqueries
    if fast:
        norm_term = key_back(dk, dv, full_k, full_v, after(moving, acc), F32)
        fc_lines = line_parts(after(fc_mine, norm_term), z, groups)
        proj_line_far = tuple(after(part, norm_term) for part in proj_line_far)
        proj_shares = shares_of(proj_line[None], proj_line_near, proj_line_far)
        proj_others = flip(proj_shares, CORE, count)
        dqueries_now = after(dqueries, norm_term, *proj_line_far)
    else:
        norm_term = back_through(dk, full_k) + back_through(dv, full_v)
        for step in range(groups - 1):
            part = norm_term[step * span_len : (step + 1) * span_len]
            moving = hop((part if moving is None else part + moving.astype(F32)).astype(BF16), -1, groups)
        norm_term = norm_term[own_base:] + moving.astype(F32)
    attn_keep, attn_send = attn_grads(which, normed, dks, dvs, dqueries_now, attended_t, resid_low)
    dqueries_now = dqueries
    if fast:
        fc_line = parts_sum([after(part, attn_send) for part in fc_lines]).astype(BF16)
        attn_chip = chip_sum(attn_keep, after(attn_send, fc_line), count)
        fc_line_near = plane_share_near(fc_line[None], count)
        attn_via = plane_first_step(attn_chip, chip, count, 0)
        fc_line_near = tuple(after(part, attn_chip) for part in fc_line_near)
        fc_line_far = plane_share_far(*fc_line_near, count)
        attn_mine = plane_second_step(attn_chip, attn_via, chip, count, 0)
        fc_line_far = tuple(after(part, *attn_via) for part in fc_line_far)
        fc_shares = shares_of(fc_line[None], fc_line_near, fc_line_far)
        fc_others = flip(fc_shares, CORE, count)
        dqueries_now = after(dqueries, *attn_via)
        (proj_sum,) = give_out(after(proj_shares, *attn_via), proj_others, here, "plane")
    normed_one_grad = back_through(dqueries_now, full_q)
    tokens_grad, _, gain_one_grad, shift_one_grad, _ = norm_back(
        mine, gain_one, resid_grad, normed_one_grad, norm_term, turned=True
    )
    vector_sums = jnp.concatenate(
        [
            gain_one_grad,
            shift_one_grad,
            query_bias_grad,
            value_bias_grad,
            out_bias_grad,
            gain_two_grad,
            shift_two_grad,
            proj_bias_grad[None],
            fc_bias_grad.reshape(chunks, width),
        ]
    )
    vector_sums = parts_sum([vector_sums] + [along_group(vector_sums, step, groups, True) for step in range(1, groups)])
    hidden_now = hidden
    if fast:
        (fc_sum,) = give_out(after(fc_shares, proj_sum), fc_others, here, "chip")
        attn_mine = second_sum(*(after(part, proj_sum, fc_sum, tokens_grad) for part in attn_mine))
        attn_line = line_parts(attn_mine, z, groups)
        vector_sums = vector_sums + flip(vector_sums, CORE, count)
        hidden_now = after(hidden, attn_mine, vector_sums)
    activations = project(hidden_now, full_proj, resid, bias_p[None])
    if fast:
        vector_sums = vector_sums + after(flip(vector_sums, ACROSS, count), activations)
        attn_line = [after(part, vector_sums) for part in attn_line]
        vector_sums = vector_sums + flip(vector_sums, DOWN, count)
    else:
        bit = 1
        while bit < count:
            vector_sums = vector_sums + flip(vector_sums, bit, count)
            bit *= 2
    if fast:
        attn_line = parts_sum([after(part, activations) for part in attn_line]).astype(BF16)
        attn_near = plane_share_near(attn_line[None], count)
        attn_far = plane_share_far(*attn_near, count)
        attn_shares = shares_of(attn_line[None], attn_near, attn_far)
        attn_others = flip(attn_shares, CORE, count)
        q_sum, k_sum, v_sum, out_sum = give_out(attn_shares, attn_others, here, "apart")

    eight = lax.dynamic_slice_in_dim(vector_sums[:8], z * shard, shard, 1)
    fc_bias_sum = lax.dynamic_slice_in_dim(vector_sums[8:].reshape(-1), z * fc_bias.shape[0], fc_bias.shape[0])
    if not fast:

        def whole_sum(part):
            part = lax.psum_scatter(part, "group", scatter_dimension=0, tiled=True)
            return lax.psum(part.astype(F32), "dp")

        proj_sum = whole_sum(joined(core, proj_keep, proj_send).reshape(chunks * width, width))
        fc_sum = whole_sum(joined(core, fc_keep, fc_send).transpose(1, 0, 2).reshape(width, chunks * width))
        attn_whole = joined(core, attn_keep, attn_send)
        q_sum, k_sum, v_sum, out_sum = (whole_sum(attn_whole[m]) for m in range(4))
    return (
        activations.T[None],
        tokens_grad.T[None],
        eight[0],
        eight[1],
        q_sum,
        eight[2],
        k_sum,
        v_sum,
        eight[3],
        out_sum,
        eight[4],
        eight[5],
        eight[6],
        fc_sum,
        fc_bias_sum,
        proj_sum,
        eight[7],
    )


def solution(mesh):
    rows, vec, mat = P("dp", "group", None), P("group"), P("group", None)
    weights = (vec, vec, mat, vec, mat, mat, vec, mat, vec, vec, vec, mat, vec, mat, vec)
    return jax.shard_map(
        partial(on_device, mesh.shape["dp"], mesh.shape["group"]),
        mesh=mesh,
        in_specs=(rows, P("dp", None), rows) + weights,
        out_specs=(rows, rows) + weights,
        check_vma=False,
    )
```

time: 797 us -> 701 us (0.88)
  the two profiles are of different devices: /device:TPU:15 before, /device:TPU:0 now
where the time goes in v3:
time: 701 us; the launch traced here: 689 us
  waiting for transfers between devices  202 us (29%)
  Pallas kernels  202 us (29%)
  starting transfers between devices  107 us (15%)
  local copies, waits for them, and re-layouts  78.7 us (11%)
  other arithmetic  66.9 us (10%)
  matrix products  27 us (4%)
    ppermute x30, waiting for transfers between devices, along_group(): return lax.ppermute(x, 'group', pairs)  112 us
    ppermute x60, waiting for transfers between devices, flip(): return lax.ppermute(x, 'dp', [(i, i ^ bit) for i in range(count)])  89.3 us
    pallas_call x3, Pallas kernels, feed_call(): pl.pallas_call(kernel, out_shape=outs, grid_spec=pltpu.PrefetchScalarGrid...  67.1 us
    ppermute x30, starting transfers between devices, along_group(): return lax.ppermute(x, 'group', pairs)  64.9 us
    ppermute x60, starting transfers between devices, flip(): return lax.ppermute(x, 'dp', [(i, i ^ bit) for i in range(count)])  42.3 us
    pallas_call x4, Pallas kernels, attend_backward(): pl.pallas_call(partial(backward_kernel, base, final, pairs, width - (pair...  36.4 us
    pallas_call x1, Pallas kernels, attn_grads(): pl.pallas_call(partial(attn_grads_kernel, len(normed)), out_shape=(part,...  24.1 us
    unnamed x232, local copies, waits for them, and re-layouts  23 us
  transfers between devices with their start and end apart: 90, of which 27 were waited for; matrix products, arithmetic and copies ran while one was open for 18% of the time, Pallas kernels for 29%

profile of v3, /device:TPU:0, one launch (start us, length us, event | category | flops | bytes accessed | tf_op | source)
XLA Modules:
  0.0 689.2 jit_solution(14571978025051118219)
XLA Ops:
  0.7 6.3 concatenate.43
  43.5 8.9 %collective-permute-done = bf16[136,1088]{1,0:T(8,128)(2,1)S(1)} collective-permute-done((bf16[136,1088]{1,0:T(8,128)(2,1)}, bf16[136,1088]{1,0:T(8,128)(2,1)S(1)}, u32[]{:S(2)}, u32[]{:S(2)}) %collective-permute-start) | collective-permute-done | bytes 295968 | tf_op jit(solution)/shard_map/ppermute | solution.py:267
  61.4 12.6 %collective-permute-done.3.refs_1_ = bf16[3,136,1088]{2,1,0:T(8,128)(2,1)} collective-permute-done((bf16[3,136,1088]{2,1,0:T(8,128)(2,1)S(1)}, bf16[3,136,1088]{2,1,0:T(8,128)(2,1)}, u32[]{:S(2)}, u32[]{:S(2)}) %collective-permute-start.3) | collective-permute-done | bytes 887840 | tf_op jit(solution)/shard_map/ppermute | solution.py:276
  103.4 6.4 assemble.3
  142.1 13.6 %collective-permute-done.17 = bf16[8,64,1088]{2,1,0:T(8,128)(2,1)S(1)} collective-permute-done((bf16[8,64,1088]{2,1,0:T(8,128)(2,1)}, bf16[8,64,1088]{2,1,0:T(8,128)(2,1)S(1)}, u32[]{:S(2)}, u32[]{:S(2)}) %collective-permute-start.17) | collective-permute-done | bytes 1114144 | tf_op jit(solution)/shard_map/ppermute | solution.py:267
  155.6 5.9 collective-permute-start.20
  171.7 6.5 attend_forward.3
  182.1 6.6 collective-permute-start.23
  193.3 6.5 attend_forward.4
  199.8 9.3 %collective-permute-done.22 = bf16[136,1088]{1,0:T(8,128)(2,1)S(1)} collective-permute-done((bf16[136,1088]{1,0:T(8,128)(2,1)S(1)}, bf16[136,1088]{1,0:T(8,128)(2,1)S(1)}, u32[]{:S(2)}, u32[]{:S(2)}) %collective-permute-start.22) | collective-permute-done | bytes 295968 | tf_op jit(solution)/shard_map/ppermute | solution.py:267
  213.7 6.2 attend_forward.5
  219.9 16.5 %collective-permute-done.26.refs_3_ = bf16[3,136,512]{2,1,0:T(8,128)(2,1)S(1)} collective-permute-done((bf16[3,136,512]{2,1,0:T(8,128)(2,1)S(1)}, bf16[3,136,512]{2,1,0:T(8,128)(2,1)S(1)}, u32[]{:S(2)}, u32[]{:S(2)}) %collective-permute-start.26) | collective-permute-done | bytes 417824 | tf_op jit(solution)/shard_map/ppermute | solution.py:276
  246.2 6.7 assemble.4
  252.9 23.1 %feed.1 = (bf16[4,512,1088]{2,1,0:T(8,128)(2,1)}, bf16[4,512,1088]{2,1,0:T(8,128)(2,1)}, bf16[4,4,136,1088]{3,2,1,0:T(8,128)(2,1)}, bf16[4,4,136,1088]{3,2,1,0:T(8,128)(2,1)}, bf16[1088,512]{1,0:T(8,128)(2,1)}) custom-call(s32[1]{0:T(128)} %bitcast.core_ref, bf16[512,1088]{1,0:T(8,128)(2,1)} %add_convert_fusion.7.x_ref, bf16[4,1088,1088]{2,1,0:T(8,128)(2,1)} %bitcast.231, ...), custom_call_target="tpu_custom_call" | custom-call | flops 12121538560 | bytes 1024 | tf_op jit(solution)/shard_map/feed/pallas_call | solution.py:378
  278.0 9.1 %collective-permute-done.41.refs_8_ = bf16[3,136,512]{2,1,0:T(8,128)(2,1)} collective-permute-done((bf16[3,136,512]{2,1,0:T(8,128)(2,1)}, bf16[3,136,512]{2,1,0:T(8,128)(2,1)}, u32[]{:S(2)}, u32[]{:S(2)}) %collective-permute-start.41) | collective-permute-done | bytes 417824 | tf_op jit(solution)/shard_map/ppermute | solution.py:276
  293.6 7.8 %assemble.5 = bf16[4,4,2,136,1088]{4,3,2,1,0:T(8,128)(2,1)} custom-call(s32[3]{0:T(128)S(1)} %pad_add_fusion.1.here_ref, bf16[4,2,136,1088]{3,2,1,0:T(8,128)(2,1)S(1)} %bitcast.209, bf16[3,136,1088]{2,1,0:T(8,128)(2,1)S(1)} %copy-done.8, bf16[3,136,1088]{2,1,0:T(8,128)(2,1)S(1)} %copy-done.16, bf16[3,136,1088]{2,1,0:T(8,128)(2,1)S(1)} %copy-done.14, ...), custom_call_target="tpu_custom_call" | custom-call | bytes 1183744 | tf_op jit(solution)/shard_map/assemble/pallas_call | solution.py:532
  301.4 6.1 add_convert_fusion.2
  313.3 30.6 %feed_back.1 = (bf16[4,4,136,1088]{3,2,1,0:T(8,128)(2,1)}, bf16[4,4,136,1088]{3,2,1,0:T(8,128)(2,1)}, f32[512,1088]{1,0:T(8,128)}, f32[4,1,1088]{2,1,0:T(1,128)}) custom-call(s32[1]{0:T(128)} %bitcast.core_ref, bf16[512,1088]{1,0:T(8,128)(2,1)} %bitcast.205, bf16[4,1088,1088]{2,1,0:T(8,128)(2,1)} %bitcast.229, ...), custom_call_target="tpu_custom_call" | custom-call | flops 12121538560 | bytes 1024 | tf_op jit(solution)/shard_map/feed_back/pallas_call | solution.py:378
  361.0 6.1 add_convert_fusion.1
  384.9 12.8 %collective-permute-done.46 = bf16[2,136,1088]{2,1,0:T(8,128)(2,1)S(1)} collective-permute-done((bf16[2,136,1088]{2,1,0:T(8,128)(2,1)S(1)}, bf16[2,136,1088]{2,1,0:T(8,128)(2,1)S(1)}, u32[]{:S(2)}, u32[]{:S(2)}) %collective-permute-start.46) | collective-permute-done | bytes 591904 | tf_op jit(solution)/shard_map/ppermute | solution.py:276
  402.6 6.8 collective-permute-start.53
  420.8 11.0 %collective-permute-done.50 = bf16[8,64,1088]{2,1,0:T(8,128)(2,1)S(1)} collective-permute-done((bf16[8,64,1088]{2,1,0:T(8,128)(2,1)S(1)}, bf16[8,64,1088]{2,1,0:T(8,128)(2,1)S(1)}, u32[]{:S(2)}, u32[]{:S(2)}) %collective-permute-start.50) | collective-permute-done | bytes 1114144 | tf_op jit(solution)/shard_map/ppermute | solution.py:267
  437.1 22.1 %collective-permute-done.52 = bf16[136,1088]{1,0:T(8,128)(2,1)} collective-permute-done((bf16[136,1088]{1,0:T(8,128)(2,1)}, bf16[136,1088]{1,0:T(8,128)(2,1)}, u32[]{:S(2)}, u32[]{:S(2)}) %collective-permute-start.52) | collective-permute-done | bytes 295968 | tf_op jit(solution)/shard_map/ppermute | solution.py:267
  470.4 17.1 %collective-permute-done.54 = bf16[8,64,1088]{2,1,0:T(8,128)(2,1)S(1)} collective-permute-done((bf16[8,64,1088]{2,1,0:T(8,128)(2,1)S(1)}, bf16[8,64,1088]{2,1,0:T(8,128)(2,1)S(1)}, u32[]{:S(2)}, u32[]{:S(2)}) %collective-permute-start.54) | collective-permute-done | bytes 1114144 | tf_op jit(solution)/shard_map/ppermute | solution.py:267
  498.9 21.5 %attend_backward.7 = (bf16[512,1088]{1,0:T(8,128)(2,1)S(1)}, bf16[512,1088]{1,0:T(8,128)(2,1)S(1)}, bf16[512,1088]{1,0:T(8,128)(2,1)S(1)}, f32[2,1088]{1,0:T(2,128)S(1)}) custom-call(s32[2]{0:T(128)S(1)} %copy-done.48, bf16[512,1088]{1,0:T(8,128)(2,1)S(1)} %copy-done.57, bf16[1088,512]{1,0:T(8,128)(2,1)S(1)} %copy-done.69, ...), custom_call_target="tpu_custom_call" | custom-call | flops 11408506880 | bytes 557056 | tf_op jit(solution)/shard_map/attend_backward/pallas_call | solution.py:242
  532.0 24.1 %attn_grads.1 = (bf16[4,4,136,1088]{3,2,1,0:T(8,128)(2,1)}, bf16[4,4,136,1088]{3,2,1,0:T(8,128)(2,1)}) custom-call(s32[1]{0:T(128)} %bitcast.core_ref, bf16[512,1088]{1,0:T(8,128)(2,1)} %copy-done.87, bf16[512,1088]{1,0:T(8,128)(2,1)} %copy-done.89, bf16[512,1088]{1,0:T(8,128)(2,1)} %get-tuple-element.342.refs_2_, bf16[512,1088]{1,0:T(8,128)(2,1)} %fusion.18.refs_3_, ...), custom_call_target="tpu_custom_call" | custom-call | flops 12121538560 | bytes 1024 | tf_op jit(solution)/shard_map/attn_grads/pallas_call | solution.py:727
  578.4 9.8 %collective-permute-done.67 = bf16[2,136,1088]{2,1,0:T(8,128)(2,1)S(1)} collective-permute-done((bf16[2,136,1088]{2,1,0:T(8,128)(2,1)S(1)}, bf16[2,136,1088]{2,1,0:T(8,128)(2,1)S(1)}, u32[]{:S(2)}, u32[]{:S(2)}) %collective-permute-start.67) | collective-permute-done | bytes 591904 | tf_op jit(solution)/shard_map/ppermute | solution.py:276
  608.9 5.6 collective-permute-done.77
  628.8 5.5 give_out.4
  638.7 13.4 %project.1 = f32[1088,512]{1,0:T(8,128)} custom-call(bf16[4,512,1088]{2,1,0:T(8,128)(2,1)} %get-tuple-element.283.h_ref, bf16[4,1088,1088]{2,1,0:T(8,128)(2,1)} %bitcast.230, f32[512,1088]{1,0:T(8,128)} %copy-done.4, f32[1,1088]{1,0:T(1,128)} %unstack.40.b_ref), custom_call_target="tpu_custom_call" | custom-call | flops 48486154240 | bytes 1024 | tf_op jit(solution)/shard_map/project/pallas_call | solution.py:378
  652.1 12.2 %collective-permute-done.83 = bf16[136,1088]{1,0:T(8,128)(2,1)S(1)} collective-permute-done((bf16[136,1088]{1,0:T(8,128)(2,1)S(1)}, bf16[136,1088]{1,0:T(8,128)(2,1)S(1)}, u32[]{:S(2)}, u32[]{:S(2)}) %collective-permute-start.83) | collective-permute-done | bytes 295968 | tf_op jit(solution)/shard_map/ppermute | solution.py:267
  665.7 7.6 %collective-permute-done.86 = bf16[1,136,1088]{2,1,0:T(8,128)(2,1)S(1)} collective-permute-done((bf16[1,136,1088]{2,1,0:T(8,128)(2,1)S(1)}, bf16[1,136,1088]{2,1,0:T(8,128)(2,1)S(1)}, u32[]{:S(2)}, u32[]{:S(2)}) %collective-permute-start.86) | collective-permute-done | bytes 295968 | tf_op jit(solution)/shard_map/ppermute | solution.py:276
  (543 shorter events, 318.8 us)
Async XLA Ops:
  7.0 35.7 %collective-permute-start.12 = (bf16[3264]{0:T(1024)(128)(2,1)S(1)}, bf16[3264]{0:T(1024)(128)(2,1)S(1)}, u32[]{:S(2)}, u32[]{:S(2)}) collective-permute-start(bf16[3264]{0:T(1024)(128)(2,1)S(1)} %concatenate.43), channel_id=1, source_target_pairs={{0,3},{1,0},{2,1},{3,2},{4,7},{5,4},{6,5},{7,6},{8,11},{9,8},{10,9... | collective-permute-start | bytes 19592 | tf_op jit(solution)/shard_map/ppermute | solution.py:267
  12.1 30.6 %collective-permute-start.11 = (bf16[3264]{0:T(1024)(128)(2,1)S(1)}, bf16[3264]{0:T(1024)(128)(2,1)S(1)}, u32[]{:S(2)}, u32[]{:S(2)}) collective-permute-start(bf16[3264]{0:T(1024)(128)(2,1)S(1)} %concatenate.43), channel_id=1, source_target_pairs={{0,2},{1,3},{2,0},{3,1},{4,6},{5,7},{6,4},{7,5},{8,10},{9,11},{10,... | collective-permute-start | bytes 19592 | tf_op jit(solution)/shard_map/ppermute | solution.py:267
  12.1 30.7 %collective-permute-start.10 = (bf16[3264]{0:T(1024)(128)(2,1)S(1)}, bf16[3264]{0:T(1024)(128)(2,1)S(1)}, u32[]{:S(2)}, u32[]{:S(2)}) collective-permute-start(bf16[3264]{0:T(1024)(128)(2,1)S(1)} %concatenate.43), channel_id=1, source_target_pairs={{0,1},{1,2},{2,3},{3,0},{4,5},{5,6},{6,7},{7,4},{8,9},{9,10},{10,1... | collective-permute-start | bytes 19592 | tf_op jit(solution)/shard_map/ppermute | solution.py:267
  55.2 31.8 %collective-permute-start.13 = (bf16[8,64,1088]{2,1,0:T(8,128)(2,1)S(1)}, bf16[8,64,1088]{2,1,0:T(8,128)(2,1)}, u32[]{:S(2)}, u32[]{:S(2)}) collective-permute-start(bf16[8,64,1088]{2,1,0:T(8,128)(2,1)S(1)} %bitcast.186), channel_id=1, source_target_pairs={{0,1},{1,2},{2,3},{4,5},{5,6},{6,7},{8,9},{9,10},{10,11},{12,13},{... | collective-permute-start | bytes 3342344 | tf_op jit(solution)/shard_map/ppermute | solution.py:267
  179.7 29.5 %collective-permute-start.25 = (bf16[3,136,1088]{2,1,0:T(8,128)(2,1)S(1)}, bf16[3,136,1088]{2,1,0:T(8,128)(2,1)S(1)}, u32[]{:S(2)}, u32[]{:S(2)}) collective-permute-start(bf16[3,136,1088]{2,1,0:T(8,128)(2,1)S(1)} %pad_maximum_fusion.8.refs_0_), channel_id=1, source_target_pairs={{0,16},{4,20},{8,24},{12,28},{16,0},{20,4},{24,8},{28,12},{1,17},{... | collective-permute-start | bytes 2663432 | tf_op jit(solution)/shard_map/ppermute | solution.py:276
  179.9 29.4 %collective-permute-start.24 = (bf16[3,136,1088]{2,1,0:T(8,128)(2,1)S(1)}, bf16[3,136,1088]{2,1,0:T(8,128)(2,1)S(1)}, u32[]{:S(2)}, u32[]{:S(2)}) collective-permute-start(bf16[3,136,1088]{2,1,0:T(8,128)(2,1)S(1)} %pad_maximum_fusion.8.refs_0_), channel_id=1, source_target_pairs={{0,8},{4,12},{8,0},{12,4},{16,24},{20,28},{24,16},{28,20},{1,9},{5... | collective-permute-start | bytes 2663432 | tf_op jit(solution)/shard_map/ppermute | solution.py:276
  209.3 31.8 %collective-permute-start.28 = (bf16[3,136,1088]{2,1,0:T(8,128)(2,1)S(1)}, bf16[3,136,1088]{2,1,0:T(8,128)(2,1)S(1)}, u32[]{:S(2)}, u32[]{:S(2)}) collective-permute-start(bf16[3,136,1088]{2,1,0:T(8,128)(2,1)S(1)} %pad_maximum_fusion.9.refs_0_), channel_id=1, source_target_pairs={{0,8},{4,12},{8,0},{12,4},{16,24},{20,28},{24,16},{28,20},{1,9},{5... | collective-permute-start | bytes 2663432 | tf_op jit(solution)/shard_map/ppermute | solution.py:276
  209.6 32.1 %collective-permute-start.29 = (bf16[3,136,1088]{2,1,0:T(8,128)(2,1)S(1)}, bf16[3,136,1088]{2,1,0:T(8,128)(2,1)S(1)}, u32[]{:S(2)}, u32[]{:S(2)}) collective-permute-start(bf16[3,136,1088]{2,1,0:T(8,128)(2,1)S(1)} %pad_maximum_fusion.9.refs_0_), channel_id=1, source_target_pairs={{0,16},{4,20},{8,24},{12,28},{16,0},{20,4},{24,8},{28,12},{1,17},{... | collective-permute-start | bytes 2663432 | tf_op jit(solution)/shard_map/ppermute | solution.py:276
  213.6 31.7 %collective-permute-start.30 = (bf16[3,136,1088]{2,1,0:T(8,128)(2,1)S(1)}, bf16[3,136,1088]{2,1,0:T(8,128)(2,1)S(1)}, u32[]{:S(2)}, u32[]{:S(2)}) collective-permute-start(bf16[3,136,1088]{2,1,0:T(8,128)(2,1)S(1)} %pad_maximum_fusion.8.refs_0_), channel_id=1, source_target_pairs={{0,4},{4,0},{8,12},{12,8},{16,20},{20,16},{24,28},{28,24},{1,5},{5... | collective-permute-start | bytes 2663432 | tf_op jit(solution)/shard_map/ppermute | solution.py:276
  244.9 31.0 %collective-permute-start.35 = (bf16[3,136,512]{2,1,0:T(8,128)(2,1)}, bf16[3,136,512]{2,1,0:T(8,128)(2,1)}, u32[]{:S(2)}, u32[]{:S(2)}) collective-permute-start(bf16[3,136,512]{2,1,0:T(8,128)(2,1)} %slice.217), channel_id=1, source_target_pairs={{0,16},{4,20},{8,24},{12,28},{16,0},{20,4},{24,8},{28,12},{1,17},{... | collective-permute-start | bytes 1253384 | tf_op jit(solution)/shard_map/ppermute | solution.py:276
  245.3 30.7 %collective-permute-start.36 = (bf16[3,136,576]{2,1,0:T(8,128)(2,1)}, bf16[3,136,576]{2,1,0:T(8,128)(2,1)}, u32[]{:S(2)}, u32[]{:S(2)}) collective-permute-start(bf16[3,136,576]{2,1,0:T(8,128)(2,1)} %slice.218), channel_id=1, source_target_pairs={{0,8},{4,12},{8,0},{12,4},{16,24},{20,28},{24,16},{28,20},{1,9},{5... | collective-permute-start | bytes 1410056 | tf_op jit(solution)/shard_map/ppermute | solution.py:276
  245.6 30.4 %collective-permute-start.37 = (bf16[3,136,1088]{2,1,0:T(8,128)(2,1)S(1)}, bf16[3,136,1088]{2,1,0:T(8,128)(2,1)S(1)}, u32[]{:S(2)}, u32[]{:S(2)}) collective-permute-start(bf16[3,136,1088]{2,1,0:T(8,128)(2,1)S(1)} %pad_maximum_fusion.9.refs_0_), channel_id=1, source_target_pairs={{0,4},{4,0},{8,12},{12,8},{16,20},{20,16},{24,28},{28,24},{1,5},{5... | collective-permute-start | bytes 2663432 | tf_op jit(solution)/shard_map/ppermute | solution.py:276
  245.6 31.3 %collective-permute-start.38 = (bf16[3,136,1088]{2,1,0:T(8,128)(2,1)S(1)}, bf16[3,136,1088]{2,1,0:T(8,128)(2,1)}, u32[]{:S(2)}, u32[]{:S(2)}) collective-permute-start(bf16[3,136,1088]{2,1,0:T(8,128)(2,1)S(1)} %collective-permute-done.28.refs_1_), channel_id=1, source_target_pairs={{0,4},{4,0},{8,12},{12,8},{16,20},{20,16},{24,28},{28,24},{1,5},{5... | collective-permute-start | bytes 2663432 | tf_op jit(solution)/shard_map/ppermute | solution.py:276
  246.1 30.8 %collective-permute-start.39 = (bf16[3,136,1088]{2,1,0:T(8,128)(2,1)S(1)}, bf16[3,136,1088]{2,1,0:T(8,128)(2,1)}, u32[]{:S(2)}, u32[]{:S(2)}) collective-permute-start(bf16[3,136,1088]{2,1,0:T(8,128)(2,1)S(1)} %collective-permute-done.29.refs_2_), channel_id=1, source_target_pairs={{0,4},{4,0},{8,12},{12,8},{16,20},{20,16},{24,28},{28,24},{1,5},{5... | collective-permute-start | bytes 2663432 | tf_op jit(solution)/shard_map/ppermute | solution.py:276
  309.9 34.0 %collective-permute-start.43 = (bf16[2,136,1088]{2,1,0:T(8,128)(2,1)S(1)}, bf16[2,136,1088]{2,1,0:T(8,128)(2,1)}, u32[]{:S(2)}, u32[]{:S(2)}) collective-permute-start(bf16[2,136,1088]{2,1,0:T(8,128)(2,1)S(1)} %get-tuple-element.320), channel_id=1, source_target_pairs={{0,8},{4,12},{8,0},{12,4},{16,24},{20,28},{24,16},{28,20},{1,9},{5... | collective-permute-start | bytes 1775624 | tf_op jit(solution)/shard_map/ppermute | solution.py:276
  311.6 32.4 %collective-permute-start.44 = (bf16[2,136,1088]{2,1,0:T(8,128)(2,1)S(1)}, bf16[2,136,1088]{2,1,0:T(8,128)(2,1)}, u32[]{:S(2)}, u32[]{:S(2)}) collective-permute-start(bf16[2,136,1088]{2,1,0:T(8,128)(2,1)S(1)} %get-tuple-element.321), channel_id=1, source_target_pairs={{0,16},{4,20},{8,24},{12,28},{16,0},{20,4},{24,8},{28,12},{1,17},{... | collective-permute-start | bytes 1775624 | tf_op jit(solution)/shard_map/ppermute | solution.py:276
  351.3 46.4 %collective-permute-start.49 = (bf16[4,136,1088]{2,1,0:T(8,128)(2,1)}, bf16[4,136,1088]{2,1,0:T(8,128)(2,1)}, u32[]{:S(2)}, u32[]{:S(2)}) collective-permute-start(bf16[4,136,1088]{2,1,0:T(8,128)(2,1)} %pad_maximum_fusion.2), channel_id=1, source_target_pairs={{0,16},{4,20},{8,24},{12,28},{16,0},{20,4},{24,8},{28,12},{1,17},{... | collective-permute-start | bytes 3551240 | tf_op jit(solution)/shard_map/ppermute | solution.py:276
  354.4 43.3 %collective-permute-start.48 = (bf16[4,136,1088]{2,1,0:T(8,128)(2,1)}, bf16[4,136,1088]{2,1,0:T(8,128)(2,1)}, u32[]{:S(2)}, u32[]{:S(2)}) collective-permute-start(bf16[4,136,1088]{2,1,0:T(8,128)(2,1)} %pad_maximum_fusion.1), channel_id=1, source_target_pairs={{0,8},{4,12},{8,0},{12,4},{16,24},{20,28},{24,16},{28,20},{1,9},{5... | collective-permute-start | bytes 3551240 | tf_op jit(solution)/shard_map/ppermute | solution.py:276
  400.1 31.7 %collective-permute-start.50 = (bf16[8,64,1088]{2,1,0:T(8,128)(2,1)S(1)}, bf16[8,64,1088]{2,1,0:T(8,128)(2,1)S(1)}, u32[]{:S(2)}, u32[]{:S(2)}) collective-permute-start(bf16[8,64,1088]{2,1,0:T(8,128)(2,1)S(1)} %bitcast.214), channel_id=1, source_target_pairs={{1,0},{2,1},{3,2},{5,4},{6,5},{7,6},{9,8},{10,9},{11,10},{13,12},{... | collective-permute-start | bytes 3342344 | tf_op jit(solution)/shard_map/ppermute | solution.py:267
  402.6 34.5 %collective-permute-start.53 = (bf16[136,1088]{1,0:T(8,128)(2,1)}, bf16[136,1088]{1,0:T(8,128)(2,1)}, u32[]{:S(2)}, u32[]{:S(2)}) collective-permute-start(bf16[136,1088]{1,0:T(8,128)(2,1)} %get-tuple-element.331), channel_id=1, source_target_pairs={{0,3},{1,0},{2,1},{3,2},{4,7},{5,4},{6,5},{7,6},{8,11},{9,8},{10,9... | collective-permute-start | bytes 887816 | tf_op jit(solution)/shard_map/ppermute | solution.py:267
  409.4 49.7 %collective-permute-start.52 = (bf16[136,1088]{1,0:T(8,128)(2,1)}, bf16[136,1088]{1,0:T(8,128)(2,1)}, u32[]{:S(2)}, u32[]{:S(2)}) collective-permute-start(bf16[136,1088]{1,0:T(8,128)(2,1)} %get-tuple-element.332), channel_id=1, source_target_pairs={{0,2},{1,3},{2,0},{3,1},{4,6},{5,7},{6,4},{7,5},{8,10},{9,11},{10,... | collective-permute-start | bytes 887816 | tf_op jit(solution)/shard_map/ppermute | solution.py:267
  409.4 49.7 %collective-permute-start.51 = (bf16[136,1088]{1,0:T(8,128)(2,1)}, bf16[136,1088]{1,0:T(8,128)(2,1)}, u32[]{:S(2)}, u32[]{:S(2)}) collective-permute-start(bf16[136,1088]{1,0:T(8,128)(2,1)} %get-tuple-element.333), channel_id=1, source_target_pairs={{0,1},{1,2},{2,3},{3,0},{4,5},{5,6},{6,7},{7,4},{8,9},{9,10},{10,1... | collective-permute-start | bytes 887816 | tf_op jit(solution)/shard_map/ppermute | solution.py:267
  412.8 78.3 %collective-permute-start.56 = (bf16[4,136,1088]{2,1,0:T(8,128)(2,1)}, bf16[4,136,1088]{2,1,0:T(8,128)(2,1)}, u32[]{:S(2)}, u32[]{:S(2)}) collective-permute-start(bf16[4,136,1088]{2,1,0:T(8,128)(2,1)} %pad_maximum_fusion.4), channel_id=1, source_target_pairs={{0,16},{4,20},{8,24},{12,28},{16,0},{20,4},{24,8},{28,12},{1,17},{... | collective-permute-start | bytes 3551240 | tf_op jit(solution)/shard_map/ppermute | solution.py:276
  431.8 59.3 %collective-permute-start.55 = (bf16[4,136,1088]{2,1,0:T(8,128)(2,1)}, bf16[4,136,1088]{2,1,0:T(8,128)(2,1)}, u32[]{:S(2)}, u32[]{:S(2)}) collective-permute-start(bf16[4,136,1088]{2,1,0:T(8,128)(2,1)} %pad_maximum_fusion.3), channel_id=1, source_target_pairs={{0,8},{4,12},{8,0},{12,4},{16,24},{20,28},{24,16},{28,20},{1,9},{5... | collective-permute-start | bytes 3551240 | tf_op jit(solution)/shard_map/ppermute | solution.py:276
  462.5 32.5 %collective-permute-start.57 = (bf16[1,136,1088]{2,1,0:T(8,128)(2,1)}, bf16[1,136,1088]{2,1,0:T(8,128)(2,1)}, u32[]{:S(2)}, u32[]{:S(2)}) collective-permute-start(bf16[1,136,1088]{2,1,0:T(8,128)(2,1)} %bitcast.66), channel_id=1, source_target_pairs={{0,8},{4,12},{8,0},{12,4},{16,24},{20,28},{24,16},{28,20},{1,9},{5... | collective-permute-start | bytes 887816 | tf_op jit(solution)/shard_map/ppermute | solution.py:276
  462.8 32.2 %collective-permute-start.58 = (bf16[1,136,1088]{2,1,0:T(8,128)(2,1)}, bf16[1,136,1088]{2,1,0:T(8,128)(2,1)}, u32[]{:S(2)}, u32[]{:S(2)}) collective-permute-start(bf16[1,136,1088]{2,1,0:T(8,128)(2,1)} %bitcast.66), channel_id=1, source_target_pairs={{0,16},{4,20},{8,24},{12,28},{16,0},{20,4},{24,8},{28,12},{1,17},{... | collective-permute-start | bytes 887816 | tf_op jit(solution)/shard_map/ppermute | solution.py:276
  491.1 30.3 %collective-permute-start.59 = (bf16[8,64,1088]{2,1,0:T(8,128)(2,1)S(1)}, bf16[8,64,1088]{2,1,0:T(8,128)(2,1)S(1)}, u32[]{:S(2)}, u32[]{:S(2)}) collective-permute-start(bf16[8,64,1088]{2,1,0:T(8,128)(2,1)S(1)} %bitcast.211), channel_id=1, source_target_pairs={{1,0},{2,1},{3,2},{5,4},{6,5},{7,6},{9,8},{10,9},{11,10},{13,12},{... | collective-permute-start | bytes 3342344 | tf_op jit(solution)/shard_map/ppermute | solution.py:267
  525.1 31.0 %collective-permute-start.64 = (bf16[136,1088]{1,0:T(8,128)(2,1)S(1)}, bf16[136,1088]{1,0:T(8,128)(2,1)S(1)}, u32[]{:S(2)}, u32[]{:S(2)}) collective-permute-start(bf16[136,1088]{1,0:T(8,128)(2,1)S(1)} %get-tuple-element.327), channel_id=1, source_target_pairs={{0,3},{1,0},{2,1},{3,2},{4,7},{5,4},{6,5},{7,6},{8,11},{9,8},{10,9... | collective-permute-start | bytes 887816 | tf_op jit(solution)/shard_map/ppermute | solution.py:267
  576.2 46.0 %collective-permute-start.68 = (bf16[4,136,1088]{2,1,0:T(8,128)(2,1)}, bf16[4,136,1088]{2,1,0:T(8,128)(2,1)}, u32[]{:S(2)}, u32[]{:S(2)}) collective-permute-start(bf16[4,136,1088]{2,1,0:T(8,128)(2,1)} %maximum_maximum_fusion.mine_ref), channel_id=1, source_target_pairs={{0,4},{4,0},{8,12},{12,8},{16,20},{20,16},{24,28},{28,24},{1,5},{5... | collective-permute-start | bytes 3551240 | tf_op jit(solution)/shard_map/ppermute | solution.py:276
  591.6 42.7 %collective-permute-start.75 = (bf16[4,136,1088]{2,1,0:T(8,128)(2,1)}, bf16[4,136,1088]{2,1,0:T(8,128)(2,1)}, u32[]{:S(2)}, u32[]{:S(2)}) collective-permute-start(bf16[4,136,1088]{2,1,0:T(8,128)(2,1)} %pad_maximum_fusion.6), channel_id=1, source_target_pairs={{0,16},{4,20},{8,24},{12,28},{16,0},{20,4},{24,8},{28,12},{1,17},{... | collective-permute-start | bytes 3551240 | tf_op jit(solution)/shard_map/ppermute | solution.py:276
  594.0 34.8 %collective-permute-start.73 = (bf16[4,136,1088]{2,1,0:T(8,128)(2,1)}, bf16[4,136,1088]{2,1,0:T(8,128)(2,1)}, u32[]{:S(2)}, u32[]{:S(2)}) collective-permute-start(bf16[4,136,1088]{2,1,0:T(8,128)(2,1)} %maximum_maximum_fusion.1.mine_ref), channel_id=1, source_target_pairs={{0,4},{4,0},{8,12},{12,8},{16,20},{20,16},{24,28},{28,24},{1,5},{5... | collective-permute-start | bytes 3551240 | tf_op jit(solution)/shard_map/ppermute | solution.py:276
  595.2 39.1 %collective-permute-start.74 = (bf16[4,136,1088]{2,1,0:T(8,128)(2,1)}, bf16[4,136,1088]{2,1,0:T(8,128)(2,1)}, u32[]{:S(2)}, u32[]{:S(2)}) collective-permute-start(bf16[4,136,1088]{2,1,0:T(8,128)(2,1)} %pad_maximum_fusion.5), channel_id=1, source_target_pairs={{0,8},{4,12},{8,0},{12,4},{16,24},{20,28},{24,16},{28,20},{1,9},{5... | collective-permute-start | bytes 3551240 | tf_op jit(solution)/shard_map/ppermute | solution.py:276
  (172 other events, 2853.5 us)

commit v4 on v3

--- a/solution.py
+++ b/solution.py
@@ -16,10 +16,11 @@
 SCALE = HEAD ** (-0.5)
 VMEM_BYTES = 40 * 1024 * 1024
 ATTEND_BYTES = 20 * 1024 * 1024
-
-
-def tile_length(span_len):
-    return 256 if span_len % 256 == 0 else span_len
+FULL_BYTES = 52 * 1024 * 1024
+
+
+def tile_length(length):
+    return 512 if length % 512 == 0 else length
 
 
 def keep_of(tile_base, tile_len, low_row, own_base):
@@ -29,17 +30,23 @@
     return (key_pos >= low_row) & (key_pos <= query_pos)
 
 
-def tile_loops(bounds_ref, tile, base_tile, count, own_tile):
-    low_tile = bounds_ref[0]
-    mid_tile = bounds_ref[1]
-    clear_end = min(max(own_tile - base_tile, 0), count)
-    begin = jnp.clip(low_tile - base_tile, 0, clear_end)
-    middle = jnp.clip(mid_tile - base_tile, begin, clear_end)
-    lax.fori_loop(begin, middle, lambda t, c: tile(t, True), None)
-    lax.fori_loop(middle, clear_end, lambda t, c: tile(t, False), None)
-    for t in range(clear_end, count):
-        tile(t, True)
-    return begin
+def each_tile(bounds_ref, tile, base, length, own_base, unread=None):
+    size = tile_length(length)
+    half = size // 2
+    least, greatest = bounds_ref[0], bounds_ref[1]
+    for first in range(0, length, size):
+        begin = base + first
+        whole = least < begin + half
+        upper = (least >= begin + half) & (least < begin + size)
+        if begin + size > own_base:
+            pl.when(whole)(partial(tile, first, size, True))
+        else:
+            pl.when(whole & (greatest > begin))(partial(tile, first, size, True))
+            pl.when(whole & (greatest <= begin))(partial(tile, first, size, False))
+        pl.when(upper)(partial(tile, first + half, half, True))
+        if unread is not None:
+            pl.when(upper)(partial(unread, first, half))
+            pl.when(least >= begin + size)(partial(unread, first, size))
 
 
 def inside(x, axis, valid):
@@ -58,7 +65,6 @@
     k_refs, v_refs = refs[:blocks], refs[blocks : 2 * blocks]
     ot_ref, lse_ref, max_ref, sum_ref, acc_ref = refs[-5:]
     span_len = qt_ref.shape[1]
-    tile_len = tile_length(span_len)
     own_base = sum(lengths) - span_len
     last = pl.program_id(0) + first == pairs - 1
     valid = jnp.where(last, last_half, LANES)
@@ -69,12 +75,12 @@
     base = 0
     for k_ref, v_ref, length in zip(k_refs, v_refs, lengths):
 
-        def tile(t, masked, k_ref=k_ref, v_ref=v_ref, base=base):
-            rows = pl.ds(pl.multiple_of(t * tile_len, tile_len), tile_len)
+        def tile(first_row, tile_len, masked, k_ref=k_ref, v_ref=v_ref, base=base):
+            rows = slice(first_row, first_row + tile_len)
             k_tile = inside(k_ref[rows, :], 1, valid)
             v_t = v_ref[rows, :].T
             if masked:
-                keep = keep_of(base + t * tile_len, tile_len, low_ref[...], own_base)
+                keep = keep_of(base + first_row, tile_len, low_ref[...], own_base)
 
             def one(head):
                 scores = jnp.dot(k_tile, heads[head], preferred_element_type=F32)
@@ -99,7 +105,7 @@
             def _():
                 one(0)
 
-        tile_loops(bounds_ref, tile, base // tile_len, length // tile_len, own_base // tile_len)
+        each_tile(bounds_ref, tile, base, length, own_base)
         base += length
     safe = jnp.where(sum_ref[...] > 0, sum_ref[...], 1.0)
     ot_ref[...] = jnp.concatenate([acc_ref[0] / safe[0], acc_ref[1] / safe[1]], axis=0).astype(BF16)
@@ -112,8 +118,6 @@
     first = base == 0
     acc_in = None if first else refs[0]
     acc_out, dk_ref, dv_ref, sums_ref, acc_ref = refs[-5:]
-    span_len = q_ref.shape[0]
-    tile_len = tile_length(span_len)
     last = pl.program_id(0) == pairs - 1
     valid = jnp.where(last, last_half, LANES)
     q_heads = halves(inside((q_ref[...].astype(F32) * SCALE).astype(BF16), 1, valid), 1)
@@ -128,13 +132,13 @@
     else:
         acc_ref[...] = acc_in[0]
 
-    def tile(t, masked):
-        rows = pl.ds(pl.multiple_of(t * tile_len, tile_len), tile_len)
+    def tile(first_row, tile_len, masked):
+        rows = slice(first_row, first_row + tile_len)
         k_tile = inside(k_ref[rows, :], 1, valid)
         v_tile = inside(v_ref[rows, :], 1, valid)
         k_t = k_tile.T
         if masked:
-            keep = keep_of(base + t * tile_len, tile_len, low_ref[...], own_base)
+            keep = keep_of(base + first_row, tile_len, low_ref[...], own_base)
 
         def one(head):
             scores = jnp.dot(k_tile, qt_heads[head], preferred_element_type=F32)
@@ -162,15 +166,12 @@
         def _():
             write(*one(0))
 
-    begin = tile_loops(bounds_ref, tile, base // tile_len, k_ref.shape[0] // tile_len, own_base // tile_len)
-
-    def clear(t, carry):
-        rows = pl.ds(pl.multiple_of(t * tile_len, tile_len), tile_len)
+    def clear(first_row, tile_len):
+        rows = slice(first_row, first_row + tile_len)
         dk_ref[rows, :] = jnp.zeros((tile_len, LANES), BF16)
         dv_ref[rows, :] = jnp.zeros((tile_len, LANES), BF16)
-        return carry
-
-    lax.fori_loop(0, begin, clear, None)
+
+    each_tile(bounds_ref, tile, base, k_ref.shape[0], own_base, clear)
     dv_sum = jnp.sum(dv_ref[...].astype(F32), axis=0, keepdims=True)
     if final:
         dq = (jnp.concatenate([acc_ref[0], acc_ref[1]], axis=0).T * SCALE).astype(BF16)
@@ -257,7 +258,7 @@
         cost_estimate=pl.CostEstimate(
             flops=40 * span_len * k.shape[0] * width, bytes_accessed=span_len * width, transcendentals=0
         ),
-        compiler_params=pltpu.CompilerParams(vmem_limit_bytes=ATTEND_BYTES),
+        compiler_params=pltpu.CompilerParams(vmem_limit_bytes=ATTEND_BYTES if k.shape[0] == span_len else VMEM_BYTES),
         name="attend_backward",
     )(*inputs)
 
@@ -386,7 +387,7 @@
             scratch_shapes=scratch,
         ),
         cost_estimate=pl.CostEstimate(flops=20 * inputs[0].size * inputs[1].shape[-1], bytes_accessed=1024, transcendentals=0),
-        compiler_params=pltpu.CompilerParams(vmem_limit_bytes=56 * 1024 * 1024),
+        compiler_params=pltpu.CompilerParams(vmem_limit_bytes=FULL_BYTES + 4 * 1024 * 1024),
         name=name,
     )(*scalars, *inputs)
 
@@ -539,7 +540,7 @@
             out_specs=[pl.BlockSpec(shape, lambda i, h, n=len(shape): (0,) * n) for shape in shapes],
             scratch_shapes=[pltpu.SemaphoreType.DMA((1 + 10 * (groups - 1) + 4,))],
         ),
-        compiler_params=pltpu.CompilerParams(vmem_limit_bytes=VMEM_BYTES),
+        compiler_params=pltpu.CompilerParams(vmem_limit_bytes=FULL_BYTES),
         cost_estimate=pl.CostEstimate(flops=0, bytes_accessed=own.size, transcendentals=0),
         name="assemble",
     )(jnp.stack(here).astype(jnp.int32), own, *sources)
@@ -781,6 +782,48 @@
         compiler_params=pltpu.CompilerParams(vmem_limit_bytes=VMEM_BYTES),
         name="give_out",
     )(jnp.stack(here).astype(jnp.int32), shares, other)
+
+
+def enter_kernel(own, x_ref, gain_ref, shift_ref, wk_ref, wv_ref, bv_ref, *refs):
+    values = x_ref[...].astype(F32)
+    center = values - jnp.mean(values, axis=-1, keepdims=True)
+    scale = lax.rsqrt(jnp.mean(center * center, axis=-1, keepdims=True) + EPSILON)
+    normed = (center * scale * gain_ref[...] + shift_ref[...]).astype(BF16)
+    if own:
+        wq_ref, bq_ref, n_ref, k_ref, v_ref, q_ref, qt_ref = refs
+        q = (jnp.dot(normed, wq_ref[...], preferred_element_type=F32) + bq_ref[...]).astype(BF16)
+        q_ref[...] = q
+        qt_ref[...] = q.T
+    else:
+        n_ref, k_ref, v_ref = refs
+    n_ref[...] = normed
+    k_ref[...] = jnp.dot(normed, wk_ref[...], preferred_element_type=F32).astype(BF16)
+    v_ref[...] = (jnp.dot(normed, wv_ref[...], preferred_element_type=F32) + bv_ref[...]).astype(BF16)
+
+
+def enter(x, gain, shift, full_k, full_v, bias_v, *query):
+    span_len, width = x.shape
+    band = span_len
+    rows = pl.BlockSpec((band, width), lambda i: (i, 0))
+    line = pl.BlockSpec((1, width), lambda i: (0, 0))
+    inputs = [x, gain[None], shift[None], full_k, full_v, bias_v[None]]
+    in_specs = [rows, line, line, in_vmem(), in_vmem(), line]
+    shapes, out_specs = [(span_len, width)] * 3, [rows] * 3
+    if query:
+        inputs += [query[0], query[1][None]]
+        in_specs += [in_vmem(), line]
+        shapes += [(span_len, width), (width, span_len)]
+        out_specs += [rows, pl.BlockSpec((width, band), lambda i: (0, i))]
+    return pl.pallas_call(
+        partial(enter_kernel, bool(query)),
+        out_shape=[jax.ShapeDtypeStruct(shape, BF16) for shape in shapes],
+        grid=(span_len // band,),
+        in_specs=in_specs,
+        out_specs=out_specs,
+        cost_estimate=pl.CostEstimate(flops=0, bytes_accessed=1024, transcendentals=0),
+        compiler_params=pltpu.CompilerParams(vmem_limit_bytes=FULL_BYTES),
+        name="enter",
+    )(*inputs)
 
 
 def mean_spread(values):
@@ -859,6 +902,11 @@
     small = jnp.concatenate(
         [norm1_gain, norm1_bias, query_bias, value_bias, out_bias, norm2_gain, norm2_bias, proj_bias, fc_bias]
     )
+    if fast:
+        attn_mats = [w.reshape(2, half, width) for w in (w_query, w_key, w_value, w_out)]
+        attn_piece = lax.select_n(chip, *(pick(w, core) for w in attn_mats))
+        attn_hops = [along_group(attn_piece, step, groups, True) for step in range(1, groups)]
+        small = after(small, attn_hops[0])
     small_rel = jnp.stack([small] + [along_group(small, step, groups, True) for step in range(1, groups)])
     small_all = jnp.take(small_rel, lax.rem(z - jnp.arange(groups) + groups, groups), axis=0)
     vectors = small_all[:, : 8 * shard].reshape(groups, 8, shard).transpose(1, 0, 2).reshape(8, width)
@@ -867,11 +915,10 @@
 
     mine = tokens[0]
     inputs = mine.astype(F32)
-    normed_one = layer_norm(inputs, gain_one, shift_one).astype(BF16)
     own_base = key_len - span_len
     if fast:
-        attn_own = jnp.stack([w_query, w_key, w_value, w_out]).reshape(4, 2, half, width)
-        attn_ring = from_planes(pick(pick(attn_own, chip), core), groups)
+        attn_own = jnp.stack(attn_mats)
+        attn_ring = jnp.stack(attn_hops)
         attn_near = plane_share_near(attn_ring, count)
         hops = [mine, hop(after(mine, attn_ring, small_rel), 1, groups)]
         attn_three = (attn_ring,) + attn_near
@@ -881,56 +928,45 @@
         hops.append(hop(hops[1], 1, groups))
         attn = assemble(attn_own, attn_three + attn_far + attn_other, here, groups, "apart")
         full_q, full_k, full_v, full_o = (part.reshape(width, width) for part in attn)
-        normed_one, hops[2] = lax.optimization_barrier((normed_one, hops[2]))
         hops.append(hop(hops[2], 1, groups))
     else:
         gather = partial(lax.all_gather, axis_name="group", axis=0, tiled=True)
         full_q, full_k, full_v, full_o = (gather(w) for w in (w_query, w_key, w_value, w_out))
         full_fc = gather(w_fc).reshape(width, chunks, width).transpose(1, 0, 2)
         full_proj = gather(w_proj).reshape(chunks, width, width)
-    queries_t = (jnp.einsum("td,df->ft", normed_one, full_q, preferred_element_type=F32) + bias_q[:, None]).astype(BF16)
-    queries = (matmul(normed_one, full_q) + bias_q).astype(BF16)
-
-    def keys_of(normed):
-        return matmul(normed, full_k).astype(BF16), (matmul(normed, full_v) + bias_v).astype(BF16)
-
-    def norm_of(block):
-        return layer_norm(block.astype(F32), gain_one, shift_one).astype(BF16)
-
-    if fast:
-        own_keys = keys_of(normed_one)
+    if fast:
+        known = (gain_one, shift_one, full_k, full_v, bias_v)
+        *own, queries, queries_t = enter(after(mine, hops[2]), *known, full_q, bias_q)
+        second = enter(after(hops[1], queries), *known)
+        third = enter(after(hops[2], second[1]), *known)
         fc_own = w_fc.reshape(2, half, chunks, width).transpose(2, 0, 1, 3)
         fc_piece = pick(pick(fc_own, chip), core)
         proj_own = w_proj.reshape(4, 2, half, width)
         proj_piece = pick(pick(proj_own, chip), core)
-        normed = [normed_one, norm_of(hops[1]), norm_of(hops[2])]
-        both = [own_keys] + [keys_of(block) for block in normed[1:]]
-        hops[3] = after(hops[3], *both[1], *both[2])
+        hops[3] = after(hops[3], third[1])
         fc_ring = from_planes(after(fc_piece, hops[3]), groups)
-        normed.append(norm_of(hops[3]))
-        both.append(keys_of(normed[3]))
-        normed, keys, values = normed[::-1], [b[0] for b in both[::-1]], [b[1] for b in both[::-1]]
+        blocks = [enter(hops[3], *known), third, second, own]
+        normed, keys, values = ([block[i] for block in blocks] for i in range(3))
     else:
         hops = [mine]
         for _ in range(groups - 1):
             hops.append(hop(hops[-1], 1, groups))
-        normed = [norm_of(jnp.concatenate(hops[::-1]))]
-        both = keys_of(normed[0])
-        keys, values = [both[0]], [both[1]]
+        normed = [layer_norm(jnp.concatenate(hops[::-1]).astype(F32), gain_one, shift_one).astype(BF16)]
+        keys = [matmul(normed[0], full_k).astype(BF16)]
+        values = [(matmul(normed[0], full_v) + bias_v).astype(BF16)]
+        queries = (matmul(normed[0][own_base:], full_q) + bias_q).astype(BF16)
+        queries_t = queries.T
 
     seg = segments[0]
     seg_mine = lax.dynamic_slice_in_dim(seg, z * span_len, span_len)
     low_row = jnp.sum((seg[None, :] < seg_mine[:, None]).astype(jnp.int32), axis=1)
     low_row = low_row + (groups - 1 - z) * span_len
-    tile_len = tile_length(span_len)
-    low_tile = low_row[0] // tile_len
-    mid_tile = jnp.clip((low_row[-1] + tile_len - 1) // tile_len, low_tile, own_base // tile_len)
-    bounds = jnp.stack([low_tile, mid_tile]).astype(jnp.int32)
+    bounds = jnp.stack([low_row[0], low_row[-1]]).astype(jnp.int32)
     low_row = low_row[None]
 
     state = None
     for number, part in enumerate(forward_parts):
-        row_now = after(low_row, queries) if number == 0 else low_row
+        row_now = low_row
         if fast and number == 1:
             fc_near = plane_share_near(after(fc_ring, state[0]), count)
             proj_ring = from_planes(after(proj_piece, fc_ring, state[0]), groups)
@@ -939,13 +975,14 @@
             fc_three = (fc_ring,) + fc_near
             fc_far = plane_share_far(*(after(part, state[0]) for part in fc_near), count)
             fc_other = tuple(flip(after(part, state[0], *fc_near), CORE, count) for part in fc_three)
-            proj_near = plane_share_near(after(proj_ring, state[0], *fc_near), count)
             row_now = after(low_row, proj_ring, *fc_near)
         state = attend_forward(part, queries_t, keys, values, row_now, bounds, state)
     attended_t, lse = state
     if fast:
-        fc_other += tuple(flip(after(part, attended_t), CORE, count) for part in fc_far)
-        attended_t = after(attended_t, *fc_far)
+        attended_t, *fc_moved = lax.optimization_barrier((attended_t, *fc_far, *fc_other))
+        fc_far, fc_other = tuple(fc_moved[:2]), tuple(fc_moved[2:])
+        fc_other += tuple(flip(part, CORE, count) for part in fc_far)
+        proj_near = plane_share_near(after(proj_ring, attended_t), count)
     resid = inputs + jnp.einsum("ft,fd->td", attended_t, full_o, preferred_element_type=F32) + bias_o
     normed_two = layer_norm(resid, gain_two, shift_two).astype(BF16)
     if fast:
@@ -956,17 +993,18 @@
     proj_bias_grad = row_sum(cot)
     which = jnp.reshape(core, (1,)).astype(jnp.int32)
     if fast:
+        proj_three = (proj_ring,) + proj_near
+        proj_far = plane_share_far(*(after(part, full_fc) for part in proj_near), count)
+        proj_other = tuple(flip(after(part, full_fc, *proj_near), CORE, count) for part in proj_three)
         normed_two = after(normed_two, *proj_near)
     hidden, slope, proj_keep, proj_send, normed_two_t = feed(which, normed_two, full_fc, bias_fc, cot)
     cot_now = cot
     if fast:
-        proj_three = (proj_ring,) + proj_near
-        proj_far = plane_share_far(*(after(part, normed_two) for part in proj_near), count)
-        proj_other = tuple(flip(after(part, normed_two, *proj_near), CORE, count) for part in proj_three)
         proj_send, *proj_moved = lax.optimization_barrier((proj_send, *proj_far, *proj_other))
         proj_far, proj_other = tuple(proj_moved[:2]), tuple(proj_moved[2:])
         proj_other += tuple(flip(part, CORE, count) for part in proj_far)
-        full_proj = assemble(proj_own, proj_three + proj_far + proj_other, here, groups, "plane")
+        proj_send = after(proj_send, *proj_other)
+        full_proj = assemble(proj_own, proj_three + proj_far + tuple(proj_other), here, groups, "plane")
         full_proj = full_proj[0].reshape(4, width, width)
         proj_chip = chip_sum(proj_keep, proj_send, count)
         cot_now, proj_chip = lax.optimization_barrier((cot, proj_chip))
@@ -1046,12 +1084,12 @@
         attn_via = plane_first_step(attn_chip, chip, count, 0)
         fc_line_near = tuple(after(part, attn_chip) for part in fc_line_near)
         fc_line_far = plane_share_far(*fc_line_near, count)
-        attn_mine = plane_second_step(attn_chip, attn_via, chip, count, 0)
+        (proj_sum,) = give_out(after(proj_shares, attn_chip), proj_others, here, "plane")
+        attn_mine = plane_second_step(after(attn_chip, proj_sum), attn_via, chip, count, 0)
         fc_line_far = tuple(after(part, *attn_via) for part in fc_line_far)
         fc_shares = shares_of(fc_line[None], fc_line_near, fc_line_far)
         fc_others = flip(fc_shares, CORE, count)
         dqueries_now = after(dqueries, *attn_via)
-        (proj_sum,) = give_out(after(proj_shares, *attn_via), proj_others, here, "plane")
     normed_one_grad = back_through(dqueries_now, full_q)
     tokens_grad, _, gain_one_grad, shift_one_grad, _ = norm_back(
         mine, gain_one, resid_grad, normed_one_grad, norm_term, turned=True
@@ -1072,15 +1110,15 @@
     vector_sums = parts_sum([vector_sums] + [along_group(vector_sums, step, groups, True) for step in range(1, groups)])
     hidden_now = hidden
     if fast:
-        (fc_sum,) = give_out(after(fc_shares, proj_sum), fc_others, here, "chip")
-        attn_mine = second_sum(*(after(part, proj_sum, fc_sum, tokens_grad) for part in attn_mine))
+        attn_mine = second_sum(*(after(part, tokens_grad) for part in attn_mine))
         attn_line = line_parts(attn_mine, z, groups)
         vector_sums = vector_sums + flip(vector_sums, CORE, count)
         hidden_now = after(hidden, attn_mine, vector_sums)
     activations = project(hidden_now, full_proj, resid, bias_p[None])
     if fast:
         vector_sums = vector_sums + after(flip(vector_sums, ACROSS, count), activations)
-        attn_line = [after(part, vector_sums) for part in attn_line]
+        (fc_sum,) = give_out(after(fc_shares, activations), fc_others, here, "chip")
+        attn_line = [after(part, vector_sums, fc_sum) for part in attn_line]
         vector_sums = vector_sums + flip(vector_sums, DOWN, count)
     else:
         bit = 1

time: 701 us -> 649 us (0.926)
  Pallas kernels: 202 us -> 237 us
  local copies, waits for them, and re-layouts: 78.7 us -> 52.6 us
  waiting for transfers between devices: 202 us -> 176 us
  matrix products: 27 us -> 7.6 us
  other arithmetic: 66.9 us -> 53.1 us
    pallas_call x0 -> x4, Pallas kernels: none -> 36.6 us  [enter(): pl.pallas_call(partial(enter_kernel, bool(query)), out_shape=[jax.ShapeDt...]
    ppermute x60, waiting for transfers between devices: 89.3 us -> 68.2 us  [flip(): return lax.ppermute(x, 'dp', [(i, i ^ bit) for i in range(count)])]
    dot_general x10 -> x0, matrix products: 19.5 us -> none  [the longest x9 17.6 us: matmul(): return jnp.dot(left, right, preferred_element_type=F32)]
    convert_element_type x4 -> x0, other arithmetic: 8.34 us -> none  [the longest x3 6.83 us: norm_of(): return layer_norm(block.astype(F32), gain_one, shift_one).astype(BF16)]
  transfers between devices with their start and end apart: 90 -> 90, of which waited for: 27 -> 33; matrix products, arithmetic and copies ran while one was open for 18% -> 14% of each run, Pallas kernels for 29% -> 36%
where the time goes in v4:
time: 649 us; the launch traced here: 640 us
  Pallas kernels  237 us (37%)
  waiting for transfers between devices  176 us (27%)
  starting transfers between devices  111 us (17%)
  other arithmetic  53.1 us (8%)
  local copies, waits for them, and re-layouts  52.6 us (8%)
  matrix products  7.6 us (1%)
    ppermute x30, waiting for transfers between devices, along_group(): return lax.ppermute(x, 'group', pairs)  108 us
    ppermute x60, waiting for transfers between devices, flip(): return lax.ppermute(x, 'dp', [(i, i ^ bit) for i in range(count)])  68.2 us
    pallas_call x3, Pallas kernels, feed_call(): pl.pallas_call(kernel, out_shape=outs, grid_spec=pltpu.PrefetchScalarGrid...  66.4 us
    ppermute x30, starting transfers between devices, along_group(): return lax.ppermute(x, 'group', pairs)  65.9 us
    ppermute x60, starting transfers between devices, flip(): return lax.ppermute(x, 'dp', [(i, i ^ bit) for i in range(count)])  45.2 us
    pallas_call x4, Pallas kernels, enter(): pl.pallas_call(partial(enter_kernel, bool(query)), out_shape=[jax.ShapeDt...  36.6 us
    pallas_call x4, Pallas kernels, attend_backward(): pl.pallas_call(partial(backward_kernel, base, final, pairs, width - (pair...  34.8 us
    pallas_call x1, Pallas kernels, attn_grads(): pl.pallas_call(partial(attn_grads_kernel, len(normed)), out_shape=(part,...  24.6 us
  transfers between devices with their start and end apart: 90, of which 33 were waited for; matrix products, arithmetic and copies ran while one was open for 14% of the time, Pallas kernels for 36%

profile of v4, /device:TPU:0, one launch (start us, length us, event | category | flops | bytes accessed | tf_op | source)
XLA Modules:
  0.0 639.9 jit_solution(15568031731739930539)
XLA Ops:
  10.5 5.9 collective-permute-done
  16.4 7.9 %collective-permute-start.5 = (bf16[3264]{0:T(1024)(128)(2,1)S(1)}, bf16[3264]{0:T(1024)(128)(2,1)S(1)}, u32[]{:S(2)}, u32[]{:S(2)}) collective-permute-start(bf16[3264]{0:T(1024)(128)(2,1)S(1)} %concatenate.42), channel_id=1, source_target_pairs={{0,3},{1,0},{2,1},{3,2},{4,7},{5,4},{6,5},{7,6},{8,11},{9,8},{10,9... | collective-permute-start | bytes 19592 | tf_op jit(solution)/shard_map/ppermute | solution.py:268
  24.3 6.8 %collective-permute-start.4 = (bf16[3264]{0:T(1024)(128)(2,1)S(1)}, bf16[3264]{0:T(1024)(128)(2,1)S(1)}, u32[]{:S(2)}, u32[]{:S(2)}) collective-permute-start(bf16[3264]{0:T(1024)(128)(2,1)S(1)} %concatenate.42), channel_id=1, source_target_pairs={{0,2},{1,3},{2,0},{3,1},{4,6},{5,7},{6,4},{7,5},{8,10},{9,11},{10,... | collective-permute-start | bytes 19592 | tf_op jit(solution)/shard_map/ppermute | solution.py:268
  40.5 6.3 reshape.239
  78.0 5.8 collective-permute-done.10.refs_3_
  88.5 6.1 collective-permute-done.7
  102.1 8.0 %assemble.3 = (bf16[4,2,136,1088]{3,2,1,0:T(8,128)(2,1)}, bf16[4,2,136,1088]{3,2,1,0:T(8,128)(2,1)}, bf16[4,2,136,1088]{3,2,1,0:T(8,128)(2,1)}, bf16[4,2,136,1088]{3,2,1,0:T(8,128)(2,1)}) custom-call(s32[3]{0:T(128)S(1)} %pad_add_fusion.1.here_ref, bf16[4,2,136,1088]{3,2,1,0:T(8,128)(2,1)} %pad_maximum_fusion.own_ref, bf16[3,136,1088]{2,1,0:T(8,128)(2,1)} %copy-done.74, ...), custom_call_target="tpu_custom_call" | custom-call | bytes 1183744 | tf_op jit(solution)/shard_map/assemble/pallas_call | solution.py:533
  110.1 11.1 %enter.4 = (bf16[512,1088]{1,0:T(8,128)(2,1)}, bf16[512,1088]{1,0:T(8,128)(2,1)}, bf16[512,1088]{1,0:T(8,128)(2,1)}, bf16[512,1088]{1,0:T(8,128)(2,1)}, bf16[1088,512]{1,0:T(8,128)(2,1)S(1)}) custom-call(bf16[512,1088]{1,0:T(8,128)(2,1)} %bitcast.177, f32[1,1088]{1,0:T(1,128)S(1)} %unstack.37.gain_ref, f32[1,1088]{1,0:T(1,128)S(1)} %unstack.39.shift_ref, ...), custom_call_target="tpu_custom_call" | custom-call | bytes 1024 | tf_op jit(solution)/shard_map/enter/pallas_call | solution.py:817
  121.2 8.7 %enter.5 = (bf16[512,1088]{1,0:T(8,128)(2,1)S(1)}, bf16[512,1088]{1,0:T(8,128)(2,1)}, bf16[512,1088]{1,0:T(8,128)(2,1)}) custom-call(bf16[512,1088]{1,0:T(8,128)(2,1)} %bitcast.22.x_ref, f32[1,1088]{1,0:T(1,128)S(1)} %unstack.37.gain_ref, f32[1,1088]{1,0:T(1,128)S(1)} %unstack.39.shift_ref, bf16[1088,1088]{1,0:T(8,128)(2,1)} %bitcast.161, ...), custom_call_target="tpu_custom_call" | custom-call | bytes 1024 | tf_op jit(solution)/shard_map/enter/pallas_call | solution.py:817
  129.9 8.7 %enter.6 = (bf16[512,1088]{1,0:T(8,128)(2,1)S(1)}, bf16[512,1088]{1,0:T(8,128)(2,1)}, bf16[512,1088]{1,0:T(8,128)(2,1)}) custom-call(bf16[512,1088]{1,0:T(8,128)(2,1)} %bitcast.13.x_ref, f32[1,1088]{1,0:T(1,128)S(1)} %unstack.37.gain_ref, f32[1,1088]{1,0:T(1,128)S(1)} %unstack.39.shift_ref, bf16[1088,1088]{1,0:T(8,128)(2,1)} %bitcast.162, ...), custom_call_target="tpu_custom_call" | custom-call | bytes 1024 | tf_op jit(solution)/shard_map/enter/pallas_call | solution.py:817
  141.7 8.2 %enter.7 = (bf16[512,1088]{1,0:T(8,128)(2,1)S(1)}, bf16[512,1088]{1,0:T(8,128)(2,1)}, bf16[512,1088]{1,0:T(8,128)(2,1)}) custom-call(bf16[512,1088]{1,0:T(8,128)(2,1)} %bitcast.29.x_ref, f32[1,1088]{1,0:T(1,128)S(1)} %unstack.37.gain_ref, f32[1,1088]{1,0:T(1,128)S(1)} %unstack.39.shift_ref, bf16[1088,1088]{1,0:T(8,128)(2,1)} %bitcast.163, ...), custom_call_target="tpu_custom_call" | custom-call | bytes 1024 | tf_op jit(solution)/shard_map/enter/pallas_call | solution.py:817
  154.1 5.5 attend_forward.3
  159.7 8.6 %collective-permute-done.19 = bf16[136,1088]{1,0:T(8,128)(2,1)S(1)} collective-permute-done((bf16[136,1088]{1,0:T(8,128)(2,1)S(1)}, bf16[136,1088]{1,0:T(8,128)(2,1)S(1)}, u32[]{:S(2)}, u32[]{:S(2)}) %collective-permute-start.19) | collective-permute-done | bytes 295968 | tf_op jit(solution)/shard_map/ppermute | solution.py:268
  183.8 17.5 %collective-permute-done.22 = bf16[136,1088]{1,0:T(8,128)(2,1)S(1)} collective-permute-done((bf16[136,1088]{1,0:T(8,128)(2,1)S(1)}, bf16[136,1088]{1,0:T(8,128)(2,1)S(1)}, u32[]{:S(2)}, u32[]{:S(2)}) %collective-permute-start.22) | collective-permute-done | bytes 295968 | tf_op jit(solution)/shard_map/ppermute | solution.py:268
  204.2 8.6 %attend_forward.5 = (bf16[1088,512]{1,0:T(8,128)(2,1)S(1)}, f32[9,2,512]{2,1,0:T(2,128)S(1)}) custom-call(s32[2]{0:T(128)S(1)} %pad_add_fusion.bounds_ref, bf16[1088,512]{1,0:T(8,128)(2,1)S(1)} %get-tuple-element.188.qt_ref, s32[1,512]{1,0:T(1,128)S(1)} %bitcast.190, ...), custom_call_target="tpu_custom_call", output_to_operand_aliasing={{0}: (11, {}), {1}: (12, {})} | custom-call | flops 16106127360 | bytes 557056 | tf_op jit(solution)/shard_map/attend_forward/pallas_call | solution.py:201
  222.4 8.0 %assemble.4 = bf16[4,4,2,136,1088]{4,3,2,1,0:T(8,128)(2,1)} custom-call(s32[3]{0:T(128)S(1)} %pad_add_fusion.1.here_ref, bf16[4,2,136,1088]{3,2,1,0:T(8,128)(2,1)} %bitcast.195, bf16[3,136,1088]{2,1,0:T(8,128)(2,1)} %copy-done.75, bf16[3,136,1088]{2,1,0:T(8,128)(2,1)} %copy-done.82, bf16[3,136,1088]{2,1,0:T(8,128)(2,1)} %copy-done.80, ...), custom_call_target="tpu_custom_call" | custom-call | bytes 1183744 | tf_op jit(solution)/shard_map/assemble/pallas_call | solution.py:533
  230.4 6.0 collective-permute-done.31.refs_1_
  240.5 22.6 %feed.1 = (bf16[4,512,1088]{2,1,0:T(8,128)(2,1)}, bf16[4,512,1088]{2,1,0:T(8,128)(2,1)}, bf16[4,4,136,1088]{3,2,1,0:T(8,128)(2,1)}, bf16[4,4,136,1088]{3,2,1,0:T(8,128)(2,1)}, bf16[1088,512]{1,0:T(8,128)(2,1)}) custom-call(s32[1]{0:T(128)} %bitcast.core_ref, bf16[512,1088]{1,0:T(8,128)(2,1)} %add_convert_fusion.6.x_ref, bf16[4,1088,1088]{2,1,0:T(8,128)(2,1)} %bitcast.198, ...), custom_call_target="tpu_custom_call" | custom-call | flops 12121538560 | bytes 1024 | tf_op jit(solution)/shard_map/feed/pallas_call | solution.py:379
  269.2 8.2 %assemble.5 = bf16[4,4,2,136,1088]{4,3,2,1,0:T(8,128)(2,1)} custom-call(s32[3]{0:T(128)S(1)} %pad_add_fusion.1.here_ref, bf16[4,2,136,1088]{3,2,1,0:T(8,128)(2,1)} %bitcast.201, bf16[3,136,1088]{2,1,0:T(8,128)(2,1)} %pad_maximum_fusion.9.refs_0_, bf16[3,136,1088]{2,1,0:T(8,128)(2,1)} %copy-done.81, bf16[3,136,1088]{2,1,0:T(8,128)(2,1)} %copy-done.79, ...), custom_call_target="tpu_custom_call" | custom-call | bytes 1183744 | tf_op jit(solution)/shard_map/assemble/pallas_call | solution.py:533
  285.6 30.6 %feed_back.1 = (bf16[4,4,136,1088]{3,2,1,0:T(8,128)(2,1)}, bf16[4,4,136,1088]{3,2,1,0:T(8,128)(2,1)}, f32[512,1088]{1,0:T(8,128)}, f32[4,1,1088]{2,1,0:T(1,128)}) custom-call(s32[1]{0:T(128)} %bitcast.core_ref, bf16[512,1088]{1,0:T(8,128)(2,1)} %bitcast.180, bf16[4,1088,1088]{2,1,0:T(8,128)(2,1)} %bitcast.196, ...), custom_call_target="tpu_custom_call" | custom-call | flops 12121538560 | bytes 1024 | tf_op jit(solution)/shard_map/feed_back/pallas_call | solution.py:379
  333.6 7.9 %add_convert_fusion.1 = bf16[4,4,136,1088]{3,2,1,0:T(8,128)(2,1)} fusion(bf16[4,4,136,1088]{3,2,1,0:T(8,128)(2,1)} %collective-permute-done.45, bf16[4,4,136,1088]{3,2,1,0:T(8,128)(2,1)} %get-tuple-element.253), kind=kLoop, calls=%fused_computation.2 | loop fusion | flops 9469952 | bytes 14204928 | tf_op jit(solution)/shard_map/convert_element_type | solution.py:556
  358.3 11.9 %collective-permute-done.46 = bf16[2,136,1088]{2,1,0:T(8,128)(2,1)S(1)} collective-permute-done((bf16[2,136,1088]{2,1,0:T(8,128)(2,1)}, bf16[2,136,1088]{2,1,0:T(8,128)(2,1)S(1)}, u32[]{:S(2)}, u32[]{:S(2)}) %collective-permute-start.46) | collective-permute-done | bytes 591904 | tf_op jit(solution)/shard_map/ppermute | solution.py:277
  375.2 5.7 collective-permute-start.53
  391.5 12.3 %collective-permute-done.50 = bf16[8,64,1088]{2,1,0:T(8,128)(2,1)S(1)} collective-permute-done((bf16[8,64,1088]{2,1,0:T(8,128)(2,1)S(1)}, bf16[8,64,1088]{2,1,0:T(8,128)(2,1)S(1)}, u32[]{:S(2)}, u32[]{:S(2)}) %collective-permute-start.50) | collective-permute-done | bytes 1114144 | tf_op jit(solution)/shard_map/ppermute | solution.py:268
  408.8 22.0 %collective-permute-done.52 = bf16[136,1088]{1,0:T(8,128)(2,1)} collective-permute-done((bf16[136,1088]{1,0:T(8,128)(2,1)}, bf16[136,1088]{1,0:T(8,128)(2,1)}, u32[]{:S(2)}, u32[]{:S(2)}) %collective-permute-start.52) | collective-permute-done | bytes 295968 | tf_op jit(solution)/shard_map/ppermute | solution.py:268
  440.7 18.7 %collective-permute-done.54 = bf16[8,64,1088]{2,1,0:T(8,128)(2,1)S(1)} collective-permute-done((bf16[8,64,1088]{2,1,0:T(8,128)(2,1)S(1)}, bf16[8,64,1088]{2,1,0:T(8,128)(2,1)S(1)}, u32[]{:S(2)}, u32[]{:S(2)}) %collective-permute-start.54) | collective-permute-done | bytes 1114144 | tf_op jit(solution)/shard_map/ppermute | solution.py:268
  469.8 19.6 %attend_backward.7 = (bf16[512,1088]{1,0:T(8,128)(2,1)S(1)}, bf16[512,1088]{1,0:T(8,128)(2,1)S(1)}, bf16[512,1088]{1,0:T(8,128)(2,1)S(1)}, f32[2,1088]{1,0:T(2,128)S(1)}) custom-call(s32[2]{0:T(128)S(1)} %copy-done.59, bf16[512,1088]{1,0:T(8,128)(2,1)S(1)} %copy-done.39, bf16[1088,512]{1,0:T(8,128)(2,1)S(1)} %copy-done.57, bf16[512,1088]{1,0:T(8,128)(2,1)S(1)} %copy-done.63, ...), custom_call_target="tpu_custom_call" | custom-call | flops 11408506880 | bytes 557056 | tf_op jit(solution)/shard_map/attend_backward/pallas_call | solution.py:243
  497.3 24.6 %attn_grads.1 = (bf16[4,4,136,1088]{3,2,1,0:T(8,128)(2,1)}, bf16[4,4,136,1088]{3,2,1,0:T(8,128)(2,1)}) custom-call(s32[1]{0:T(128)} %bitcast.core_ref, bf16[512,1088]{1,0:T(8,128)(2,1)} %copy-done.34, bf16[512,1088]{1,0:T(8,128)(2,1)} %copy-done.33, bf16[512,1088]{1,0:T(8,128)(2,1)} %copy-done.32, bf16[512,1088]{1,0:T(8,128)(2,1)} %get-tuple-element.230.refs_3_, ...), custom_call_target="tpu_custom_call" | custom-call | flops 12121538560 | bytes 1024 | tf_op jit(solution)/shard_map/attn_grads/pallas_call | solution.py:728
  545.6 7.7 %collective-permute-done.68 = bf16[2,136,1088]{2,1,0:T(8,128)(2,1)S(1)} collective-permute-done((bf16[2,136,1088]{2,1,0:T(8,128)(2,1)S(1)}, bf16[2,136,1088]{2,1,0:T(8,128)(2,1)S(1)}, u32[]{:S(2)}, u32[]{:S(2)}) %collective-permute-start.68) | collective-permute-done | bytes 591904 | tf_op jit(solution)/shard_map/ppermute | solution.py:277
  578.3 5.7 collective-permute-done.70
  593.1 13.2 %project.1 = f32[1088,512]{1,0:T(8,128)} custom-call(bf16[4,512,1088]{2,1,0:T(8,128)(2,1)} %get-tuple-element.318.h_ref, bf16[4,1088,1088]{2,1,0:T(8,128)(2,1)} %bitcast.197, f32[512,1088]{1,0:T(8,128)} %copy-done.2, f32[1,1088]{1,0:T(1,128)} %unstack.49.b_ref), custom_call_target="tpu_custom_call" | custom-call | flops 48486154240 | bytes 1024 | tf_op jit(solution)/shard_map/project/pallas_call | solution.py:379
  617.1 6.9 %collective-permute-done.86 = bf16[1,136,1088]{2,1,0:T(8,128)(2,1)S(1)} collective-permute-done((bf16[1,136,1088]{2,1,0:T(8,128)(2,1)S(1)}, bf16[1,136,1088]{2,1,0:T(8,128)(2,1)S(1)}, u32[]{:S(2)}, u32[]{:S(2)}) %collective-permute-start.86) | collective-permute-done | bytes 295968 | tf_op jit(solution)/shard_map/ppermute | solution.py:277
  (514 shorter events, 282.1 us)
Async XLA Ops:
  5.9 27.2 %collective-permute-start.2 = (bf16[136,1088]{1,0:T(8,128)(2,1)}, bf16[136,1088]{1,0:T(8,128)(2,1)S(1)}, u32[]{:S(2)}, u32[]{:S(2)}) collective-permute-start(bf16[136,1088]{1,0:T(8,128)(2,1)} %select_bitcast_fusion), channel_id=1, source_target_pairs={{0,3},{1,0},{2,1},{3,2},{4,7},{5,4},{6,5},{7,6},{8,11},{9,8},{10,9... | collective-permute-start | bytes 887816 | tf_op jit(solution)/shard_map/ppermute | solution.py:268
  8.0 28.1 %collective-permute-start.1 = (bf16[136,1088]{1,0:T(8,128)(2,1)}, bf16[136,1088]{1,0:T(8,128)(2,1)S(1)}, u32[]{:S(2)}, u32[]{:S(2)}) collective-permute-start(bf16[136,1088]{1,0:T(8,128)(2,1)} %select_bitcast_fusion), channel_id=1, source_target_pairs={{0,2},{1,3},{2,0},{3,1},{4,6},{5,7},{6,4},{7,5},{8,10},{9,11},{10,... | collective-permute-start | bytes 887816 | tf_op jit(solution)/shard_map/ppermute | solution.py:268
  38.1 26.9 %collective-permute-start.6 = (bf16[8,64,1088]{2,1,0:T(8,128)(2,1)S(1)}, bf16[8,64,1088]{2,1,0:T(8,128)(2,1)}, u32[]{:S(2)}, u32[]{:S(2)}) collective-permute-start(bf16[8,64,1088]{2,1,0:T(8,128)(2,1)S(1)} %bitcast.176), channel_id=1, source_target_pairs={{0,1},{1,2},{2,3},{4,5},{5,6},{6,7},{8,9},{9,10},{10,11},{12,13},{... | collective-permute-start | bytes 3342344 | tf_op jit(solution)/shard_map/ppermute | solution.py:268
  65.0 29.6 %collective-permute-start.7 = (bf16[8,64,1088]{2,1,0:T(8,128)(2,1)}, bf16[8,64,1088]{2,1,0:T(8,128)(2,1)}, u32[]{:S(2)}, u32[]{:S(2)}) collective-permute-start(bf16[8,64,1088]{2,1,0:T(8,128)(2,1)} %collective-permute-done.6), channel_id=1, source_target_pairs={{0,1},{1,2},{2,3},{4,5},{5,6},{6,7},{8,9},{9,10},{10,11},{12,13},{... | collective-permute-start | bytes 3342344 | tf_op jit(solution)/shard_map/ppermute | solution.py:268
  94.5 45.0 %collective-permute-start.17 = (bf16[8,64,1088]{2,1,0:T(8,128)(2,1)}, bf16[8,64,1088]{2,1,0:T(8,128)(2,1)}, u32[]{:S(2)}, u32[]{:S(2)}) collective-permute-start(bf16[8,64,1088]{2,1,0:T(8,128)(2,1)} %collective-permute-done.7), channel_id=1, source_target_pairs={{0,1},{1,2},{2,3},{4,5},{5,6},{6,7},{8,9},{9,10},{10,11},{12,13},{... | collective-permute-start | bytes 3342344 | tf_op jit(solution)/shard_map/ppermute | solution.py:268
  139.7 28.6 %collective-permute-start.19 = (bf16[136,1088]{1,0:T(8,128)(2,1)S(1)}, bf16[136,1088]{1,0:T(8,128)(2,1)S(1)}, u32[]{:S(2)}, u32[]{:S(2)}) collective-permute-start(bf16[136,1088]{1,0:T(8,128)(2,1)S(1)} %bitcast.231), channel_id=1, source_target_pairs={{0,2},{1,3},{2,0},{3,1},{4,6},{5,7},{6,4},{7,5},{8,10},{9,11},{10,... | collective-permute-start | bytes 887816 | tf_op jit(solution)/shard_map/ppermute | solution.py:268
  140.4 27.9 %collective-permute-start.18 = (bf16[136,1088]{1,0:T(8,128)(2,1)S(1)}, bf16[136,1088]{1,0:T(8,128)(2,1)S(1)}, u32[]{:S(2)}, u32[]{:S(2)}) collective-permute-start(bf16[136,1088]{1,0:T(8,128)(2,1)S(1)} %bitcast.232), channel_id=1, source_target_pairs={{0,1},{1,2},{2,3},{3,0},{4,5},{5,6},{6,7},{7,4},{8,9},{9,10},{10,1... | collective-permute-start | bytes 887816 | tf_op jit(solution)/shard_map/ppermute | solution.py:268
  168.4 33.9 %collective-permute-start.25 = (bf16[3,136,1088]{2,1,0:T(8,128)(2,1)S(1)}, bf16[3,136,1088]{2,1,0:T(8,128)(2,1)S(1)}, u32[]{:S(2)}, u32[]{:S(2)}) collective-permute-start(bf16[3,136,1088]{2,1,0:T(8,128)(2,1)S(1)} %pad_maximum_fusion.8.refs_0_), channel_id=1, source_target_pairs={{0,16},{4,20},{8,24},{12,28},{16,0},{20,4},{24,8},{28,12},{1,17},{... | collective-permute-start | bytes 2663432 | tf_op jit(solution)/shard_map/ppermute | solution.py:277
  170.0 32.3 %collective-permute-start.24 = (bf16[3,136,1088]{2,1,0:T(8,128)(2,1)S(1)}, bf16[3,136,1088]{2,1,0:T(8,128)(2,1)S(1)}, u32[]{:S(2)}, u32[]{:S(2)}) collective-permute-start(bf16[3,136,1088]{2,1,0:T(8,128)(2,1)S(1)} %pad_maximum_fusion.8.refs_0_), channel_id=1, source_target_pairs={{0,8},{4,12},{8,0},{12,4},{16,24},{20,28},{24,16},{28,20},{1,9},{5... | collective-permute-start | bytes 2663432 | tf_op jit(solution)/shard_map/ppermute | solution.py:277
  283.5 32.6 %collective-permute-start.43 = (bf16[2,136,1088]{2,1,0:T(8,128)(2,1)S(1)}, bf16[2,136,1088]{2,1,0:T(8,128)(2,1)}, u32[]{:S(2)}, u32[]{:S(2)}) collective-permute-start(bf16[2,136,1088]{2,1,0:T(8,128)(2,1)S(1)} %get-tuple-element.360), channel_id=1, source_target_pairs={{0,8},{4,12},{8,0},{12,4},{16,24},{20,28},{24,16},{28,20},{1,9},{5... | collective-permute-start | bytes 1775624 | tf_op jit(solution)/shard_map/ppermute | solution.py:277
  285.0 31.1 %collective-permute-start.44 = (bf16[2,136,1088]{2,1,0:T(8,128)(2,1)S(1)}, bf16[2,136,1088]{2,1,0:T(8,128)(2,1)}, u32[]{:S(2)}, u32[]{:S(2)}) collective-permute-start(bf16[2,136,1088]{2,1,0:T(8,128)(2,1)S(1)} %get-tuple-element.361), channel_id=1, source_target_pairs={{0,16},{4,20},{8,24},{12,28},{16,0},{20,4},{24,8},{28,12},{1,17},{... | collective-permute-start | bytes 1775624 | tf_op jit(solution)/shard_map/ppermute | solution.py:277
  322.8 47.4 %collective-permute-start.49 = (bf16[4,136,1088]{2,1,0:T(8,128)(2,1)}, bf16[4,136,1088]{2,1,0:T(8,128)(2,1)}, u32[]{:S(2)}, u32[]{:S(2)}) collective-permute-start(bf16[4,136,1088]{2,1,0:T(8,128)(2,1)} %pad_maximum_fusion.2), channel_id=1, source_target_pairs={{0,16},{4,20},{8,24},{12,28},{16,0},{20,4},{24,8},{28,12},{1,17},{... | collective-permute-start | bytes 3551240 | tf_op jit(solution)/shard_map/ppermute | solution.py:277
  326.9 43.3 %collective-permute-start.48 = (bf16[4,136,1088]{2,1,0:T(8,128)(2,1)}, bf16[4,136,1088]{2,1,0:T(8,128)(2,1)}, u32[]{:S(2)}, u32[]{:S(2)}) collective-permute-start(bf16[4,136,1088]{2,1,0:T(8,128)(2,1)} %pad_maximum_fusion.1), channel_id=1, source_target_pairs={{0,8},{4,12},{8,0},{12,4},{16,24},{20,28},{24,16},{28,20},{1,9},{5... | collective-permute-start | bytes 3551240 | tf_op jit(solution)/shard_map/ppermute | solution.py:277
  372.8 30.9 %collective-permute-start.50 = (bf16[8,64,1088]{2,1,0:T(8,128)(2,1)S(1)}, bf16[8,64,1088]{2,1,0:T(8,128)(2,1)S(1)}, u32[]{:S(2)}, u32[]{:S(2)}) collective-permute-start(bf16[8,64,1088]{2,1,0:T(8,128)(2,1)S(1)} %bitcast.186), channel_id=1, source_target_pairs={{1,0},{2,1},{3,2},{5,4},{6,5},{7,6},{9,8},{10,9},{11,10},{13,12},{... | collective-permute-start | bytes 3342344 | tf_op jit(solution)/shard_map/ppermute | solution.py:268
  375.2 33.6 %collective-permute-start.53 = (bf16[136,1088]{1,0:T(8,128)(2,1)}, bf16[136,1088]{1,0:T(8,128)(2,1)S(1)}, u32[]{:S(2)}, u32[]{:S(2)}) collective-permute-start(bf16[136,1088]{1,0:T(8,128)(2,1)} %get-tuple-element.371), channel_id=1, source_target_pairs={{0,3},{1,0},{2,1},{3,2},{4,7},{5,4},{6,5},{7,6},{8,11},{9,8},{10,9... | collective-permute-start | bytes 887816 | tf_op jit(solution)/shard_map/ppermute | solution.py:268
  380.9 49.9 %collective-permute-start.52 = (bf16[136,1088]{1,0:T(8,128)(2,1)}, bf16[136,1088]{1,0:T(8,128)(2,1)}, u32[]{:S(2)}, u32[]{:S(2)}) collective-permute-start(bf16[136,1088]{1,0:T(8,128)(2,1)} %get-tuple-element.372), channel_id=1, source_target_pairs={{0,2},{1,3},{2,0},{3,1},{4,6},{5,7},{6,4},{7,5},{8,10},{9,11},{10,... | collective-permute-start | bytes 887816 | tf_op jit(solution)/shard_map/ppermute | solution.py:268
  380.9 49.9 %collective-permute-start.51 = (bf16[136,1088]{1,0:T(8,128)(2,1)}, bf16[136,1088]{1,0:T(8,128)(2,1)}, u32[]{:S(2)}, u32[]{:S(2)}) collective-permute-start(bf16[136,1088]{1,0:T(8,128)(2,1)} %get-tuple-element.373), channel_id=1, source_target_pairs={{0,1},{1,2},{2,3},{3,0},{4,5},{5,6},{6,7},{7,4},{8,9},{9,10},{10,1... | collective-permute-start | bytes 887816 | tf_op jit(solution)/shard_map/ppermute | solution.py:268
  384.5 78.4 %collective-permute-start.56 = (bf16[4,136,1088]{2,1,0:T(8,128)(2,1)}, bf16[4,136,1088]{2,1,0:T(8,128)(2,1)}, u32[]{:S(2)}, u32[]{:S(2)}) collective-permute-start(bf16[4,136,1088]{2,1,0:T(8,128)(2,1)} %pad_maximum_fusion.4), channel_id=1, source_target_pairs={{0,16},{4,20},{8,24},{12,28},{16,0},{20,4},{24,8},{28,12},{1,17},{... | collective-permute-start | bytes 3551240 | tf_op jit(solution)/shard_map/ppermute | solution.py:277
  403.8 59.2 %collective-permute-start.55 = (bf16[4,136,1088]{2,1,0:T(8,128)(2,1)}, bf16[4,136,1088]{2,1,0:T(8,128)(2,1)}, u32[]{:S(2)}, u32[]{:S(2)}) collective-permute-start(bf16[4,136,1088]{2,1,0:T(8,128)(2,1)} %pad_maximum_fusion.3), channel_id=1, source_target_pairs={{0,8},{4,12},{8,0},{12,4},{16,24},{20,28},{24,16},{28,20},{1,9},{5... | collective-permute-start | bytes 3551240 | tf_op jit(solution)/shard_map/ppermute | solution.py:277
  430.8 28.5 %collective-permute-start.54 = (bf16[8,64,1088]{2,1,0:T(8,128)(2,1)S(1)}, bf16[8,64,1088]{2,1,0:T(8,128)(2,1)S(1)}, u32[]{:S(2)}, u32[]{:S(2)}) collective-permute-start(bf16[8,64,1088]{2,1,0:T(8,128)(2,1)S(1)} %bitcast.184), channel_id=1, source_target_pairs={{1,0},{2,1},{3,2},{5,4},{6,5},{7,6},{9,8},{10,9},{11,10},{13,12},{... | collective-permute-start | bytes 3342344 | tf_op jit(solution)/shard_map/ppermute | solution.py:268
  433.4 34.2 %collective-permute-start.57 = (bf16[1,136,1088]{2,1,0:T(8,128)(2,1)S(1)}, bf16[1,136,1088]{2,1,0:T(8,128)(2,1)S(1)}, u32[]{:S(2)}, u32[]{:S(2)}) collective-permute-start(bf16[1,136,1088]{2,1,0:T(8,128)(2,1)S(1)} %bitcast.218), channel_id=1, source_target_pairs={{0,8},{4,12},{8,0},{12,4},{16,24},{20,28},{24,16},{28,20},{1,9},{5... | collective-permute-start | bytes 887816 | tf_op jit(solution)/shard_map/ppermute | solution.py:277
  435.1 32.5 %collective-permute-start.58 = (bf16[1,136,1088]{2,1,0:T(8,128)(2,1)S(1)}, bf16[1,136,1088]{2,1,0:T(8,128)(2,1)S(1)}, u32[]{:S(2)}, u32[]{:S(2)}) collective-permute-start(bf16[1,136,1088]{2,1,0:T(8,128)(2,1)S(1)} %bitcast.219), channel_id=1, source_target_pairs={{0,16},{4,20},{8,24},{12,28},{16,0},{20,4},{24,8},{28,12},{1,17},{... | collective-permute-start | bytes 887816 | tf_op jit(solution)/shard_map/ppermute | solution.py:277
  462.9 27.7 %collective-permute-start.59 = (bf16[8,64,1088]{2,1,0:T(8,128)(2,1)S(1)}, bf16[8,64,1088]{2,1,0:T(8,128)(2,1)S(1)}, u32[]{:S(2)}, u32[]{:S(2)}) collective-permute-start(bf16[8,64,1088]{2,1,0:T(8,128)(2,1)S(1)} %bitcast.183), channel_id=1, source_target_pairs={{1,0},{2,1},{3,2},{5,4},{6,5},{7,6},{9,8},{10,9},{11,10},{13,12},{... | collective-permute-start | bytes 3342344 | tf_op jit(solution)/shard_map/ppermute | solution.py:268
  467.6 26.6 %collective-permute-start.60 = (bf16[1,136,512]{2,1,0:T(8,128)(2,1)S(1)}, bf16[1,136,512]{2,1,0:T(8,128)(2,1)S(1)}, u32[]{:S(2)}, u32[]{:S(2)}) collective-permute-start(bf16[1,136,512]{2,1,0:T(8,128)(2,1)S(1)} %slice.243), channel_id=1, source_target_pairs={{0,16},{4,20},{8,24},{12,28},{16,0},{20,4},{24,8},{28,12},{1,17},{... | collective-permute-start | bytes 417800 | tf_op jit(solution)/shard_map/ppermute | solution.py:277
  468.1 26.1 %collective-permute-start.61 = (bf16[1,136,576]{2,1,0:T(8,128)(2,1)S(1)}, bf16[1,136,576]{2,1,0:T(8,128)(2,1)S(1)}, u32[]{:S(2)}, u32[]{:S(2)}) collective-permute-start(bf16[1,136,576]{2,1,0:T(8,128)(2,1)S(1)} %slice.244), channel_id=1, source_target_pairs={{0,8},{4,12},{8,0},{12,4},{16,24},{20,28},{24,16},{28,20},{1,9},{5... | collective-permute-start | bytes 470024 | tf_op jit(solution)/shard_map/ppermute | solution.py:277
  494.4 27.6 %collective-permute-start.64 = (bf16[136,1088]{1,0:T(8,128)(2,1)S(1)}, bf16[136,1088]{1,0:T(8,128)(2,1)S(1)}, u32[]{:S(2)}, u32[]{:S(2)}) collective-permute-start(bf16[136,1088]{1,0:T(8,128)(2,1)S(1)} %get-tuple-element.367), channel_id=1, source_target_pairs={{0,3},{1,0},{2,1},{3,2},{4,7},{5,4},{6,5},{7,6},{8,11},{9,8},{10,9... | collective-permute-start | bytes 887816 | tf_op jit(solution)/shard_map/ppermute | solution.py:268
  494.9 27.1 %collective-permute-start.63 = (bf16[136,1088]{1,0:T(8,128)(2,1)S(1)}, bf16[136,1088]{1,0:T(8,128)(2,1)S(1)}, u32[]{:S(2)}, u32[]{:S(2)}) collective-permute-start(bf16[136,1088]{1,0:T(8,128)(2,1)S(1)} %get-tuple-element.368), channel_id=1, source_target_pairs={{0,2},{1,3},{2,0},{3,1},{4,6},{5,7},{6,4},{7,5},{8,10},{9,11},{10,... | collective-permute-start | bytes 887816 | tf_op jit(solution)/shard_map/ppermute | solution.py:268
  542.7 25.9 %collective-permute-start.80 = (bf16[1,136,576]{2,1,0:T(8,128)(2,1)}, bf16[1,136,576]{2,1,0:T(8,128)(2,1)S(1)}, u32[]{:S(2)}, u32[]{:S(2)}) collective-permute-start(bf16[1,136,576]{2,1,0:T(8,128)(2,1)} %slice.266), channel_id=1, source_target_pairs={{0,8},{4,12},{8,0},{12,4},{16,24},{20,28},{24,16},{28,20},{1,9},{5... | collective-permute-start | bytes 470024 | tf_op jit(solution)/shard_map/ppermute | solution.py:277
  556.4 27.6 %collective-permute-start.70 = (bf16[4,136,1088]{2,1,0:T(8,128)(2,1)}, bf16[4,136,1088]{2,1,0:T(8,128)(2,1)}, u32[]{:S(2)}, u32[]{:S(2)}) collective-permute-start(bf16[4,136,1088]{2,1,0:T(8,128)(2,1)} %pad_maximum_fusion.6), channel_id=1, source_target_pairs={{0,16},{4,20},{8,24},{12,28},{16,0},{20,4},{24,8},{28,12},{1,17},{... | collective-permute-start | bytes 3551240 | tf_op jit(solution)/shard_map/ppermute | solution.py:277
  558.0 28.3 %collective-permute-start.69 = (bf16[4,136,1088]{2,1,0:T(8,128)(2,1)}, bf16[4,136,1088]{2,1,0:T(8,128)(2,1)}, u32[]{:S(2)}, u32[]{:S(2)}) collective-permute-start(bf16[4,136,1088]{2,1,0:T(8,128)(2,1)} %pad_maximum_fusion.5), channel_id=1, source_target_pairs={{0,8},{4,12},{8,0},{12,4},{16,24},{20,28},{24,16},{28,20},{1,9},{5... | collective-permute-start | bytes 3551240 | tf_op jit(solution)/shard_map/ppermute | solution.py:277
  576.0 30.4 %collective-permute-start.81 = (bf16[4,136,1088]{2,1,0:T(8,128)(2,1)S(1)}, bf16[4,136,1088]{2,1,0:T(8,128)(2,1)S(1)}, u32[]{:S(2)}, u32[]{:S(2)}) collective-permute-start(bf16[4,136,1088]{2,1,0:T(8,128)(2,1)S(1)} %maximum_maximum_fusion.1.mine_ref), channel_id=1, source_target_pairs={{0,4},{4,0},{8,12},{12,8},{16,20},{20,16},{24,28},{28,24},{1,5},{5... | collective-permute-start | bytes 3551240 | tf_op jit(solution)/shard_map/ppermute | solution.py:277
  576.5 29.8 %collective-permute-start.75 = (f32[12,1088]{1,0:T(8,128)S(1)}, f32[12,1088]{1,0:T(8,128)S(1)}, u32[]{:S(2)}, u32[]{:S(2)}) collective-permute-start(f32[12,1088]{1,0:T(8,128)S(1)} %add.322), channel_id=1, source_target_pairs={{0,8},{4,12},{8,0},{12,4},{16,24},{20,28},{24,16},{28,20},{1,9},{5... | collective-permute-start | bytes 156680 | tf_op jit(solution)/shard_map/ppermute | solution.py:277
  (172 other events, 2220.3 us)
